TPU v7x, 32 devices: a whole 2x2x4 slice. The times are simulated.
32 devices in a mesh: groups: 2 (over y), seq: 4 (over z), adapter: 2 (over x), head: 2 (over core).
Axes of the slice: x: 2, y: 2, z: 4, core: 2. Of those that a mesh axis runs over, the one named last changes fastest.
Arguments:
- hidden: bfloat16 [64, 3, 8192], P(('groups', 'seq', 'adapter'), None, 'head'), parts along dimension 0, may hold values from -6 to 6
- base_query_rows: bfloat16 [64, 3, 8192], P(('groups', 'seq', 'adapter'), None, 'head'), parts along dimension 0, may hold values from -16 to 16
- fresh_key_value: bfloat16 [2, 64, 3, 1024], P(None, ('groups', 'seq', 'adapter'), None, 'head'), parts along dimension 1, may hold values from -12 to 12
- suffix_key_value: bfloat16 [2, 64, 32, 1024], P(None, ('groups', 'seq', 'adapter'), None, 'head'), parts along dimension 1, may hold values from -12 to 12
- suffix_length: int32 [64], P(('groups', 'seq', 'adapter')), parts along dimension 0, may hold values from 0 to 32, as said below
- row_adapter_index: int32 [64, 1], P(('groups', 'seq', 'adapter')), parts along dimension 0, may hold values from 0 to 1
- prompt_key_value: bfloat16 [2, 8192, 1024], P(None, ('groups', 'seq'), 'head'), parts along dimension 1, may hold values from -16 to 16
- query_down_factors: bfloat16 [4, 64, 8192], P(('groups', 'adapter'), None, 'head'), parts along dimension 0, may hold values from -0.0625 to 0.0625
- query_up_factors: bfloat16 [4, 64, 8192], P(('groups', 'adapter'), None, 'head'), parts along dimension 0, may hold values from -0.75 to 0.75
- output_down_factors: bfloat16 [4, 64, 8192], P(('groups', 'adapter'), None, 'head'), parts along dimension 0, may hold values from -0.0625 to 0.0625
- output_up_factors: bfloat16 [4, 64, 8192], P(('groups', 'adapter'), None, 'head'), parts along dimension 0, may hold values from -0.75 to 0.75
Outputs:
- attended: bfloat16 [64, 3, 8192], P(('groups', 'seq', 'adapter'), None, 'head'), parts along dimension 0
- adapted: bfloat16 [64, 3, 8192], P(('groups', 'seq', 'adapter'), None, 'head'), parts along dimension 0
There are 2 independent parts, one for each index of `groups`. A program takes and returns all parts, laid end to end along the dimension named above; each array names one. Nothing has to cross between parts.
Inputs may be any that keep to these rules, and one draw needn't show every extreme that they name: `suffix_length`: each row's suffix holds at most 32 tokens, and some row holds exactly 32.
All inputs are finite; a program needn't handle non-finite values.
Results may differ from a plain program's by a relative error of at most 0.011.
Values may be sent and summed in bfloat16 or wider, within the bound.
No kernel may reach another device: no remote copies, remote signals or barrier semaphores. Data moves between devices by JAX's collectives and lax.ppermute only.
A program may use at most 64 MiB of HBM per device.

v0:
```python
import math

import jax
import jax.numpy as jnp
from jax import lax
from jax.sharding import PartitionSpec as P

HEAD_SIZE = 128


rope_base = 1000000.0


def rotate(values_in, position):
    half_dim = values_in.shape[-1] // 2
    frequency = rope_base ** (-2.0 * jnp.arange(half_dim, dtype=jnp.float32) / values_in.shape[-1])
    angles = position[..., None] * frequency
    cos_part = jnp.cos(angles)
    sin_part = jnp.sin(angles)
    first_half = values_in[..., :half_dim]
    second_half = values_in[..., half_dim:]
    return jnp.concatenate(
        [
            first_half * cos_part - second_half * sin_part,
            second_half * cos_part + first_half * sin_part,
        ],
        -1,
    )


def rank_mask(rank_whole, adapter_of_row, first_adapter, adapter_count):
    picked = (
        adapter_of_row[:, None]
        == first_adapter + jnp.arange(adapter_count, dtype=jnp.int32)[None, :]
    )
    return jnp.where(picked[:, None, :, None], rank_whole, jnp.zeros((), jnp.bfloat16))


def on_device(
    hidden,
    base_query_rows,
    fresh_key_value,
    suffix_key_value,
    suffix_length,
    row_adapter_index,
    prompt_key_value,
    query_down_factors,
    query_up_factors,
    output_down_factors,
    output_up_factors,
):
    row_count = hidden.shape[0]
    step_count = hidden.shape[1]
    head_dim = HEAD_SIZE
    kv_heads = prompt_key_value.shape[2] // head_dim
    query_heads = base_query_rows.shape[2] // head_dim
    group_size = query_heads // kv_heads
    resident_adapters = query_down_factors.shape[0]
    first_adapter = lax.axis_index("adapter") * resident_adapters
    score_scale = 1.0 / math.sqrt(head_dim)
    relocated, moved_ids = (
        lax.all_gather(hidden, "adapter", axis=0, tiled=True),
        lax.all_gather(row_adapter_index, "adapter", axis=0, tiled=True),
    )
    rank_piece = jnp.einsum(
        "mza,uya->mzuy", relocated, query_down_factors, preferred_element_type=jnp.float32
    )
    rank_whole = lax.psum(rank_piece, "head").astype(jnp.bfloat16)
    chosen = rank_mask(rank_whole, moved_ids[:, 0], first_adapter, resident_adapters)
    chosen = chosen.reshape(chosen.shape[0], step_count, -1)
    up_factor_matrix = query_up_factors.reshape(-1, query_up_factors.shape[2])
    picked_rows = chosen
    query_adjustment = lax.psum_scatter(
        jnp.einsum(
            "rtk,kc->rtc", picked_rows, up_factor_matrix, preferred_element_type=jnp.float32
        ),
        "adapter",
        scatter_dimension=0,
        tiled=True,
    )
    prompt_total = prompt_key_value.shape[1] * lax.axis_size("seq")
    position = (
        prompt_total + suffix_length[:, None] + jnp.arange(step_count, dtype=jnp.int32)[None, :]
    ).astype(jnp.float32)
    merged_query = (base_query_rows.astype(jnp.float32) + query_adjustment).reshape(
        row_count, step_count, query_heads, head_dim
    )
    rotated = rotate(merged_query, position[:, :, None]).astype(jnp.bfloat16)
    token_count = row_count * step_count
    query_flat = rotated.reshape(token_count, query_heads * head_dim)
    gathered = lax.all_gather(query_flat, "seq", axis=0, tiled=True)
    seq_count = lax.axis_size("seq")
    block_rows = math.gcd(seq_count, 4) * token_count
    prompt_keys = prompt_key_value[0].reshape(-1, kv_heads, head_dim)
    prompt_values = prompt_key_value[1].reshape(-1, kv_heads, head_dim)

    def prompt_block(block):
        grouped = block.reshape(block_rows, kv_heads, group_size, head_dim)
        scores = (
            jnp.einsum("nkgd,pkd->nkgp", grouped, prompt_keys, preferred_element_type=jnp.float32)
            * score_scale
        )
        peaks = jnp.max(scores, -1)
        weight = jnp.exp(scores - peaks[..., None]).astype(jnp.bfloat16)
        weighted = jnp.einsum(
            "nkgp,pkd->nkgd", weight, prompt_values, preferred_element_type=jnp.float32
        )
        return (weighted, peaks, jnp.sum(weight, -1, dtype=jnp.float32))

    weighted, peaks, totals = lax.map(
        prompt_block, gathered.reshape(-1, block_rows, query_heads * head_dim)
    )
    weighted = weighted.reshape(seq_count, token_count, kv_heads, group_size, head_dim)
    peaks = peaks.reshape(seq_count, token_count, kv_heads, group_size)
    totals = totals.reshape(seq_count, token_count, kv_heads, group_size)
    suffix_slots = suffix_key_value.shape[2]
    local_keys = jnp.concatenate([suffix_key_value[0], fresh_key_value[0]], 1).reshape(
        row_count, suffix_slots + step_count, kv_heads, head_dim
    )
    local_values = jnp.concatenate([suffix_key_value[1], fresh_key_value[1]], 1).reshape(
        row_count, suffix_slots + step_count, kv_heads, head_dim
    )
    own_query = rotated.reshape(row_count, step_count, kv_heads, group_size, head_dim)
    local_scores = (
        jnp.einsum("rtkgd,rpkd->rtkgp", own_query, local_keys, preferred_element_type=jnp.float32)
        * score_scale
    )
    key_slot = jnp.arange(suffix_slots + step_count, dtype=jnp.int32)[None, None, :]
    admitted = jnp.where(
        key_slot < suffix_slots,
        key_slot < suffix_length[:, None, None],
        key_slot - suffix_slots <= jnp.arange(step_count, dtype=jnp.int32)[None, :, None],
    )
    admitted = admitted[:, :, None, None, :]
    masked = jnp.where(admitted, local_scores, -1e30)
    local_peaks = jnp.max(masked, -1)
    local_weight = jnp.where(admitted, jnp.exp(masked - local_peaks[..., None]), 0.0).astype(
        jnp.bfloat16
    )
    local_weighted = jnp.einsum(
        "rtkgp,rpkd->rtkgd", local_weight, local_values, preferred_element_type=jnp.float32
    )
    local_totals = jnp.sum(local_weight, -1, dtype=jnp.float32)
    local_part = (
        local_weighted.reshape(token_count, kv_heads, group_size, head_dim),
        local_peaks.reshape(token_count, kv_heads, group_size),
        local_totals.reshape(token_count, kv_heads, group_size),
    )
    arrived = (
        lax.all_to_all(weighted, "seq", split_axis=0, concat_axis=0, tiled=True),
        lax.all_to_all(peaks, "seq", split_axis=0, concat_axis=0, tiled=True),
        lax.all_to_all(totals, "seq", split_axis=0, concat_axis=0, tiled=True),
    )
    highest = jnp.maximum(jnp.max(arrived[1], 0), local_part[1])
    factors = jnp.exp(arrived[1] - highest[None])
    local_factor = jnp.exp(local_part[1] - highest)
    combined = (
        jnp.sum(arrived[0] * factors[..., None], 0) + local_part[0] * local_factor[..., None],
        highest,
        jnp.sum(arrived[2] * factors, 0) + local_part[2] * local_factor,
    )
    attended = (
        (combined[0] / combined[2][..., None])
        .reshape(row_count, step_count, query_heads * head_dim)
        .astype(jnp.bfloat16)
    )
    relocated_output = lax.all_gather(attended, "adapter", axis=0, tiled=True)
    out_adapter = moved_ids[:, 0]
    output_piece = jnp.einsum(
        "aod,bxd->aobx", relocated_output, output_down_factors, preferred_element_type=jnp.float32
    )
    out_whole = lax.psum(output_piece, "head").astype(jnp.bfloat16)
    out_chosen = rank_mask(out_whole, out_adapter, first_adapter, resident_adapters)
    out_chosen = out_chosen.reshape(out_chosen.shape[0], step_count, -1)
    output_matrix = output_up_factors.reshape(-1, output_up_factors.shape[2])
    picked_rows = out_chosen
    adapted = lax.psum_scatter(
        jnp.einsum(
            "rtk,kc->rtc", picked_rows, output_matrix, preferred_element_type=jnp.float32
        ).astype(jnp.bfloat16),
        "adapter",
        scatter_dimension=0,
        tiled=True,
    )
    return (attended, adapted)


def solution(mesh):
    placed = (
        P(("groups", "seq", "adapter"), None, "head"),
        P(("groups", "seq", "adapter"), None, "head"),
        P(None, ("groups", "seq", "adapter"), None, "head"),
        P(None, ("groups", "seq", "adapter"), None, "head"),
        P(("groups", "seq", "adapter")),
        P(("groups", "seq", "adapter"), None),
        P(None, ("groups", "seq"), "head"),
        P(("groups", "adapter"), None, "head"),
        P(("groups", "adapter"), None, "head"),
        P(("groups", "adapter"), None, "head"),
        P(("groups", "adapter"), None, "head"),
    )
    return jax.shard_map(
        on_device,
        mesh=mesh,
        in_specs=placed,
        out_specs=(
            P(("groups", "seq", "adapter"), None, "head"),
            P(("groups", "seq", "adapter"), None, "head"),
        ),
        check_vma=False,
    )
```

profile of v0, /device:TPU:0, one launch (start us, length us, event | category | flops | bytes accessed | tf_op | source)
XLA Modules:
  0.0 158.5 jit_solution(6702682194150986861)
XLA Ops:
  7.3 1.3 fusion.39
  9.2 0.8 bitcast_dynamic-update-slice_fusion
  10.0 5.2 %all-reduce = s32[8]{0:T(128)S(1)} all-reduce(s32[8]{0:T(128)S(1)} %bitcast_dynamic-update-slice_fusion), channel_id=1, replica_groups=mesh['groups'=2,'seq'=4,'adapter'=2,'head'=2] {'adapter'}, use_global_device_ids=true, to_apply=%add | all-reduce | flops 8 | bytes 64
  15.2 1.0 copy.71
  16.2 5.6 %all_gather.13 = bf16[8,3,4096]{2,1,0:T(4,128)(2,1)S(1)} all-gather(bf16[4,3,4096]{2,1,0:T(4,128)(2,1)S(1)} %copy.71), channel_id=1, replica_groups=mesh['groups'=2,'seq'=4,'adapter'=2,'head'=2] {'adapter'}, dimensions={0}, use_global_device_ids=true | all-gather | bytes 294912 | tf_op jit(solution)/shard_map/all_gather | solution.py:62
  21.8 1.4 convolution_bitcast_fusion.2
  23.2 3.3 %psum.14 = bf16[8,3,1,64]{3,0,1,2:T(8,128)(2,1)S(1)} all-reduce(f32[8,3,1,64]{3,0,1,2:T(8,128)S(1)} %convolution_bitcast_fusion.2), channel_id=1, replica_groups=mesh['groups'=2,'seq'=4,'adapter'=2,'head'=2] {'head'}, use_global_device_ids=true, to_apply=%region_0.0 | all-reduce | flops 1536 | bytes 9216 | tf_op jit(solution)/shard_map/psum | solution.py:68
  26.5 1.0 fusion.6
  27.5 1.3 iota_compare_fusion.1
  29.5 1.3 fusion.38
  30.8 2.7 %fusion.36 = (bf16[1,1024,512]{2,1,0:T(8,128)(2,1)S(1)}, bf16[1,1024,512]{2,1,0:T(8,128)(2,1)}) fusion(bf16[2,1024,512]{2,1,0:T(8,128)(2,1)} %param.17), kind=kLoop, calls=%fused_computation.71 | loop fusion | bytes 4194304 | tf_op jit(solution)/shard_map/slice | solution.py:95
  33.5 1.5 copy.130
  37.0 18.2 %all-reduce.6.cloned.1.call-done = f32[8,3,4096]{2,0,1:T(8,128)} async-done(((f32[8,3,4096]{2,0,1:T(8,128)}), f32[8,3,4096]{2,0,1:T(8,128)}) %all-reduce.6.cloned.1.call-update) | async-done | bytes 393232
  55.2 1.1 dynamic-slice_add_fusion
  57.3 15.6 %all-gather = bf16[4,12,4096]{2,1,0:T(8,128)(2,1)S(1)} all-gather(bf16[1,12,4096]{2,1,0:T(8,128)(2,1)S(1)} %reshape.233), channel_id=1, replica_groups=mesh['groups'=2,'seq'=4,'adapter'=2,'head'=2] {'seq'}, dimensions={0}, use_global_device_ids=true | all-gather | bytes 491520 | tf_op jit(solution)/shard_map/all_gather | solution.py:91
  73.2 1.1 bitcast_reduce_fusion
  74.3 2.7 %copy-done.1 = f32[4,48,8,1024]{3,2,1,0:T(8,128)} copy-done((f32[4,48,8,1024]{3,2,1,0:T(8,128)}, f32[4,48,8,1024]{3,2,1,0:T(8,128)S(1)}, u32[]{:S(2)}) %copy-start.1) | copy-done | bytes 6291480
  77.0 1.3 convert_reduce_fusion
  79.2 5.4 %all-to-all-start.2 = ((f32[4,1,384]{2,1,0:T(1,128)}), f32[4,1,384]{2,1,0:T(1,128)S(1)}, u32[]{:S(2)}, u32[]{:S(2)}) async-start(f32[4,1,384]{2,1,0:T(1,128)} %reshape.257), calls=%async_computation.2 | async-start | bytes 12288 | tf_op jit(solution)/shard_map/all_to_all | solution.py:152
  86.1 4.1 %all-to-all-done.2 = f32[4,1,384]{2,1,0:T(1,128)S(1)} async-done(((f32[4,1,384]{2,1,0:T(1,128)}), f32[4,1,384]{2,1,0:T(1,128)S(1)}, u32[]{:S(2)}, u32[]{:S(2)}) %all-to-all-start.2) | async-done | bytes 6176 | tf_op jit(solution)/shard_map/all_to_all | solution.py:152
  90.2 3.2 %all-to-all-start.1 = ((f32[4,1,384]{2,1,0:T(1,128)}), f32[4,1,384]{2,1,0:T(1,128)S(1)}, u32[]{:S(2)}, u32[]{:S(2)}) async-start(f32[4,1,384]{2,1,0:T(1,128)} %reshape.259), calls=%async_computation.1 | async-start | bytes 12288 | tf_op jit(solution)/shard_map/all_to_all | solution.py:151
  93.4 4.0 %fusion.9 = f32[4,48,8,128]{3,2,1,0:T(8,128)S(1)} fusion(bf16[1024,4,128,1]{0,2,3,1:T(8,128)(2,1)S(1)} %bitcast.113, f32[4,48,8,1024]{3,2,1,0:T(8,128)} %copy-done.1, f32[48,4,8]{2,0,1:T(8,128)S(1)} %get-tuple-element.43), kind=kOutput, calls=%fused_computation.18 | convolution fusion | flops 407371776 | bytes 8132608 | tf_op jit(solution)/shard_map/while/body/eval_jaxpr/nkgp,pkd->nkgd/dot_general | solution.py:105
  97.4 0.9 copy.79
  99.0 4.6 %all-to-all-start = ((f32[4,12,4,8,128]{4,3,1,2,0:T(8,128)}), f32[4,12,4,8,128]{4,3,1,2,0:T(8,128)S(1)}, u32[]{:S(2)}, u32[]{:S(2)}) async-start(f32[4,12,4,8,128]{4,3,1,2,0:T(8,128)} %copy.79), calls=%async_computation | async-start | bytes 1572864 | tf_op jit(solution)/shard_map/all_to_all | solution.py:150
  103.7 0.9 concatenate.35
  104.7 1.3 fusion.40
  109.8 8.8 %all-to-all-done = f32[4,12,4,8,128]{4,3,1,2,0:T(8,128)S(1)} async-done(((f32[4,12,4,8,128]{4,3,1,2,0:T(8,128)}), f32[4,12,4,8,128]{4,3,1,2,0:T(8,128)S(1)}, u32[]{:S(2)}, u32[]{:S(2)}) %all-to-all-start) | async-done | bytes 786464 | tf_op jit(solution)/shard_map/all_to_all | solution.py:150
  119.2 5.6 %all_gather.15 = bf16[8,3,4096]{2,1,0:T(4,128)(2,1)S(1)} all-gather(bf16[4,3,4096]{2,1,0:T(4,128)(2,1)S(1)} %fusion.13), channel_id=1, replica_groups=mesh['groups'=2,'seq'=4,'adapter'=2,'head'=2] {'adapter'}, dimensions={0}, use_global_device_ids=true | all-gather | bytes 294912 | tf_op jit(solution)/shard_map/all_gather | solution.py:167
  125.2 3.3 %psum.15 = bf16[8,3,1,64]{3,0,1,2:T(8,128)(2,1)S(1)} all-reduce(f32[8,3,1,64]{3,0,1,2:T(8,128)S(1)} %convolution_bitcast_fusion.1), channel_id=1, replica_groups=mesh['groups'=2,'seq'=4,'adapter'=2,'head'=2] {'head'}, use_global_device_ids=true, to_apply=%region_9.10 | all-reduce | flops 1536 | bytes 9216 | tf_op jit(solution)/shard_map/psum | solution.py:172
  128.5 0.9 convolution_convert_fusion
  130.2 19.8 %all-reduce.8.cloned.1.call-done = bf16[8,3,4096]{2,0,1:T(8,128)(2,1)} async-done(((bf16[8,3,4096]{2,0,1:T(8,128)(2,1)}), bf16[8,3,4096]{2,0,1:T(8,128)(2,1)}) %all-reduce.8.cloned.1.call-update) | async-done | bytes 196624
  150.0 1.6 %constant_dynamic-slice_fusion = bf16[4,3,4096]{2,0,1:T(4,128)(2,1)} fusion(bf16[8,3,4096]{2,0,1:T(8,128)(2,1)} %all-reduce.8.cloned.1.call-done, u32[]{:T(128)S(6)} %multiply.11), kind=kLoop, calls=%fused_computation.59 | loop fusion | bytes 196612
  (91 shorter events, 11.7 us)
Async XLA Ops:
  7.2 19.3 %copy-start = (bf16[1,64,4096]{2,1,0:T(8,128)(2,1)S(1)}, bf16[1,64,4096]{2,1,0:T(8,128)(2,1)}, u32[]{:S(2)}) copy-start(bf16[1,64,4096]{2,1,0:T(8,128)(2,1)} %param.19) | copy-start | bytes 1572868
  7.2 29.1 %copy-start.7 = (bf16[2,4,32,512]{3,2,1,0:T(8,128)(2,1)S(1)}, bf16[2,4,32,512]{3,2,1,0:T(8,128)(2,1)}, u32[]{:S(2)}) copy-start(bf16[2,4,32,512]{3,2,1,0:T(8,128)(2,1)} %param.14) | copy-start | bytes 786436
  7.2 48.0 %copy-start.8 = (bf16[4,3,4096]{2,0,1:T(4,128)(2,1)S(1)}, bf16[4,3,4096]{2,0,1:T(4,128)(2,1)}, u32[]{:S(2)}) copy-start(bf16[4,3,4096]{2,0,1:T(4,128)(2,1)} %param.12) | copy-start | bytes 294916
  7.2 48.0 %all-reduce.6.cloned.1.call-start = ((), (), s32[]{:S(2)}) async-start(), calls=%async_computation.3 | async-start | bytes 786432
  56.5 0.6 copy-start.5
  56.5 0.7 copy-start.6
  74.3 2.7 %copy-start.1 = (f32[4,48,8,1024]{3,2,1,0:T(8,128)}, f32[4,48,8,1024]{3,2,1,0:T(8,128)S(1)}, u32[]{:S(2)}) copy-start(f32[4,48,8,1024]{3,2,1,0:T(8,128)S(1)} %get-tuple-element.44) | copy-start | bytes 18874372
  79.2 11.0 %all-to-all-start.2 = ((f32[4,1,384]{2,1,0:T(1,128)}), f32[4,1,384]{2,1,0:T(1,128)S(1)}, u32[]{:S(2)}, u32[]{:S(2)}) async-start(f32[4,1,384]{2,1,0:T(1,128)} %reshape.257), calls=%async_computation.2 | async-start | bytes 12288 | tf_op jit(solution)/shard_map/all_to_all | solution.py:152
  85.1 18.4 %copy-start.10 = (pred[4,35]{1,0:T(4,128)(4,1)S(1)}, pred[4,35]{1,0:T(4,128)(4,1)}, u32[]{:S(2)}) copy-start(pred[4,35]{1,0:T(4,128)(4,1)} %iota_compare_fusion.1) | copy-start | bytes 424
  85.1 18.4 %copy-start.11 = (pred[3,35]{1,0:T(4,128)(4,1)S(1)}, pred[3,35]{1,0:T(4,128)(4,1)}, u32[]{:S(2)}) copy-start(pred[3,35]{1,0:T(4,128)(4,1)} %iota_compare_fusion) | copy-start | bytes 319
  85.2 18.4 %copy-start.9 = (bf16[1,4,3,512]{3,1,2,0:T(4,128)(2,1)S(1)}, bf16[1,4,3,512]{3,1,2,0:T(4,128)(2,1)}, u32[]{:S(2)}) copy-start(bf16[1,4,3,512]{3,1,2,0:T(4,128)(2,1)} %get-tuple-element.37) | copy-start | bytes 36868
  85.2 19.5 %copy-start.4 = (bf16[1,4,32,512]{3,2,1,0:T(8,128)(2,1)S(1)}, bf16[1,4,32,512]{3,2,1,0:T(8,128)(2,1)}, u32[]{:S(2)}) copy-start(bf16[1,4,32,512]{3,2,1,0:T(8,128)(2,1)} %get-tuple-element.34) | copy-start | bytes 393220
  90.2 8.8 %all-to-all-start.1 = ((f32[4,1,384]{2,1,0:T(1,128)}), f32[4,1,384]{2,1,0:T(1,128)S(1)}, u32[]{:S(2)}, u32[]{:S(2)}) async-start(f32[4,1,384]{2,1,0:T(1,128)} %reshape.259), calls=%async_computation.1 | async-start | bytes 12288 | tf_op jit(solution)/shard_map/all_to_all | solution.py:151
  97.4 27.4 %copy-start.3 = (bf16[1,64,4096]{2,1,0:T(8,128)(2,1)S(1)}, bf16[1,64,4096]{2,1,0:T(8,128)(2,1)}, u32[]{:S(2)}) copy-start(bf16[1,64,4096]{2,1,0:T(8,128)(2,1)} %param.20) | copy-start | bytes 1572868
  98.4 30.1 %copy-start.2 = (bf16[1,64,4096]{2,1,0:T(8,128)(2,1)S(1)}, bf16[1,64,4096]{2,1,0:T(8,128)(2,1)}, u32[]{:S(2)}) copy-start(bf16[1,64,4096]{2,1,0:T(8,128)(2,1)} %param.21) | copy-start | bytes 1572868
  99.0 19.7 %all-to-all-start = ((f32[4,12,4,8,128]{4,3,1,2,0:T(8,128)}), f32[4,12,4,8,128]{4,3,1,2,0:T(8,128)S(1)}, u32[]{:S(2)}, u32[]{:S(2)}) async-start(f32[4,12,4,8,128]{4,3,1,2,0:T(8,128)} %copy.79), calls=%async_computation | async-start | bytes 1572864 | tf_op jit(solution)/shard_map/all_to_all | solution.py:150
  103.6 46.4 %all-reduce.8.cloned.1.call-start = ((), (), s32[]{:S(2)}) async-start(), calls=%async_computation.4 | async-start | bytes 393216
Sparse Core Ops, SparseCore 0:
  27.6 27.5 all-reduce.5
  129.5 20.4 all-reduce.7
where the time goes:
time: 159 us; the launch traced here: 158 us
  waiting for transfers between devices  51.6 us (32%)
  blocking collectives  38.7 us (24%)
  local copies, waits for them, and re-layouts  21.6 us (14%)
  between operations  15.8 us (10%)
  starting transfers between devices  13.3 us (8%)
  matrix products  10.3 us (6%)
  other arithmetic  7.28 us (5%)
    unnamed x4, waiting for transfers between devices  38.1 us
    all_gather x1, blocking collectives, on_device(): gathered = lax.all_gather(query_flat, 'seq', axis=0, tiled=True)  15.6 us
    unnamed x37, local copies, waits for them, and re-layouts  12.4 us
    all_to_all x1, waiting for transfers between devices, on_device(): lax.all_to_all(weighted, 'seq', split_axis=0, concat_axis=0, tiled=True)  8.84 us
    all_gather x1, blocking collectives, on_device(): lax.all_gather(hidden, 'adapter', axis=0, tiled=True)  5.64 us
    all_gather x1, blocking collectives, on_device(): relocated_output = lax.all_gather(attended, 'adapter', axis=0, tiled=True)  5.64 us
    all_to_all x1, starting transfers between devices, on_device(): lax.all_to_all(totals, 'seq', split_axis=0, concat_axis=0, tiled=True)  5.38 us
    unnamed x1, blocking collectives  5.19 us
  transfers between devices with their start and end apart: 5, of which 5 were waited for; matrix products, arithmetic and copies ran while one was open for 14% of the time, Pallas kernels for 0%

commit v1 on v0

v1 whole, which is shorter than its diff:
```python
import functools
import math

import jax
import jax.numpy as jnp
from jax import lax
from jax.experimental import pallas as pl
from jax.experimental.pallas import tpu as pltpu
from jax.sharding import PartitionSpec as P

HEAD_SIZE = 128
LANES = 128
rope_base = 1000000.0
MASKED = -1e30

VMEM = pl.BlockSpec(memory_space=pltpu.VMEM)
SMEM = pl.BlockSpec(memory_space=pltpu.SMEM)
F32 = jnp.float32
BF16 = jnp.bfloat16


def peer(index, offset, size):
    if size & (size - 1) == 0:
        return index ^ offset
    return (index + offset) % size


def fetch(value, axis, offset):
    size = lax.axis_size(axis)
    return lax.ppermute(value, axis, [(peer(i, offset, size), i) for i in range(size)])


def send(value, axis, offset):
    size = lax.axis_size(axis)
    return lax.ppermute(value, axis, [(i, peer(i, offset, size)) for i in range(size)])


def dot(left, right, contract):
    return lax.dot_general(left, right, (contract, ((), ())), preferred_element_type=F32)


def call(kernel, out_shape, args, specs=None, scratch=(), flops=1 << 20, vmem=24 << 20):
    return pl.pallas_call(
        kernel,
        out_shape=out_shape,
        in_specs=specs or [VMEM] * len(args),
        out_specs=jax.tree.map(lambda unused: VMEM, out_shape),
        scratch_shapes=scratch,
        compiler_params=pltpu.CompilerParams(vmem_limit_bytes=vmem),
        cost_estimate=pl.CostEstimate(flops=flops, bytes_accessed=1 << 20, transcendentals=0),
    )(*args)


def row_values(ref, rows, shape):
    row = lax.broadcasted_iota(jnp.int32, shape, 0) % rows
    out = jnp.zeros(shape, jnp.int32)
    for r in range(rows):
        out = jnp.where(row == r, ref[r], out)
    return out


def pack_kernel(base_ref, length_ref, id_ref, out_ref):
    steps, rows, width = base_ref.shape
    lane = lax.broadcasted_iota(jnp.int32, (rows, LANES), 1)
    lengths = row_values(length_ref, rows, (rows, LANES))
    ids = row_values(id_ref, rows, (rows, LANES))
    for t in range(steps):
        out_ref[t, :, :width] = base_ref[t]
        meta = jnp.where(lane == 0, lengths + t, jnp.where(lane == 1, ids, 0))
        out_ref[t, :, width:] = meta.astype(F32).astype(BF16)


def rank_kernel(adapters, *refs):
    hidden = refs[:adapters]
    down_ref, out_ref, gathered = refs[adapters:]
    steps, rows, width = hidden[0].shape
    pad_rows = out_ref.shape[3]
    resident, rank, _ = down_ref.shape
    gathered[...] = jnp.zeros_like(gathered)
    for j in range(adapters):
        for t in range(steps):
            at = j * pad_rows + t * rows
            gathered[at : at + rows, :] = hidden[j][t].astype(F32)
    result = dot(
        gathered[...].astype(BF16), down_ref[...].reshape(resident * rank, width), ((1,), (1,))
    )
    high = result.astype(BF16).astype(F32)
    low = result - high
    both = jnp.concatenate([high, low], axis=1).astype(BF16)
    me = lax.axis_index("adapter")
    for j in range(adapters):
        block = both[j * pad_rows : (j + 1) * pad_rows]
        target = peer(me, j, adapters)
        for s in range(out_ref.shape[0]):
            for h in range(out_ref.shape[2]):
                out_ref[s, target, h] = block


def rope_kernel(count, *refs):
    pieces = refs[:count]
    table_ref, out_ref, aux_ref = refs[count:]
    steps, rows, full = pieces[0].shape
    width = full - LANES
    tokens = out_ref.shape[0]
    for i in range(count):
        for t in range(steps):
            at = (i * steps + t) * rows
            out_ref[at : at + rows, :] = pieces[i][t, :, :width].astype(F32)
            aux_ref[at : at + rows, 2 * LANES :] = pieces[i][t, :, width:].astype(F32)
    meta = aux_ref[:, 2 * LANES :]
    slots = table_ref.shape[0]
    picked = lax.broadcasted_iota(jnp.int32, (tokens, slots), 1).astype(F32) == meta[:, 0:1]
    angles = lax.dot_general(
        picked.astype(F32),
        table_ref[...],
        (((1,), (0,)), ((), ())),
        precision=lax.Precision.HIGHEST,
        preferred_element_type=F32,
    )
    aux_ref[:, : 2 * LANES] = angles
    cos_part, sin_part = angles[:, :LANES], angles[:, LANES:]
    for h in range(width // HEAD_SIZE):
        at = pl.ds(h * HEAD_SIZE, HEAD_SIZE)
        piece = out_ref[:, at]
        out_ref[:, at] = piece * cos_part + pltpu.roll(piece, HEAD_SIZE // 2, 1) * sin_part


def attend(query, key, value, scale, extra=None):
    scores = dot(query, key, ((1,), (1,)))
    if extra is not None:
        more_key, more_value, bias = extra
        scores = jnp.concatenate([scores, dot(query, more_key, ((1,), (1,))) + bias], axis=1)
        value = jnp.concatenate([value, more_value], axis=0)
    peaks = jnp.max(scores, axis=1, keepdims=True)
    weight = jnp.exp2((scores - peaks) * scale).astype(BF16)
    ones = jnp.ones((value.shape[0], LANES), BF16)
    summed = dot(weight, jnp.concatenate([value, ones], axis=1), ((1,), (0,)))
    total = summed[:, HEAD_SIZE:]
    return summed[:, :HEAD_SIZE] / total, peaks * scale + jnp.log2(total)


def split_stat(stat, heads):
    first = stat.astype(BF16).astype(F32)
    second = (stat - first).astype(BF16).astype(F32)
    third = stat - first - second
    lane = lax.broadcasted_iota(jnp.int32, stat.shape, 1)
    out = jnp.where(lane < heads, first, 0.0)
    out = jnp.where((lane >= heads) & (lane < 2 * heads), pltpu.roll(second, heads, 1), out)
    out = jnp.where(
        (lane >= 2 * heads) & (lane < 3 * heads), pltpu.roll(third, 2 * heads, 1), out
    )
    return out


def store_messages(out_refs, kept, stats, steps, rows, heads):
    width = kept.shape[1]
    packed = split_stat(stats[...], heads)
    for i, ref in enumerate(out_refs):
        for t in range(steps):
            at = (i * steps + t) * rows
            ref[t, :, :width] = kept[at : at + rows, :].astype(BF16)
            ref[t, :, width:] = packed[at : at + rows, :].astype(BF16)


def far_kernel(order, split, adapters, scale, *refs):
    rope_ref, aux_ref, rank_ref = refs[:3]
    ups = refs[3 : 3 + adapters]
    kv_ref = refs[3 + adapters]
    out_refs = refs[4 + adapters : 4 + adapters + split]
    query_ref, ranks, kept, stats = refs[4 + adapters + split :]
    steps, rows, _ = out_refs[0].shape
    tokens = steps * rows
    seq_count, _, halves, pad_rows, double = rank_ref.shape
    depth = double // 2
    resident, rank, width = ups[0].shape
    heads = width // HEAD_SIZE
    kv_heads = kv_ref.shape[2] // HEAD_SIZE
    group = heads // kv_heads
    z, x = lax.axis_index("seq"), lax.axis_index("adapter")
    for i, k in enumerate(order):
        columns = []
        for j in range(adapters):
            total = jnp.zeros((pad_rows, double), F32)
            for h in range(halves):
                total += rank_ref[peer(z, k, seq_count), peer(x, j, adapters), h].astype(F32)
            columns.append(total[:, :depth] + total[:, depth:])
        ranks[i * tokens : (i + 1) * tokens, :] = jnp.concatenate(columns, axis=1)[:tokens]
    ids = aux_ref[:, 2 * LANES + 1 : 2 * LANES + 2]
    lane = lax.broadcasted_iota(jnp.int32, ranks.shape, 1)
    owner = (peer(x, lane // depth, adapters) * resident + lane % depth // rank).astype(F32)
    chosen = jnp.where(owner == ids, ranks[...], 0.0).astype(BF16)
    cos_part, sin_part = aux_ref[:, :LANES], aux_ref[:, LANES : 2 * LANES]
    cut = split * tokens
    lane = lax.broadcasted_iota(jnp.int32, (cut, LANES), 1)
    for kv in range(kv_heads):
        first = kv * group * HEAD_SIZE
        factors = jnp.concatenate(
            [up[u, :, first : first + group * HEAD_SIZE] for up in ups for u in range(resident)],
            axis=0,
        )
        delta = dot(chosen, factors, ((1,), (0,)))
        near, far = [], []
        for g in range(group):
            piece = delta[:, g * HEAD_SIZE : (g + 1) * HEAD_SIZE]
            turned = piece * cos_part + pltpu.roll(piece, HEAD_SIZE // 2, 1) * sin_part
            turned += rope_ref[:, first + g * HEAD_SIZE : first + (g + 1) * HEAD_SIZE]
            far.append(turned[:cut])
            near.append(turned[cut:])
        query_ref[kv] = jnp.concatenate(near, axis=0).astype(BF16)
        at = pl.ds(kv * HEAD_SIZE, HEAD_SIZE)
        result, level = attend(
            jnp.concatenate(far, axis=0).astype(BF16), kv_ref[0, :, at], kv_ref[1, :, at], scale
        )
        for g in range(group):
            head = kv * group + g
            kept[:, head * HEAD_SIZE : (head + 1) * HEAD_SIZE] = result[g * cut : (g + 1) * cut]
            piece = level[g * cut : (g + 1) * cut]
            stats[...] = jnp.where(lane == head, piece, stats[...] if head else 0.0)
    store_messages(out_refs, kept, stats, steps, rows, heads)


def near_kernel(split, scale, *refs):
    query_ref, kv_ref, suffix_ref, fresh_ref, length_ref = refs[:5]
    out_refs = refs[5 : 5 + split - 1]
    own_ref, level_ref, kept, stats, fresh_rows = refs[5 + split - 1 :]
    _, steps, rows, _ = fresh_ref.shape
    slots = suffix_ref.shape[2]
    width = kept.shape[1]
    heads = width // HEAD_SIZE
    kv_heads = kv_ref.shape[2] // HEAD_SIZE
    group = heads // kv_heads
    tokens = steps * rows
    cut = split * tokens
    fresh_slots = fresh_rows.shape[1]
    fresh_rows[...] = jnp.zeros_like(fresh_rows)
    for part in range(2):
        for t in range(steps):
            fresh_rows[part, t * rows : (t + 1) * rows, :] = fresh_ref[part, t].astype(F32)
    suffix_count = rows * slots
    shape = (cut, suffix_count + fresh_slots)
    token = lax.broadcasted_iota(jnp.int32, shape, 0)
    column = lax.broadcasted_iota(jnp.int32, shape, 1)
    token_row, token_step = token % rows, token // rows
    fresh_at = column - suffix_count
    in_suffix = (column < suffix_count) & (column // slots == token_row)
    in_suffix &= column % slots < row_values(length_ref, rows, shape)
    in_fresh = (column >= suffix_count) & (fresh_at % rows == token_row)
    in_fresh &= fresh_at // rows <= token_step
    bias = jnp.where((in_suffix | in_fresh) & (token < tokens), 0.0, MASKED)
    bias = jnp.concatenate([bias] * group, axis=0)
    lane = lax.broadcasted_iota(jnp.int32, (cut, LANES), 1)
    for kv in range(kv_heads):
        at = pl.ds(kv * HEAD_SIZE, HEAD_SIZE)
        more = [
            jnp.concatenate(
                [suffix_ref[part, r, :, at] for r in range(rows)]
                + [fresh_rows[part, :, at].astype(BF16)],
                axis=0,
            )
            for part in range(2)
        ]
        result, level = attend(
            query_ref[kv], kv_ref[0, :, at], kv_ref[1, :, at], scale, (more[0], more[1], bias)
        )
        for g in range(group):
            head = kv * group + g
            kept[:, head * HEAD_SIZE : (head + 1) * HEAD_SIZE] = result[g * cut : (g + 1) * cut]
            piece = level[g * cut : (g + 1) * cut]
            stats[...] = jnp.where(lane == head, piece, stats[...] if head else 0.0)
    for t in range(steps):
        own_ref[t] = kept[t * rows : (t + 1) * rows, :]
        level_ref[t] = stats[t * rows : (t + 1) * rows, :]
    packed = split_stat(stats[...], heads)
    for i, ref in enumerate(out_refs):
        for t in range(steps):
            at = ((i + 1) * steps + t) * rows
            ref[t, :, :width] = kept[at : at + rows, :].astype(BF16)
            ref[t, :, width:] = packed[at : at + rows, :].astype(BF16)


def merge_kernel(messages, adapters, *refs):
    own_ref, level_ref = refs[:2]
    arrived = refs[2 : 2 + messages]
    downs = refs[2 + messages : 2 + messages + adapters]
    id_ref, out_ref, rank_ref, rows_ref = refs[2 + messages + adapters :]
    steps, rows, width = own_ref.shape
    heads = width // HEAD_SIZE
    resident, rank, _ = downs[0].shape
    depth = resident * rank
    x = lax.axis_index("adapter")
    rows_ref[...] = jnp.zeros_like(rows_ref)
    for t in range(steps):
        levels = [level_ref[t]]
        for ref in arrived:
            packed = ref[t, :, width:].astype(F32)
            count = packed.shape[1]
            levels.append(
                packed
                + pltpu.roll(packed, count - heads, 1)
                + pltpu.roll(packed, count - 2 * heads, 1)
            )
        highest = functools.reduce(jnp.maximum, levels)
        shares = [jnp.exp2(level - highest) for level in levels]
        total = functools.reduce(jnp.add, shares)
        shares = [share / total for share in shares]
        for h in range(heads):
            at = pl.ds(h * HEAD_SIZE, HEAD_SIZE)
            mixed = own_ref[t, :, at] * shares[0][:, h : h + 1]
            for ref, share in zip(arrived, shares[1:]):
                mixed += ref[t, :, at].astype(F32) * share[:, h : h + 1]
            out_ref[t, :, at] = mixed.astype(BF16)
            rows_ref[t * rows : (t + 1) * rows, at] = mixed
    factors = jnp.concatenate([down[u] for down in downs for u in range(resident)], axis=0)
    result = dot(rows_ref[...].astype(BF16), factors, ((1,), (1,)))
    ids = row_values(id_ref, rows, result.shape)
    lane = lax.broadcasted_iota(jnp.int32, result.shape, 1)
    owner = peer(x, lane // depth, adapters) * resident + lane % depth // rank
    rank_ref[...] = jnp.where(owner == ids, result, 0.0)


def up_kernel(parts, adapters, *refs):
    ranks = refs[:parts]
    ups = refs[parts : parts + adapters]
    out_ref = refs[parts + adapters]
    steps, rows, width = out_ref.shape
    resident = ups[0].shape[0]
    chosen = functools.reduce(jnp.add, [ref[...] for ref in ranks]).astype(BF16)
    factors = jnp.concatenate([up[u] for up in ups for u in range(resident)], axis=0)
    result = dot(chosen, factors, ((1,), (0,)))
    for t in range(steps):
        out_ref[t] = result[t * rows : (t + 1) * rows].astype(BF16)


def rope_table(slots, first_position):
    half_dim = HEAD_SIZE // 2
    frequency = rope_base ** (-2.0 * jnp.arange(half_dim, dtype=F32) / HEAD_SIZE)
    position = (first_position + jnp.arange(slots, dtype=jnp.int32)).astype(F32)
    angles = position[:, None] * frequency
    cos_part, sin_part = jnp.cos(angles), jnp.sin(angles)
    return jnp.concatenate([cos_part, cos_part, -sin_part, sin_part], axis=1)


def on_device(
    hidden,
    base_query_rows,
    fresh_key_value,
    suffix_key_value,
    suffix_length,
    row_adapter_index,
    prompt_key_value,
    query_down_factors,
    query_up_factors,
    output_down_factors,
    output_up_factors,
):
    rows, steps, width = hidden.shape
    seq_count, adapters, halves = (lax.axis_size(name) for name in ("seq", "adapter", "head"))
    slots = suffix_key_value.shape[2]
    resident, rank, _ = query_down_factors.shape
    depth = resident * rank
    tokens = rows * steps
    pad_rows = -(-tokens // 16) * 16
    heads = width // HEAD_SIZE
    kv_heads = prompt_key_value.shape[2] // HEAD_SIZE
    group = heads // kv_heads
    scale = math.log2(math.e) / math.sqrt(HEAD_SIZE)
    stat_lanes = -(-3 * heads // LANES) * LANES
    ids = row_adapter_index.reshape(-1)
    hidden = hidden.transpose(1, 0, 2)
    base = base_query_rows.transpose(1, 0, 2)
    fresh = fresh_key_value.transpose(0, 2, 1, 3)

    hidden_of = [hidden] + [fetch(hidden, "adapter", j) for j in range(1, adapters)]
    query_ups = [query_up_factors] + [
        fetch(query_up_factors, "adapter", j) for j in range(1, adapters)
    ]
    packed = call(
        pack_kernel,
        jax.ShapeDtypeStruct((steps, rows, width + LANES), BF16),
        (base, suffix_length, ids),
        [VMEM, SMEM, SMEM],
    )
    split = seq_count // 2
    order = list(range(seq_count - 1, split - 1, -1)) + list(range(split))
    pieces = [fetch(packed, "seq", k) if k else packed for k in order]
    table_slots = -(-(slots + steps) // 8) * 8
    table = rope_table(table_slots, prompt_key_value.shape[1] * seq_count)
    roped, aux = call(
        functools.partial(rope_kernel, seq_count),
        (
            jax.ShapeDtypeStruct((seq_count * tokens, width), F32),
            jax.ShapeDtypeStruct((seq_count * tokens, 3 * LANES), F32),
        ),
        (*pieces, table),
        flops=1 << 34,
    )
    rank_parts = call(
        functools.partial(rank_kernel, adapters),
        jax.ShapeDtypeStruct((seq_count, adapters, halves, pad_rows, 2 * depth), BF16),
        (*hidden_of, query_down_factors),
        scratch=[pltpu.VMEM((adapters * pad_rows, width), F32)],
    )
    spread = (seq_count * adapters * halves,) + rank_parts.shape[3:]
    rank_parts = lax.all_to_all(
        rank_parts.reshape(spread),
        ("seq", "adapter", "head"),
        split_axis=0,
        concat_axis=0,
        tiled=True,
    ).reshape(rank_parts.shape)

    message = jax.ShapeDtypeStruct((steps, rows, width + stat_lanes), BF16)
    *far_messages, near_query = call(
        functools.partial(far_kernel, order, seq_count - split, adapters, scale),
        (message,) * (seq_count - split)
        + (jax.ShapeDtypeStruct((kv_heads, group * split * tokens, HEAD_SIZE), BF16),),
        (roped, aux, rank_parts, *query_ups, prompt_key_value),
        scratch=[
            pltpu.VMEM((seq_count * tokens, adapters * depth), F32),
            pltpu.VMEM(((seq_count - split) * tokens, width), F32),
            pltpu.VMEM(((seq_count - split) * tokens, LANES), F32),
        ],
    )
    output_downs = [output_down_factors] + [
        fetch(output_down_factors, "adapter", j) for j in range(1, adapters)
    ]
    output_ups = [output_up_factors] + [
        fetch(output_up_factors, "adapter", j) for j in range(1, adapters)
    ]
    arrived = [send(part, "seq", k) for part, k in zip(far_messages, order)]
    fresh_slots = -(-tokens // LANES) * LANES
    *near_messages, own, level = call(
        functools.partial(near_kernel, split, scale),
        (message,) * (split - 1)
        + (
            jax.ShapeDtypeStruct((steps, rows, width), F32),
            jax.ShapeDtypeStruct((steps, rows, LANES), F32),
        ),
        (near_query, prompt_key_value, suffix_key_value, fresh, suffix_length),
        [VMEM] * 4 + [SMEM],
        scratch=[
            pltpu.VMEM((split * tokens, width), F32),
            pltpu.VMEM((split * tokens, LANES), F32),
            pltpu.VMEM((2, fresh_slots, fresh.shape[3]), F32),
        ],
    )
    arrived += [send(part, "seq", k) for part, k in zip(near_messages, order[seq_count - split + 1 :])]
    attended, out_rank = call(
        functools.partial(merge_kernel, seq_count - 1, adapters),
        (
            jax.ShapeDtypeStruct((steps, rows, width), BF16),
            jax.ShapeDtypeStruct((pad_rows, adapters * depth), F32),
        ),
        (own, level, *arrived, *output_downs, ids),
        [VMEM] * (2 + len(arrived) + adapters) + [SMEM],
        scratch=[pltpu.VMEM((pad_rows, width), F32)],
    )
    out_ranks = [out_rank] + [fetch(out_rank, "head", j) for j in range(1, halves)]
    adapted = call(
        functools.partial(up_kernel, halves, adapters),
        jax.ShapeDtypeStruct((steps, rows, width), BF16),
        (*out_ranks, *output_ups),
    )
    return attended.transpose(1, 0, 2), adapted.transpose(1, 0, 2)


def solution(mesh):
    rows = ("groups", "seq", "adapter")
    factors = P(("groups", "adapter"), None, "head")
    placed = (
        P(rows, None, "head"),
        P(rows, None, "head"),
        P(None, rows, None, "head"),
        P(None, rows, None, "head"),
        P(rows),
        P(rows, None),
        P(None, ("groups", "seq"), "head"),
        factors,
        factors,
        factors,
        factors,
    )
    return jax.shard_map(
        on_device,
        mesh=mesh,
        in_specs=placed,
        out_specs=(P(rows, None, "head"), P(rows, None, "head")),
        check_vma=False,
    )
```

time: 159 us -> 64.1 us (0.40)
  blocking collectives: 38.7 us -> 0 us
  waiting for transfers between devices: 51.6 us -> 18.1 us
  between operations: 15.8 us -> 0.78 us
  Pallas kernels: 0 us -> 11.3 us
  matrix products: 10.3 us -> 0 us
  local copies, waits for them, and re-layouts: 21.6 us -> 11.5 us
  starting transfers between devices: 13.3 us -> 20.9 us
  other arithmetic: 7.28 us -> 0.88 us
    unnamed x4 -> x0, waiting for transfers between devices: 38.1 us -> none
    all_gather x3 -> x0, blocking collectives: 26.9 us -> none  [the longest x1 15.6 us: on_device(): gathered = lax.all_gather(query_flat, 'seq', axis=0, tiled=True)]
    ppermute x0 -> x11, starting transfers between devices: none -> 15.9 us  [the longest x8 11.5 us: fetch(): lax.ppermute(value, axis, [(peer(i, offset, size), i) for i in range(size)])]
    ppermute x0 -> x11, waiting for transfers between devices: none -> 13.4 us  [the longest x3 9.37 us: send(): lax.ppermute(value, axis, [(i, peer(i, offset, size)) for i in range(size)])]
    pallas_call x0 -> x7, Pallas kernels: none -> 11.3 us  [call(): pl.pallas_call(kernel, out_shape=out_shape, in_specs=specs or [VMEM] * le...]
    dot_general x8 -> x0, matrix products: 10.3 us -> none  [the longest x1 4.01 us: prompt_block(): jnp.einsum('nkgp,pkd->nkgd', weight, prompt_values, preferred_element_typ...]
    all_to_all x3 -> x1, waiting for transfers between devices: 13.5 us -> 4.69 us  [on_device(): lax.all_to_all(rank_parts.reshape(spread), ('seq', 'adapter', 'head'), sp...]
    all_to_all x3 -> x1, starting transfers between devices: 13.2 us -> 4.99 us  [on_device(): lax.all_to_all(rank_parts.reshape(spread), ('seq', 'adapter', 'head'), sp...]
  transfers between devices with their start and end apart: 5 -> 12, of which waited for: 5 -> 6; matrix products, arithmetic and copies ran while one was open for 14% -> 1% of each run, Pallas kernels for 0% -> 16%
where the time goes in v1:
time: 64.1 us; the launch traced here: 63.5 us
  starting transfers between devices  20.9 us (33%)
  waiting for transfers between devices  18.1 us (28%)
  local copies, waits for them, and re-layouts  11.5 us (18%)
  Pallas kernels  11.3 us (18%)
  other arithmetic  0.88 us (1%)
  between operations  0.78 us (1%)
    ppermute x8, starting transfers between devices, fetch(): lax.ppermute(value, axis, [(peer(i, offset, size), i) for i in range(size)])  11.5 us
    unnamed x44, local copies, waits for them, and re-layouts  11.5 us
    pallas_call x7, Pallas kernels, call(): pl.pallas_call(kernel, out_shape=out_shape, in_specs=specs or [VMEM] * le...  11.3 us
    ppermute x3, waiting for transfers between devices, send(): lax.ppermute(value, axis, [(i, peer(i, offset, size)) for i in range(size)])  9.37 us
    all_to_all x1, starting transfers between devices, on_device(): lax.all_to_all(rank_parts.reshape(spread), ('seq', 'adapter', 'head'), sp...  4.99 us
    all_to_all x1, waiting for transfers between devices, on_device(): lax.all_to_all(rank_parts.reshape(spread), ('seq', 'adapter', 'head'), sp...  4.69 us
    ppermute x3, starting transfers between devices, send(): lax.ppermute(value, axis, [(i, peer(i, offset, size)) for i in range(size)])  4.44 us
    ppermute x8, waiting for transfers between devices, fetch(): lax.ppermute(value, axis, [(peer(i, offset, size), i) for i in range(size)])  4.07 us
  transfers between devices with their start and end apart: 12, of which 6 were waited for; matrix products, arithmetic and copies ran while one was open for 1% of the time, Pallas kernels for 16%

profile of v1, /device:TPU:0, one launch (start us, length us, event | category | flops | bytes accessed | tf_op | source)
XLA Modules:
  0.0 63.5 jit_solution(15123682489235793665)
XLA Ops:
  0.6 0.9 %copy-done.9 = bf16[4,3,4096]{2,0,1:T(4,128)(2,1)S(1)} copy-done((bf16[4,3,4096]{2,0,1:T(4,128)(2,1)S(1)}, bf16[4,3,4096]{2,0,1:T(4,128)(2,1)}, u32[]{:S(2)}) %copy-start.9) | copy-done | bytes 98328
  1.5 0.7 %copy-done.12 = s32[4,1]{0,1:T(1,128)S(1)} copy-done((s32[4,1]{0,1:T(1,128)S(1)}, s32[4,1]{0,1:T(1,128)}, u32[]{:S(2)}) %copy-start.12) | copy-done | bytes 40
  2.2 0.7 %copy-done.14 = s32[4]{0:T(128)S(1)} copy-done((s32[4]{0:T(128)S(1)}, s32[4]{0:T(128)}, u32[]{:S(2)}) %copy-start.14) | copy-done | bytes 40
  3.4 3.1 %collective-permute-start.2 = (bf16[3,4,4224]{2,1,0:T(4,128)(2,1)S(1)}, bf16[3,4,4224]{2,1,0:T(4,128)(2,1)S(1)}, u32[]{:S(2)}, u32[]{:S(2)}) collective-permute-start(bf16[3,4,4224]{2,1,0:T(4,128)(2,1)S(1)} %shard_map.122.refs_2_), channel_id=1, source_target_pairs={{4,0},{0,4},{12,8},{8,12},{5,1},{1,5},{13,9},{9,13},{6,2},{2,6},{1... | collective-permute-start | bytes 304136 | tf_op jit(solution)/shard_map/ppermute | solution.py:30
  6.5 2.6 %collective-permute-start.1 = (bf16[3,4,4224]{2,1,0:T(4,128)(2,1)S(1)}, bf16[3,4,4224]{2,1,0:T(4,128)(2,1)S(1)}, u32[]{:S(2)}, u32[]{:S(2)}) collective-permute-start(bf16[3,4,4224]{2,1,0:T(4,128)(2,1)S(1)} %shard_map.122.refs_2_), channel_id=1, source_target_pairs={{8,0},{12,4},{0,8},{4,12},{9,1},{13,5},{1,9},{5,13},{10,2},{14,6},... | collective-permute-start | bytes 304136 | tf_op jit(solution)/shard_map/ppermute | solution.py:30
  9.1 1.7 %collective-permute-start.3 = (bf16[3,4,4096]{2,1,0:T(4,128)(2,1)}, bf16[3,4,4096]{2,1,0:T(4,128)(2,1)S(1)}, u32[]{:S(2)}, u32[]{:S(2)}) collective-permute-start(bf16[3,4,4096]{2,1,0:T(4,128)(2,1)} %bitcast.9), channel_id=1, source_target_pairs={{2,0},{0,2},{3,1},{1,3},{6,4},{4,6},{7,5},{5,7},{10,8},{8,10},{11,... | collective-permute-start | bytes 294920 | tf_op jit(solution)/shard_map/ppermute | solution.py:30
  11.3 0.7 %pad_maximum_fusion.refs_4_ = f32[40,256]{1,0:T(8,128)} fusion(f32[40,64]{1,0:T(8,128)S(1)} %get-tuple-element.24, f32[40,64]{1,0:T(8,128)S(1)} %get-tuple-element.23, f32[40,64]{1,0:T(8,128)S(1)} %get-tuple-element.22), kind=kLoop, calls=%fused_computation | loop fusion | flops 30720 | bytes 71680 | tf_op jit(solution)/shard_map/concatenate | solution.py:340
  12.0 2.9 %collective-permute-done.3.refs_1_ = bf16[3,4,4096]{2,1,0:T(4,128)(2,1)S(1)} collective-permute-done((bf16[3,4,4096]{2,1,0:T(4,128)(2,1)}, bf16[3,4,4096]{2,1,0:T(4,128)(2,1)S(1)}, u32[]{:S(2)}, u32[]{:S(2)}) %collective-permute-start.3) | collective-permute-done | bytes 98336 | tf_op jit(solution)/shard_map/ppermute | solution.py:30
  14.9 1.8 %collective-permute-start.8 = (bf16[1,64,4096]{2,1,0:T(8,128)(2,1)}, bf16[1,64,4096]{2,1,0:T(8,128)(2,1)}, u32[]{:S(2)}, u32[]{:S(2)}) collective-permute-start(bf16[1,64,4096]{2,1,0:T(8,128)(2,1)} %refs_5_.3), channel_id=1, source_target_pairs={{2,0},{0,2},{3,1},{1,3},{6,4},{4,6},{7,5},{5,7},{10,8},{8,10},{11,... | collective-permute-start | bytes 1572872 | tf_op jit(solution)/shard_map/ppermute | solution.py:30
  16.7 1.0 %copy-done.1 = bf16[1,64,4096]{2,1,0:T(8,128)(2,1)S(1)} copy-done((bf16[1,64,4096]{2,1,0:T(8,128)(2,1)S(1)}, bf16[1,64,4096]{2,1,0:T(8,128)(2,1)}, u32[]{:S(2)}) %copy-start.1) | copy-done | bytes 524312
  17.8 0.9 %copy-done.8 = bf16[4,3,4096]{2,0,1:T(4,128)(2,1)S(1)} copy-done((bf16[4,3,4096]{2,0,1:T(4,128)(2,1)S(1)}, bf16[4,3,4096]{2,0,1:T(4,128)(2,1)}, u32[]{:S(2)}) %copy-start.8) | copy-done | bytes 98328
  18.7 1.0 %shard_map.124 = bf16[4,2,2,16,128]{4,3,2,1,0:T(8,128)(2,1)} custom-call(bf16[3,4,4096]{2,1,0:T(4,128)(2,1)S(1)} %bitcast.10, bf16[3,4,4096]{2,1,0:T(4,128)(2,1)S(1)} %collective-permute-done.3.refs_1_, bf16[1,64,4096]{2,1,0:T(8,128)(2,1)S(1)} %copy-done.1), custom_call_target="tpu_custom_call" | custom-call | flops 1048576 | bytes 1048576 | tf_op jit(solution)/shard_map/pallas_call | solution.py:43
  19.7 5.0 %all-to-all-start = ((bf16[16,16,128]{2,1,0:T(8,128)(2,1)}), bf16[16,16,128]{2,1,0:T(8,128)(2,1)S(1)}, u32[]{:S(2)}, u32[]{:S(2)}) async-start(bf16[16,16,128]{2,1,0:T(8,128)(2,1)} %bitcast.3), calls=%async_computation | async-start | bytes 131072 | tf_op jit(solution)/shard_map/all_to_all | solution.py:404
  25.3 1.9 %collective-permute-start.10 = (bf16[1,64,4096]{2,1,0:T(8,128)(2,1)}, bf16[1,64,4096]{2,1,0:T(8,128)(2,1)S(1)}, u32[]{:S(2)}, u32[]{:S(2)}) collective-permute-start(bf16[1,64,4096]{2,1,0:T(8,128)(2,1)} %refs_2_.5), channel_id=1, source_target_pairs={{2,0},{0,2},{3,1},{1,3},{6,4},{4,6},{7,5},{5,7},{10,8},{8,10},{11,... | collective-permute-start | bytes 1572872 | tf_op jit(solution)/shard_map/ppermute | solution.py:30
  27.3 0.6 copy-done.18
  27.9 0.6 copy-done.20
  28.5 0.9 %copy-done.7 = bf16[3,4,4224]{2,1,0:T(4,128)(2,1)S(1)} copy-done((bf16[3,4,4224]{2,1,0:T(4,128)(2,1)S(1)}, bf16[3,4,4224]{2,1,0:T(4,128)(2,1)}, u32[]{:S(2)}) %copy-start.7) | copy-done | bytes 101400
  29.4 0.8 %copy-done.10 = f32[40,256]{1,0:T(8,128)S(1)} copy-done((f32[40,256]{1,0:T(8,128)S(1)}, f32[40,256]{1,0:T(8,128)}, u32[]{:S(2)}) %copy-start.10) | copy-done | bytes 40984
  30.2 0.9 %copy-done.17 = bf16[3,4,4224]{2,1,0:T(4,128)(2,1)S(1)} copy-done((bf16[3,4,4224]{2,1,0:T(4,128)(2,1)S(1)}, bf16[3,4,4224]{2,1,0:T(4,128)(2,1)}, u32[]{:S(2)}) %copy-start.17) | copy-done | bytes 101400
  31.1 0.9 %copy-done.19 = bf16[3,4,4224]{2,1,0:T(4,128)(2,1)S(1)} copy-done((bf16[3,4,4224]{2,1,0:T(4,128)(2,1)S(1)}, bf16[3,4,4224]{2,1,0:T(4,128)(2,1)}, u32[]{:S(2)}) %copy-start.19) | copy-done | bytes 101400
  32.0 0.9 %copy-done.21 = bf16[3,4,4224]{2,1,0:T(4,128)(2,1)S(1)} copy-done((bf16[3,4,4224]{2,1,0:T(4,128)(2,1)S(1)}, bf16[3,4,4224]{2,1,0:T(4,128)(2,1)}, u32[]{:S(2)}) %copy-start.21) | copy-done | bytes 101400
  33.3 4.7 %all-to-all-done = bf16[16,16,128]{2,1,0:T(8,128)(2,1)S(1)} async-done(((bf16[16,16,128]{2,1,0:T(8,128)(2,1)}), bf16[16,16,128]{2,1,0:T(8,128)(2,1)S(1)}, u32[]{:S(2)}, u32[]{:S(2)}) %all-to-all-start) | async-done | bytes 65568 | tf_op jit(solution)/shard_map/all_to_all | solution.py:404
  38.0 1.0 %copy-done.4 = bf16[1,64,4096]{2,1,0:T(8,128)(2,1)S(1)} copy-done((bf16[1,64,4096]{2,1,0:T(8,128)(2,1)S(1)}, bf16[1,64,4096]{2,1,0:T(8,128)(2,1)}, u32[]{:S(2)}) %copy-start.4) | copy-done | bytes 524312
  39.0 3.5 %shard_map.125 = (bf16[3,4,4224]{2,1,0:T(4,128)(2,1)S(1)}, bf16[3,4,4224]{2,1,0:T(4,128)(2,1)S(1)}, bf16[4,192,128]{2,1,0:T(8,128)(2,1)S(1)}) custom-call(f32[48,4096]{1,0:T(8,128)S(1)} %get-tuple-element.12.refs_0_, f32[48,384]{1,0:T(8,128)S(1)} %get-tuple-element.13.refs_1_, bf16[4,2,2,16,128]{4,3,2,1,0:T(8,128)(2,1)S(1)} %bitcast.8, ...), custom_call_target="tpu_custom_call" | custom-call | flops 1048576 | bytes 1048576 | tf_op jit(solution)/shard_map/pallas_call | solution.py:43
  42.6 2.3 %shard_map.126 = (bf16[3,4,4224]{2,1,0:T(4,128)(2,1)S(1)}, f32[3,4,4096]{2,1,0:T(4,128)S(1)}, f32[3,4,128]{2,1,0:T(4,128)S(1)}) custom-call(bf16[4,192,128]{2,1,0:T(8,128)(2,1)S(1)} %get-tuple-element.14.refs_0_, bf16[2,1024,512]{2,1,0:T(8,128)(2,1)S(1)} %copy-done, bf16[2,4,32,512]{3,2,1,0:T(8,128)(2,1)S(1)} %copy-done.5, ...), custom_call_target="tpu_custom_call" | custom-call | flops 1048576 | bytes 1048576 | tf_op jit(solution)/shard_map/pallas_call | solution.py:43
  44.9 1.0 %collective-permute-start.7 = (bf16[3,4,4224]{2,1,0:T(4,128)(2,1)S(1)}, bf16[3,4,4224]{2,1,0:T(4,128)(2,1)S(1)}, u32[]{:S(2)}, u32[]{:S(2)}) collective-permute-start(bf16[3,4,4224]{2,1,0:T(4,128)(2,1)S(1)} %get-tuple-element.19), channel_id=1, source_target_pairs={{0,4},{4,0},{8,12},{12,8},{1,5},{5,1},{9,13},{13,9},{2,6},{6,2},{1... | collective-permute-start | bytes 304136 | tf_op jit(solution)/shard_map/ppermute | solution.py:35
  45.9 3.0 %collective-permute-start.5 = (bf16[3,4,4224]{2,1,0:T(4,128)(2,1)S(1)}, bf16[3,4,4224]{2,1,0:T(4,128)(2,1)S(1)}, u32[]{:S(2)}, u32[]{:S(2)}) collective-permute-start(bf16[3,4,4224]{2,1,0:T(4,128)(2,1)S(1)} %get-tuple-element.17), channel_id=1, source_target_pairs={{0,12},{4,8},{8,4},{12,0},{1,13},{5,9},{9,5},{13,1},{2,14},{6,10},... | collective-permute-start | bytes 304136 | tf_op jit(solution)/shard_map/ppermute | solution.py:35
  49.8 4.9 %collective-permute-done.5.refs_2_ = bf16[3,4,4224]{2,1,0:T(4,128)(2,1)S(1)} collective-permute-done((bf16[3,4,4224]{2,1,0:T(4,128)(2,1)S(1)}, bf16[3,4,4224]{2,1,0:T(4,128)(2,1)S(1)}, u32[]{:S(2)}, u32[]{:S(2)}) %collective-permute-start.5) | collective-permute-done | bytes 101408 | tf_op jit(solution)/shard_map/ppermute | solution.py:35
  54.7 4.0 %collective-permute-done.6.refs_3_ = bf16[3,4,4224]{2,1,0:T(4,128)(2,1)S(1)} collective-permute-done((bf16[3,4,4224]{2,1,0:T(4,128)(2,1)S(1)}, bf16[3,4,4224]{2,1,0:T(4,128)(2,1)S(1)}, u32[]{:S(2)}, u32[]{:S(2)}) %collective-permute-start.6) | collective-permute-done | bytes 101408 | tf_op jit(solution)/shard_map/ppermute | solution.py:35
  58.7 2.6 %shard_map.127 = (bf16[3,4,4096]{2,1,0:T(4,128)(2,1)}, f32[16,128]{1,0:T(8,128)S(1)}) custom-call(f32[3,4,4096]{2,1,0:T(4,128)S(1)} %get-tuple-element.15.refs_0_, f32[3,4,128]{2,1,0:T(4,128)S(1)} %get-tuple-element.16.refs_1_, bf16[3,4,4224]{2,1,0:T(4,128)(2,1)S(1)} %collective-permute-done.5.refs_2_, ...), custom_call_target="tpu_custom_call" | custom-call | flops 1048576 | bytes 1048576 | tf_op jit(solution)/shard_map/pallas_call | solution.py:43
  61.4 1.2 %collective-permute-done.9.refs_1_ = f32[16,128]{1,0:T(8,128)S(1)} collective-permute-done((f32[16,128]{1,0:T(8,128)S(1)}, f32[16,128]{1,0:T(8,128)S(1)}, u32[]{:S(2)}, u32[]{:S(2)}) %collective-permute-start.9) | collective-permute-done | bytes 8224 | tf_op jit(solution)/shard_map/ppermute | solution.py:30
  62.6 0.9 %shard_map.128 = bf16[3,4,4096]{2,1,0:T(4,128)(2,1)} custom-call(f32[16,128]{1,0:T(8,128)S(1)} %get-tuple-element.21.refs_0_, f32[16,128]{1,0:T(8,128)S(1)} %collective-permute-done.9.refs_1_, bf16[1,64,4096]{2,1,0:T(8,128)(2,1)S(1)} %copy-done.3, bf16[1,64,4096]{2,1,0:T(8,128)(2,1)S(1)} %collective-permute-done.10.refs_3_), custom_call_target="tpu_custom_call" | custom-call | flops 1048576 | bytes 1048576 | tf_op jit(solution)/shard_map/pallas_call | solution.py:43
  (47 shorter events, 3.1 us)
Async XLA Ops:
  0.6 0.9 %copy-start.9 = (bf16[4,3,4096]{2,0,1:T(4,128)(2,1)S(1)}, bf16[4,3,4096]{2,0,1:T(4,128)(2,1)}, u32[]{:S(2)}) copy-start(bf16[4,3,4096]{2,0,1:T(4,128)(2,1)} %param.12) | copy-start | bytes 294916
  1.5 0.7 %copy-start.12 = (s32[4,1]{0,1:T(1,128)S(1)}, s32[4,1]{0,1:T(1,128)}, u32[]{:S(2)}) copy-start(s32[4,1]{0,1:T(1,128)} %param.16) | copy-start | bytes 52
  2.2 0.7 %copy-start.14 = (s32[4]{0:T(128)S(1)}, s32[4]{0:T(128)}, u32[]{:S(2)}) copy-start(s32[4]{0:T(128)} %refs_4_.1) | copy-start | bytes 52
  3.4 23.9 %copy-start.6 = (bf16[3,4,4224]{2,1,0:T(4,128)(2,1)}, bf16[3,4,4224]{2,1,0:T(4,128)(2,1)S(1)}, u32[]{:S(2)}) copy-start(bf16[3,4,4224]{2,1,0:T(4,128)(2,1)S(1)} %shard_map.122.refs_2_) | copy-start | bytes 304132
  3.4 21.3 %collective-permute-start.2 = (bf16[3,4,4224]{2,1,0:T(4,128)(2,1)S(1)}, bf16[3,4,4224]{2,1,0:T(4,128)(2,1)S(1)}, u32[]{:S(2)}, u32[]{:S(2)}) collective-permute-start(bf16[3,4,4224]{2,1,0:T(4,128)(2,1)S(1)} %shard_map.122.refs_2_), channel_id=1, source_target_pairs={{4,0},{0,4},{12,8},{8,12},{5,1},{1,5},{13,9},{9,13},{6,2},{2,6},{1... | collective-permute-start | bytes 304136 | tf_op jit(solution)/shard_map/ppermute | solution.py:30
  6.5 20.8 %collective-permute-start.1 = (bf16[3,4,4224]{2,1,0:T(4,128)(2,1)S(1)}, bf16[3,4,4224]{2,1,0:T(4,128)(2,1)S(1)}, u32[]{:S(2)}, u32[]{:S(2)}) collective-permute-start(bf16[3,4,4224]{2,1,0:T(4,128)(2,1)S(1)} %shard_map.122.refs_2_), channel_id=1, source_target_pairs={{8,0},{12,4},{0,8},{4,12},{9,1},{13,5},{1,9},{5,13},{10,2},{14,6},... | collective-permute-start | bytes 304136 | tf_op jit(solution)/shard_map/ppermute | solution.py:30
  9.1 18.8 %collective-permute-start = (bf16[3,4,4224]{2,1,0:T(4,128)(2,1)S(1)}, bf16[3,4,4224]{2,1,0:T(4,128)(2,1)S(1)}, u32[]{:S(2)}, u32[]{:S(2)}) collective-permute-start(bf16[3,4,4224]{2,1,0:T(4,128)(2,1)S(1)} %shard_map.122.refs_2_), channel_id=1, source_target_pairs={{12,0},{8,4},{4,8},{0,12},{13,1},{9,5},{5,9},{1,13},{14,2},{10,6},... | collective-permute-start | bytes 304136 | tf_op jit(solution)/shard_map/ppermute | solution.py:30
  9.1 5.8 %collective-permute-start.3 = (bf16[3,4,4096]{2,1,0:T(4,128)(2,1)}, bf16[3,4,4096]{2,1,0:T(4,128)(2,1)S(1)}, u32[]{:S(2)}, u32[]{:S(2)}) collective-permute-start(bf16[3,4,4096]{2,1,0:T(4,128)(2,1)} %bitcast.9), channel_id=1, source_target_pairs={{2,0},{0,2},{3,1},{1,3},{6,4},{4,6},{7,5},{5,7},{10,8},{8,10},{11,... | collective-permute-start | bytes 294920 | tf_op jit(solution)/shard_map/ppermute | solution.py:30
  10.8 27.2 %collective-permute-start.4 = (bf16[1,64,4096]{2,1,0:T(8,128)(2,1)}, bf16[1,64,4096]{2,1,0:T(8,128)(2,1)}, u32[]{:S(2)}, u32[]{:S(2)}) collective-permute-start(bf16[1,64,4096]{2,1,0:T(8,128)(2,1)} %refs_3_.1), channel_id=1, source_target_pairs={{2,0},{0,2},{3,1},{1,3},{6,4},{4,6},{7,5},{5,7},{10,8},{8,10},{11,... | collective-permute-start | bytes 1572872 | tf_op jit(solution)/shard_map/ppermute | solution.py:30
  14.9 34.5 %collective-permute-start.8 = (bf16[1,64,4096]{2,1,0:T(8,128)(2,1)}, bf16[1,64,4096]{2,1,0:T(8,128)(2,1)}, u32[]{:S(2)}, u32[]{:S(2)}) collective-permute-start(bf16[1,64,4096]{2,1,0:T(8,128)(2,1)} %refs_5_.3), channel_id=1, source_target_pairs={{2,0},{0,2},{3,1},{1,3},{6,4},{4,6},{7,5},{5,7},{10,8},{8,10},{11,... | collective-permute-start | bytes 1572872 | tf_op jit(solution)/shard_map/ppermute | solution.py:30
  16.7 1.0 %copy-start.1 = (bf16[1,64,4096]{2,1,0:T(8,128)(2,1)S(1)}, bf16[1,64,4096]{2,1,0:T(8,128)(2,1)}, u32[]{:S(2)}) copy-start(bf16[1,64,4096]{2,1,0:T(8,128)(2,1)} %refs_2_.3) | copy-start | bytes 1572868
  17.8 0.9 %copy-start.8 = (bf16[4,3,4096]{2,0,1:T(4,128)(2,1)S(1)}, bf16[4,3,4096]{2,0,1:T(4,128)(2,1)}, u32[]{:S(2)}) copy-start(bf16[4,3,4096]{2,0,1:T(4,128)(2,1)} %param.11) | copy-start | bytes 294916
  19.7 18.3 %all-to-all-start = ((bf16[16,16,128]{2,1,0:T(8,128)(2,1)}), bf16[16,16,128]{2,1,0:T(8,128)(2,1)S(1)}, u32[]{:S(2)}, u32[]{:S(2)}) async-start(bf16[16,16,128]{2,1,0:T(8,128)(2,1)} %bitcast.3), calls=%async_computation | async-start | bytes 131072 | tf_op jit(solution)/shard_map/all_to_all | solution.py:404
  24.7 13.3 %copy-start = (bf16[2,1024,512]{2,1,0:T(8,128)(2,1)S(1)}, bf16[2,1024,512]{2,1,0:T(8,128)(2,1)}, u32[]{:S(2)}) copy-start(bf16[2,1024,512]{2,1,0:T(8,128)(2,1)} %refs_1_.1) | copy-start | bytes 6291460
  24.7 0.6 %copy-start.16 = (bf16[3,4,4224]{2,1,0:T(4,128)(2,1)}, bf16[3,4,4224]{2,1,0:T(4,128)(2,1)S(1)}, u32[]{:S(2)}) copy-start(bf16[3,4,4224]{2,1,0:T(4,128)(2,1)S(1)} %collective-permute-done.2.refs_3_) | copy-start | bytes 304132
  25.3 36.0 %collective-permute-start.10 = (bf16[1,64,4096]{2,1,0:T(8,128)(2,1)}, bf16[1,64,4096]{2,1,0:T(8,128)(2,1)S(1)}, u32[]{:S(2)}, u32[]{:S(2)}) collective-permute-start(bf16[1,64,4096]{2,1,0:T(8,128)(2,1)} %refs_2_.5), channel_id=1, source_target_pairs={{2,0},{0,2},{3,1},{1,3},{6,4},{4,6},{7,5},{5,7},{10,8},{8,10},{11,... | collective-permute-start | bytes 1572872 | tf_op jit(solution)/shard_map/ppermute | solution.py:30
  28.5 0.9 %copy-start.7 = (bf16[3,4,4224]{2,1,0:T(4,128)(2,1)S(1)}, bf16[3,4,4224]{2,1,0:T(4,128)(2,1)}, u32[]{:S(2)}) copy-start(bf16[3,4,4224]{2,1,0:T(4,128)(2,1)} %copy-done.6) | copy-start | bytes 304132
  29.4 0.8 %copy-start.10 = (f32[40,256]{1,0:T(8,128)S(1)}, f32[40,256]{1,0:T(8,128)}, u32[]{:S(2)}) copy-start(f32[40,256]{1,0:T(8,128)} %pad_maximum_fusion.refs_4_) | copy-start | bytes 122884
  30.2 0.9 %copy-start.17 = (bf16[3,4,4224]{2,1,0:T(4,128)(2,1)S(1)}, bf16[3,4,4224]{2,1,0:T(4,128)(2,1)}, u32[]{:S(2)}) copy-start(bf16[3,4,4224]{2,1,0:T(4,128)(2,1)} %copy-done.16) | copy-start | bytes 304132
  31.1 0.9 %copy-start.19 = (bf16[3,4,4224]{2,1,0:T(4,128)(2,1)S(1)}, bf16[3,4,4224]{2,1,0:T(4,128)(2,1)}, u32[]{:S(2)}) copy-start(bf16[3,4,4224]{2,1,0:T(4,128)(2,1)} %copy-done.18) | copy-start | bytes 304132
  32.0 0.9 %copy-start.21 = (bf16[3,4,4224]{2,1,0:T(4,128)(2,1)S(1)}, bf16[3,4,4224]{2,1,0:T(4,128)(2,1)}, u32[]{:S(2)}) copy-start(bf16[3,4,4224]{2,1,0:T(4,128)(2,1)} %copy-done.20) | copy-start | bytes 304132
  33.3 9.3 %copy-start.15 = (s32[4]{0:T(128)S(1)}, s32[4]{0:T(128)}, u32[]{:S(2)}) copy-start(s32[4]{0:T(128)} %refs_4_.1) | copy-start | bytes 52
  38.0 1.0 %copy-start.4 = (bf16[1,64,4096]{2,1,0:T(8,128)(2,1)S(1)}, bf16[1,64,4096]{2,1,0:T(8,128)(2,1)}, u32[]{:S(2)}) copy-start(bf16[1,64,4096]{2,1,0:T(8,128)(2,1)} %refs_3_.1) | copy-start | bytes 1572868
  39.0 3.5 %copy-start.5 = (bf16[2,4,32,512]{3,2,1,0:T(8,128)(2,1)S(1)}, bf16[2,4,32,512]{3,2,1,0:T(8,128)(2,1)}, u32[]{:S(2)}) copy-start(bf16[2,4,32,512]{3,2,1,0:T(8,128)(2,1)} %refs_2_.4) | copy-start | bytes 786436
  39.0 3.6 %copy-start.11 = (bf16[2,4,3,512]{3,1,2,0:T(4,128)(2,1)S(1)}, bf16[2,4,3,512]{3,1,2,0:T(4,128)(2,1)}, u32[]{:S(2)}) copy-start(bf16[2,4,3,512]{3,1,2,0:T(4,128)(2,1)} %param.13) | copy-start | bytes 73732
  42.6 16.2 %copy-start.2 = (bf16[1,64,4096]{2,1,0:T(8,128)(2,1)S(1)}, bf16[1,64,4096]{2,1,0:T(8,128)(2,1)}, u32[]{:S(2)}) copy-start(bf16[1,64,4096]{2,1,0:T(8,128)(2,1)} %refs_5_.3) | copy-start | bytes 1572868
  42.6 16.2 %copy-start.13 = (s32[4,1]{0,1:T(1,128)S(1)}, s32[4,1]{0,1:T(1,128)}, u32[]{:S(2)}) copy-start(s32[4,1]{0,1:T(1,128)} %param.16) | copy-start | bytes 52
  42.6 20.0 %copy-start.3 = (bf16[1,64,4096]{2,1,0:T(8,128)(2,1)S(1)}, bf16[1,64,4096]{2,1,0:T(8,128)(2,1)}, u32[]{:S(2)}) copy-start(bf16[1,64,4096]{2,1,0:T(8,128)(2,1)} %refs_2_.5) | copy-start | bytes 1572868
  44.9 4.9 %collective-permute-start.7 = (bf16[3,4,4224]{2,1,0:T(4,128)(2,1)S(1)}, bf16[3,4,4224]{2,1,0:T(4,128)(2,1)S(1)}, u32[]{:S(2)}, u32[]{:S(2)}) collective-permute-start(bf16[3,4,4224]{2,1,0:T(4,128)(2,1)S(1)} %get-tuple-element.19), channel_id=1, source_target_pairs={{0,4},{4,0},{8,12},{12,8},{1,5},{5,1},{9,13},{13,9},{2,6},{6,2},{1... | collective-permute-start | bytes 304136 | tf_op jit(solution)/shard_map/ppermute | solution.py:35
  45.9 8.8 %collective-permute-start.5 = (bf16[3,4,4224]{2,1,0:T(4,128)(2,1)S(1)}, bf16[3,4,4224]{2,1,0:T(4,128)(2,1)S(1)}, u32[]{:S(2)}, u32[]{:S(2)}) collective-permute-start(bf16[3,4,4224]{2,1,0:T(4,128)(2,1)S(1)} %get-tuple-element.17), channel_id=1, source_target_pairs={{0,12},{4,8},{8,4},{12,0},{1,13},{5,9},{9,5},{13,1},{2,14},{6,10},... | collective-permute-start | bytes 304136 | tf_op jit(solution)/shard_map/ppermute | solution.py:35
  48.9 9.9 %collective-permute-start.6 = (bf16[3,4,4224]{2,1,0:T(4,128)(2,1)S(1)}, bf16[3,4,4224]{2,1,0:T(4,128)(2,1)S(1)}, u32[]{:S(2)}, u32[]{:S(2)}) collective-permute-start(bf16[3,4,4224]{2,1,0:T(4,128)(2,1)S(1)} %get-tuple-element.18), channel_id=1, source_target_pairs={{0,8},{4,12},{8,0},{12,4},{1,9},{5,13},{9,1},{13,5},{2,10},{6,14},... | collective-permute-start | bytes 304136 | tf_op jit(solution)/shard_map/ppermute | solution.py:35
  61.4 1.2 %collective-permute-start.9 = (f32[16,128]{1,0:T(8,128)S(1)}, f32[16,128]{1,0:T(8,128)S(1)}, u32[]{:S(2)}, u32[]{:S(2)}) collective-permute-start(f32[16,128]{1,0:T(8,128)S(1)} %get-tuple-element.21.refs_0_), channel_id=1, source_target_pairs={{1,0},{0,1},{3,2},{2,3},{5,4},{4,5},{7,6},{6,7},{9,8},{8,9},{11,10... | collective-permute-start | bytes 24584 | tf_op jit(solution)/shard_map/ppermute | solution.py:30
  (2 other events, 1.3 us)

commit v2 on v1

v2 whole, which is shorter than its diff:
```python
import functools
import math

import jax
import jax.numpy as jnp
from jax import lax
from jax.experimental import pallas as pl
from jax.experimental.pallas import tpu as pltpu
from jax.sharding import PartitionSpec as P

HEAD_SIZE = 128
LANES = 128
rope_base = 1000000.0
MASKED = -1e30
VMEM_BYTES = 8 << 20

VMEM = pl.BlockSpec(memory_space=pltpu.VMEM)
SMEM = pl.BlockSpec(memory_space=pltpu.SMEM)
F32 = jnp.float32
BF16 = jnp.bfloat16


def peer(index, offset, size):
    if size & (size - 1) == 0:
        return index ^ offset
    return (index + offset) % size


def fetch(value, axis, offset):
    size = lax.axis_size(axis)
    return lax.ppermute(value, axis, [(peer(i, offset, size), i) for i in range(size)])


def send(value, axis, offset):
    size = lax.axis_size(axis)
    return lax.ppermute(value, axis, [(i, peer(i, offset, size)) for i in range(size)])


def dot(left, right, contract):
    return lax.dot_general(left, right, (contract, ((), ())), preferred_element_type=F32)


def call(kernel, out_shape, args, specs=None, scratch=(), flops=1 << 20, out_specs=None):
    return pl.pallas_call(
        kernel,
        out_shape=out_shape,
        in_specs=specs or [VMEM] * len(args),
        out_specs=out_specs or jax.tree.map(lambda unused: VMEM, out_shape),
        scratch_shapes=scratch,
        compiler_params=pltpu.CompilerParams(vmem_limit_bytes=VMEM_BYTES),
        cost_estimate=pl.CostEstimate(flops=flops, bytes_accessed=1 << 20, transcendentals=0),
    )(*args)


def row_values(ref, rows, shape):
    row = lax.broadcasted_iota(jnp.int32, shape, 0) % rows
    out = jnp.zeros(shape, jnp.int32)
    for r in range(rows):
        out = jnp.where(row == r, ref[r], out)
    return out


def rank_kernel(count, *refs):
    parts = refs[:count]
    down_ref = refs[count]
    earlier = refs[count + 1 : -3]
    out_ref, kept_ref, gathered = refs[-3:]
    kept_ref[...] = down_ref[...]
    steps, rows, width = parts[0].shape
    resident, rank, _ = down_ref.shape
    pad_rows = gathered.shape[0] // count
    for j, ref in enumerate(parts):
        for t in range(steps):
            at = j * pad_rows + t * rows
            gathered[at : at + rows, :] = ref[t].astype(F32)
        at = j * pad_rows + steps * rows
        gathered[at : (j + 1) * pad_rows, :] = jnp.zeros((pad_rows - steps * rows, width), F32)
    result = dot(
        gathered[...].astype(BF16), down_ref[...].reshape(resident * rank, width), ((1,), (1,))
    )
    for ref in earlier:
        out_ref[: ref.shape[0], :] = ref[...]
    out_ref[out_ref.shape[0] - result.shape[0] :, :] = result


def correction_kernel(parts, *refs):
    ranks = functools.reduce(jnp.add, [ref[...] for ref in refs[:parts]]).astype(BF16)
    up_ref = refs[parts]
    out_refs = refs[parts + 1 :]
    resident, rank, _ = up_ref.shape
    _, steps, rows, _ = out_refs[0].shape
    pad_rows = ranks.shape[0] // len(out_refs)
    for u in range(resident):
        result = dot(ranks[:, u * rank : (u + 1) * rank], up_ref[u], ((1,), (0,)))
        for j, ref in enumerate(out_refs):
            for t in range(steps):
                at = j * pad_rows + t * rows
                ref[u, t] = result[at : at + rows]


def copy_kernel(in_ref, out_ref):
    out_ref[...] = in_ref[...]


def prepare_kernel(correction_ref, base_ref, suffix_ref, fresh_ref, length_ref, id_ref, *refs):
    sum_ref, id_rows_ref, suffix_out, fresh_out, bias_ref, token_ref = refs
    resident, steps, rows, width = correction_ref.shape
    x = lax.axis_index("adapter")
    ids = row_values(id_ref, rows, (rows, LANES))
    id_rows_ref[...] = ids
    for t in range(steps):
        for h in range(width // HEAD_SIZE):
            at = pl.ds(h * HEAD_SIZE, HEAD_SIZE)
            piece = base_ref[t, :, at].astype(F32)
            for u in range(resident):
                piece += jnp.where(ids == x * resident + u, correction_ref[u, t, :, at], 0.0)
            sum_ref[t, :, at] = piece
    suffix_out[...] = suffix_ref[...]
    fresh_out[...] = jnp.zeros_like(fresh_out)
    for part in range(2):
        for t in range(steps):
            fresh_out[part, t * rows : (t + 1) * rows, :] = fresh_ref[part, t].astype(F32)
    slots = suffix_ref.shape[2]
    suffix_count = rows * slots
    shape = bias_ref.shape
    token = lax.broadcasted_iota(jnp.int32, shape, 0)
    column = lax.broadcasted_iota(jnp.int32, shape, 1)
    token_row, token_step = token % rows, token // rows
    fresh_at = column - suffix_count
    in_suffix = (column < suffix_count) & (column // slots == token_row)
    in_suffix &= column % slots < row_values(length_ref, rows, shape)
    in_fresh = (column >= suffix_count) & (fresh_at % rows == token_row)
    in_fresh &= fresh_at // rows <= token_step
    bias_ref[...] = jnp.where(in_suffix | in_fresh, 0.0, MASKED)
    token_ref[...] = jnp.zeros_like(token_ref)


def rotate_kernel(others, *refs):
    corrections = refs[:others]
    sum_ref, cos_ref, sin_ref, id_ref, _, out_ref = refs[others:]
    steps, rows, width = sum_ref.shape
    x = lax.axis_index("adapter")
    ids = id_ref[...]
    for t in range(steps):
        cos_part, sin_part = cos_ref[t], sin_ref[t]
        for h in range(width // HEAD_SIZE):
            at = pl.ds(h * HEAD_SIZE, HEAD_SIZE)
            piece = sum_ref[t, :, at]
            for j, ref in enumerate(corrections):
                resident = ref.shape[0]
                for u in range(resident):
                    owner = peer(x, j + 1, others + 1) * resident + u
                    piece += jnp.where(ids == owner, ref[u, t, :, at], 0.0)
            turned = piece * cos_part + pltpu.roll(piece, HEAD_SIZE // 2, 1) * sin_part
            out_ref[t, :, at] = turned.astype(BF16)


def load_queries(query_ref, rows_ref):
    steps, rows, _ = query_ref.shape
    rows_ref[...] = jnp.zeros_like(rows_ref)
    for t in range(steps):
        rows_ref[t * rows : (t + 1) * rows, :] = query_ref[t].astype(F32)


def group_queries(rows_ref, first, group):
    pieces = [
        rows_ref[:, first + g * HEAD_SIZE : first + (g + 1) * HEAD_SIZE] for g in range(group)
    ]
    return jnp.concatenate(pieces, axis=0).astype(BF16)


def attend(query, key, value, scale, extra=None):
    scores = dot(query, key, ((1,), (1,)))
    if extra is not None:
        more_key, more_value, bias = extra
        scores = jnp.concatenate([scores, dot(query, more_key, ((1,), (1,))) + bias], axis=1)
        value = jnp.concatenate([value, more_value], axis=0)
    peaks = jnp.max(scores, axis=1, keepdims=True)
    weight = jnp.exp2((scores - peaks) * scale).astype(BF16)
    ones = jnp.ones((value.shape[0], LANES), BF16)
    summed = dot(weight, jnp.concatenate([value, ones], axis=1), ((1,), (0,)))
    total = summed[:, HEAD_SIZE:]
    return summed[:, :HEAD_SIZE] / total, peaks * scale + jnp.log2(total)


def split_stat(stat, heads):
    first = stat.astype(BF16).astype(F32)
    second = (stat - first).astype(BF16).astype(F32)
    third = stat - first - second
    lane = lax.broadcasted_iota(jnp.int32, stat.shape, 1)
    out = jnp.where(lane < heads, first, 0.0)
    out = jnp.where((lane >= heads) & (lane < 2 * heads), pltpu.roll(second, heads, 1), out)
    out = jnp.where(
        (lane >= 2 * heads) & (lane < 3 * heads), pltpu.roll(third, 2 * heads, 1), out
    )
    return out


def far_kernel(scale, query_ref, kv_ref, *refs):
    out_ref, rows_ref, kept, stats = refs[-4:]
    steps, rows, width = query_ref.shape
    heads = width // HEAD_SIZE
    kv_heads = kv_ref.shape[2] // HEAD_SIZE
    group = heads // kv_heads
    cut = rows_ref.shape[0]
    load_queries(query_ref, rows_ref)
    lane = lax.broadcasted_iota(jnp.int32, (cut, LANES), 1)
    for kv in range(kv_heads):
        at = pl.ds(kv * HEAD_SIZE, HEAD_SIZE)
        queries = group_queries(rows_ref, kv * group * HEAD_SIZE, group)
        result, level = attend(queries, kv_ref[0, :, at], kv_ref[1, :, at], scale)
        for g in range(group):
            head = kv * group + g
            kept[:, head * HEAD_SIZE : (head + 1) * HEAD_SIZE] = result[g * cut : (g + 1) * cut]
            piece = level[g * cut : (g + 1) * cut]
            stats[...] = jnp.where(lane == head, piece, stats[...] if head else 0.0)
    packed = split_stat(stats[...], heads)
    for t in range(steps):
        at = t * rows
        out_ref[t, :, :width] = kept[at : at + rows, :].astype(BF16)
        out_ref[t, :, width:] = packed[at : at + rows, :].astype(BF16)


def near_kernel(scale, query_ref, kv_ref, suffix_ref, fresh_ref, bias_ref, *refs):
    own_ref, level_ref, token_ref, rows_ref, kept, stats = refs
    load_queries(query_ref, rows_ref)
    token_ref[...] = jnp.zeros_like(token_ref)
    steps, rows, width = query_ref.shape
    heads = width // HEAD_SIZE
    kv_heads = kv_ref.shape[2] // HEAD_SIZE
    group = heads // kv_heads
    cut = rows_ref.shape[0]
    bias = jnp.concatenate([bias_ref[...]] * group, axis=0)
    lane = lax.broadcasted_iota(jnp.int32, (cut, LANES), 1)
    for kv in range(kv_heads):
        at = pl.ds(kv * HEAD_SIZE, HEAD_SIZE)
        more = [
            jnp.concatenate(
                [suffix_ref[part, r, :, at] for r in range(rows)]
                + [fresh_ref[part, :, at].astype(BF16)],
                axis=0,
            )
            for part in range(2)
        ]
        result, level = attend(
            group_queries(rows_ref, kv * group * HEAD_SIZE, group),
            kv_ref[0, :, at],
            kv_ref[1, :, at],
            scale,
            (more[0], more[1], bias),
        )
        for g in range(group):
            head = kv * group + g
            kept[:, head * HEAD_SIZE : (head + 1) * HEAD_SIZE] = result[g * cut : (g + 1) * cut]
            piece = level[g * cut : (g + 1) * cut]
            stats[...] = jnp.where(lane == head, piece, stats[...] if head else 0.0)
    for t in range(steps):
        own_ref[t] = kept[t * rows : (t + 1) * rows, :]
        level_ref[t] = stats[t * rows : (t + 1) * rows, :]


def merge_kernel(messages, adapters, *refs):
    arrived = refs[:messages]
    own_ref, level_ref = refs[messages : messages + 2]
    downs = refs[2 + messages : 2 + messages + adapters]
    id_ref, out_hbm, rank_ref, rows_ref, out_ref, sem = refs[2 + messages + adapters :]
    steps, rows, width = own_ref.shape
    heads = width // HEAD_SIZE
    resident, rank, _ = downs[0].shape
    depth = resident * rank
    x = lax.axis_index("adapter")
    rows_ref[...] = jnp.zeros_like(rows_ref)
    for t in range(steps):
        levels = [level_ref[t]]
        for ref in arrived:
            packed = ref[t, :, width:].astype(F32)
            count = packed.shape[1]
            levels.append(
                packed
                + pltpu.roll(packed, count - heads, 1)
                + pltpu.roll(packed, count - 2 * heads, 1)
            )
        highest = functools.reduce(jnp.maximum, levels)
        shares = [jnp.exp2(level - highest) for level in levels]
        total = functools.reduce(jnp.add, shares)
        shares = [share / total for share in shares]
        for h in range(heads):
            at = pl.ds(h * HEAD_SIZE, HEAD_SIZE)
            mixed = own_ref[t, :, at] * shares[0][:, h : h + 1]
            for ref, share in zip(arrived, shares[1:]):
                mixed += ref[t, :, at].astype(F32) * share[:, h : h + 1]
            out_ref[t, :, at] = mixed.astype(BF16)
            rows_ref[t * rows : (t + 1) * rows, at] = mixed
    copy = pltpu.make_async_copy(out_ref, out_hbm, sem)
    copy.start()
    factors = jnp.concatenate([down[u] for down in downs for u in range(resident)], axis=0)
    result = dot(rows_ref[...].astype(BF16), factors, ((1,), (1,)))
    ids = row_values(id_ref, rows, result.shape)
    lane = lax.broadcasted_iota(jnp.int32, result.shape, 1)
    owner = peer(x, lane // depth, adapters) * resident + lane % depth // rank
    rank_ref[...] = jnp.where(owner == ids, result, 0.0)
    copy.wait()


def up_kernel(parts, adapters, *refs):
    ranks = refs[:parts]
    ups = refs[parts : parts + adapters]
    out_ref = refs[parts + adapters]
    steps, rows, width = out_ref.shape
    resident = ups[0].shape[0]
    chosen = functools.reduce(jnp.add, [ref[...] for ref in ranks]).astype(BF16)
    factors = jnp.concatenate([up[u] for up in ups for u in range(resident)], axis=0)
    result = dot(chosen, factors, ((1,), (0,)))
    for t in range(steps):
        out_ref[t] = result[t * rows : (t + 1) * rows].astype(BF16)


def rope_parts(suffix_length, steps, first_position):
    half_dim = HEAD_SIZE // 2
    frequency = rope_base ** (-2.0 * jnp.arange(half_dim, dtype=F32) / HEAD_SIZE)
    position = first_position + suffix_length[None, :] + jnp.arange(steps, dtype=jnp.int32)[:, None]
    angles = position.astype(F32)[..., None] * frequency
    cos_part, sin_part = jnp.cos(angles), jnp.sin(angles)
    return (
        jnp.concatenate([cos_part, cos_part], axis=-1),
        jnp.concatenate([-sin_part, sin_part], axis=-1),
    )


def on_device(
    hidden,
    base_query_rows,
    fresh_key_value,
    suffix_key_value,
    suffix_length,
    row_adapter_index,
    prompt_key_value,
    query_down_factors,
    query_up_factors,
    output_down_factors,
    output_up_factors,
):
    rows, steps, width = hidden.shape
    seq_count, adapters, halves = (lax.axis_size(name) for name in ("seq", "adapter", "head"))
    slots = suffix_key_value.shape[2]
    resident, rank, _ = query_down_factors.shape
    depth = resident * rank
    tokens = rows * steps
    pad_rows = -(-tokens // 16) * 16
    heads = width // HEAD_SIZE
    kv_heads = prompt_key_value.shape[2] // HEAD_SIZE
    group = heads // kv_heads
    scale = math.log2(math.e) / math.sqrt(HEAD_SIZE)
    stat_lanes = -(-3 * heads // LANES) * LANES
    ids = row_adapter_index.reshape(-1)
    hidden = hidden.transpose(1, 0, 2)
    base = base_query_rows.transpose(1, 0, 2)
    fresh = fresh_key_value.transpose(0, 2, 1, 3)

    own_rows = jax.ShapeDtypeStruct((pad_rows, depth), F32)
    factors = jax.ShapeDtypeStruct(query_down_factors.shape, BF16)
    own_ranks, own_down = call(
        functools.partial(rank_kernel, 1),
        (own_rows, factors),
        (hidden, query_down_factors),
        scratch=[pltpu.VMEM((pad_rows, width), F32)],
    )
    hidden_of = [fetch(hidden, "adapter", j) for j in range(1, adapters)]
    ranks, _ = call(
        functools.partial(rank_kernel, adapters - 1),
        (jax.ShapeDtypeStruct((adapters * pad_rows, depth), F32), factors),
        (*hidden_of, own_down, own_ranks),
        scratch=[pltpu.VMEM(((adapters - 1) * pad_rows, width), F32)],
    )
    rank_parts = [ranks] + [fetch(ranks, "head", j) for j in range(1, halves)]
    own_up = call(
        copy_kernel, jax.ShapeDtypeStruct(query_up_factors.shape, BF16), (query_up_factors,)
    )
    corrections = call(
        functools.partial(correction_kernel, halves),
        (jax.ShapeDtypeStruct((resident, steps, rows, width), F32),) * adapters,
        (*rank_parts, own_up),
    )
    arrived = [send(part, "adapter", j) for j, part in enumerate(corrections) if j]
    cos_part, sin_part = rope_parts(suffix_length, steps, prompt_key_value.shape[1] * seq_count)
    fresh_slots = -(-tokens // LANES) * LANES
    token_shape = jax.ShapeDtypeStruct((8, LANES), F32)
    query_sum, id_rows, suffix, fresh, bias, token = call(
        prepare_kernel,
        (
            jax.ShapeDtypeStruct((steps, rows, width), F32),
            jax.ShapeDtypeStruct((rows, LANES), jnp.int32),
            jax.ShapeDtypeStruct(suffix_key_value.shape, BF16),
            jax.ShapeDtypeStruct((2, fresh_slots, fresh.shape[3]), F32),
            jax.ShapeDtypeStruct((pad_rows, rows * slots + fresh_slots), F32),
            token_shape,
        ),
        (corrections[0], base, suffix_key_value, fresh, suffix_length, ids),
        [VMEM] * 4 + [SMEM] * 2,
    )
    output_down_factors, output_up_factors, token = lax.optimization_barrier(
        (output_down_factors, output_up_factors, token)
    )
    queries = call(
        functools.partial(rotate_kernel, adapters - 1),
        jax.ShapeDtypeStruct((steps, rows, width), BF16),
        (*arrived, query_sum, cos_part, sin_part, id_rows, token),
    )
    order = list(range(seq_count - 1, 0, -1))
    message = jax.ShapeDtypeStruct((steps, rows, width + stat_lanes), BF16)
    query_scratch = [
        pltpu.VMEM((pad_rows, width), F32),
        pltpu.VMEM((pad_rows, width), F32),
        pltpu.VMEM((pad_rows, LANES), F32),
    ]
    pieces = [fetch(queries, "seq", k) for k in order]
    own, level, token = call(
        functools.partial(near_kernel, scale),
        (
            jax.ShapeDtypeStruct((steps, rows, width), F32),
            jax.ShapeDtypeStruct((steps, rows, LANES), F32),
            token_shape,
        ),
        (queries, prompt_key_value, suffix, fresh, bias),
        scratch=query_scratch,
    )
    messages = [
        call(
            functools.partial(far_kernel, scale),
            message,
            (piece, prompt_key_value) + ((token,) if i == 0 else ()),
            scratch=query_scratch,
        )
        for i, piece in enumerate(pieces)
    ]
    output_downs = [output_down_factors] + [
        fetch(output_down_factors, "adapter", j) for j in range(1, adapters)
    ]
    output_ups = [output_up_factors] + [
        fetch(output_up_factors, "adapter", j) for j in range(1, adapters)
    ]
    partials = [send(part, "seq", k) for part, k in zip(messages, order)]
    attended, out_rank = call(
        functools.partial(merge_kernel, seq_count - 1, adapters),
        (
            jax.ShapeDtypeStruct((steps, rows, width), BF16),
            jax.ShapeDtypeStruct((pad_rows, adapters * depth), F32),
        ),
        (*partials, own, level, *output_downs, ids),
        [VMEM] * (2 + len(partials) + adapters) + [SMEM],
        scratch=[
            pltpu.VMEM((pad_rows, width), F32),
            pltpu.VMEM((steps, rows, width), BF16),
            pltpu.SemaphoreType.DMA,
        ],
        out_specs=(pl.BlockSpec(memory_space=pl.ANY), VMEM),
    )
    out_ranks = [out_rank] + [fetch(out_rank, "head", j) for j in range(1, halves)]
    adapted = call(
        functools.partial(up_kernel, halves, adapters),
        jax.ShapeDtypeStruct((steps, rows, width), BF16),
        (*out_ranks, *output_ups),
    )
    return attended.transpose(1, 0, 2), adapted.transpose(1, 0, 2)


def solution(mesh):
    rows = ("groups", "seq", "adapter")
    factors = P(("groups", "adapter"), None, "head")
    placed = (
        P(rows, None, "head"),
        P(rows, None, "head"),
        P(None, rows, None, "head"),
        P(None, rows, None, "head"),
        P(rows),
        P(rows, None),
        P(None, ("groups", "seq"), "head"),
        factors,
        factors,
        factors,
        factors,
    )
    return jax.shard_map(
        on_device,
        mesh=mesh,
        in_specs=placed,
        out_specs=(P(rows, None, "head"), P(rows, None, "head")),
        check_vma=False,
    )
```

time: 64.1 us -> 45.3 us (0.71)
  waiting for transfers between devices: 18.1 us -> 7.71 us
  local copies, waits for them, and re-layouts: 11.5 us -> 6.88 us
  starting transfers between devices: 20.9 us -> 18.4 us
  Pallas kernels: 11.3 us -> 10.3 us
    ppermute x3 -> x4, waiting for transfers between devices: 9.37 us -> 3.29 us  [send(): lax.ppermute(value, axis, [(i, peer(i, offset, size)) for i in range(size)])]
    all_to_all x1 -> x0, starting transfers between devices: 4.99 us -> none  [on_device(): lax.all_to_all(rank_parts.reshape(spread), ('seq', 'adapter', 'head'), sp...]
    all_to_all x1 -> x0, waiting for transfers between devices: 4.69 us -> none  [on_device(): lax.all_to_all(rank_parts.reshape(spread), ('seq', 'adapter', 'head'), sp...]
    unnamed x44 -> x24, local copies, waits for them, and re-layouts: 11.5 us -> 6.88 us
    ppermute x3 -> x4, starting transfers between devices: 4.44 us -> 8.8 us  [send(): lax.ppermute(value, axis, [(i, peer(i, offset, size)) for i in range(size)])]
    ppermute x8, starting transfers between devices: 11.5 us -> 9.62 us  [fetch(): lax.ppermute(value, axis, [(peer(i, offset, size), i) for i in range(size)])]
    pallas_call x7 -> x12, Pallas kernels: 11.3 us -> 10.3 us  [call(): pl.pallas_call(kernel, out_shape=out_shape, in_specs=specs or [VMEM] * le...]
    add x0 -> x1, other arithmetic: none -> 0.66 us  [rope_parts(): first_position + suffix_length[None, :]]
  transfers between devices with their start and end apart: 12 -> 12, of which waited for: 6 -> 7; matrix products, arithmetic and copies ran while one was open for 1% -> 2% of each run, Pallas kernels for 16% -> 18%
where the time goes in v2:
time: 45.3 us; the launch traced here: 44.9 us
  starting transfers between devices  18.4 us (41%)
  Pallas kernels  10.3 us (23%)
  waiting for transfers between devices  7.71 us (17%)
  local copies, waits for them, and re-layouts  6.88 us (15%)
  other arithmetic  0.88 us (2%)
  between operations  0.74 us (2%)
    pallas_call x12, Pallas kernels, call(): pl.pallas_call(kernel, out_shape=out_shape, in_specs=specs or [VMEM] * le...  10.3 us
    ppermute x8, starting transfers between devices, fetch(): lax.ppermute(value, axis, [(peer(i, offset, size), i) for i in range(size)])  9.62 us
    ppermute x4, starting transfers between devices, send(): lax.ppermute(value, axis, [(i, peer(i, offset, size)) for i in range(size)])  8.8 us
    unnamed x24, local copies, waits for them, and re-layouts  6.88 us
    ppermute x8, waiting for transfers between devices, fetch(): lax.ppermute(value, axis, [(peer(i, offset, size), i) for i in range(size)])  4.42 us
    ppermute x4, waiting for transfers between devices, send(): lax.ppermute(value, axis, [(i, peer(i, offset, size)) for i in range(size)])  3.29 us
  transfers between devices with their start and end apart: 12, of which 7 were waited for; matrix products, arithmetic and copies ran while one was open for 2% of the time, Pallas kernels for 18%

profile of v2, /device:TPU:0, one launch (start us, length us, event | category | flops | bytes accessed | tf_op | source)
XLA Modules:
  0.0 44.9 jit_solution(11410456193858888629)
XLA Ops:
  0.6 3.0 %collective-permute-start = (bf16[3,4,4096]{2,1,0:T(4,128)(2,1)}, bf16[3,4,4096]{2,1,0:T(4,128)(2,1)S(1)}, u32[]{:S(2)}, u32[]{:S(2)}) collective-permute-start(bf16[3,4,4096]{2,1,0:T(4,128)(2,1)} %bitcast.6), channel_id=1, source_target_pairs={{2,0},{0,2},{3,1},{1,3},{6,4},{4,6},{7,5},{5,7},{10,8},{8,10},{11,... | collective-permute-start | bytes 294920 | tf_op jit(solution)/shard_map/ppermute | solution.py:31
  3.6 0.7 %broadcast_add_fusion = s32[4]{0:T(128)S(1)} fusion(s32[4]{0:T(128)} %length_ref.1), kind=kLoop, calls=%fused_computation.6 | loop fusion | flops 4 | bytes 32 | tf_op jit(solution)/shard_map/add | solution.py:321
  4.3 1.0 %copy-done.1 = bf16[1,64,4096]{2,1,0:T(8,128)(2,1)S(1)} copy-done((bf16[1,64,4096]{2,1,0:T(8,128)(2,1)S(1)}, bf16[1,64,4096]{2,1,0:T(8,128)(2,1)}, u32[]{:S(2)}) %copy-start.1) | copy-done | bytes 524312
  5.4 0.9 %copy-done.6 = bf16[4,3,4096]{2,0,1:T(4,128)(2,1)S(1)} copy-done((bf16[4,3,4096]{2,0,1:T(4,128)(2,1)S(1)}, bf16[4,3,4096]{2,0,1:T(4,128)(2,1)}, u32[]{:S(2)}) %copy-start.6) | copy-done | bytes 98328
  6.2 0.3 shard_map.122
  6.7 1.0 %shard_map.123 = (f32[32,64]{1,0:T(8,128)S(1)}, bf16[1,64,4096]{2,1,0:T(8,128)(2,1)}) custom-call(bf16[3,4,4096]{2,1,0:T(4,128)(2,1)S(1)} %collective-permute-done.refs_0_, bf16[1,64,4096]{2,1,0:T(8,128)(2,1)S(1)} %get-tuple-element.21.refs_1_, f32[16,64]{1,0:T(8,128)S(1)} %get-tuple-element.22.refs_2_), custom_call_target="tpu_custom_call" | custom-call | flops 1048576 | bytes 1048576 | tf_op jit(solution)/shard_map/pallas_call | solution.py:44
  7.6 1.0 %copy-done.2 = bf16[1,64,4096]{2,1,0:T(8,128)(2,1)S(1)} copy-done((bf16[1,64,4096]{2,1,0:T(8,128)(2,1)S(1)}, bf16[1,64,4096]{2,1,0:T(8,128)(2,1)}, u32[]{:S(2)}) %copy-start.2) | copy-done | bytes 524312
  8.8 0.2 shard_map.125
  9.0 1.9 %collective-permute-start.2 = (f32[1,3,4,4096]{3,2,1,0:T(4,128)S(1)}, f32[1,3,4,4096]{3,2,1,0:T(4,128)S(1)}, u32[]{:S(2)}, u32[]{:S(2)}) collective-permute-start(f32[1,3,4,4096]{3,2,1,0:T(4,128)S(1)} %get-tuple-element.24), channel_id=1, source_target_pairs={{0,2},{2,0},{1,3},{3,1},{4,6},{6,4},{5,7},{7,5},{8,10},{10,8},{9,1... | collective-permute-start | bytes 589832 | tf_op jit(solution)/shard_map/ppermute | solution.py:36
  10.9 0.9 %copy-done.5 = bf16[2,4,32,512]{3,2,1,0:T(8,128)(2,1)S(1)} copy-done((bf16[2,4,32,512]{3,2,1,0:T(8,128)(2,1)S(1)}, bf16[2,4,32,512]{3,2,1,0:T(8,128)(2,1)}, u32[]{:S(2)}) %copy-start.5) | copy-done | bytes 262168
  11.9 0.9 %copy-done.7 = bf16[4,3,4096]{2,0,1:T(4,128)(2,1)S(1)} copy-done((bf16[4,3,4096]{2,0,1:T(4,128)(2,1)S(1)}, bf16[4,3,4096]{2,0,1:T(4,128)(2,1)}, u32[]{:S(2)}) %copy-start.7) | copy-done | bytes 98328
  12.8 0.7 %copy-done.8 = bf16[2,4,3,512]{3,1,2,0:T(4,128)(2,1)S(1)} copy-done((bf16[2,4,3,512]{3,1,2,0:T(4,128)(2,1)S(1)}, bf16[2,4,3,512]{3,1,2,0:T(4,128)(2,1)}, u32[]{:S(2)}) %copy-start.8) | copy-done | bytes 24600
  13.5 0.7 %copy-done.9 = s32[4,1]{0,1:T(1,128)S(1)} copy-done((s32[4,1]{0,1:T(1,128)S(1)}, s32[4,1]{0,1:T(1,128)}, u32[]{:S(2)}) %copy-start.9) | copy-done | bytes 40
  14.1 0.7 %copy-done.11 = s32[4]{0:T(128)S(1)} copy-done((s32[4]{0:T(128)S(1)}, s32[4]{0:T(128)}, u32[]{:S(2)}) %copy-start.11) | copy-done | bytes 40
  14.8 0.7 %shard_map.126 = (f32[3,4,4096]{2,1,0:T(4,128)S(1)}, s32[4,128]{1,0:T(4,128)S(1)}, bf16[2,4,32,512]{3,2,1,0:T(8,128)(2,1)S(1)}, f32[2,128,512]{2,1,0:T(8,128)S(1...) custom-call(f32[1,3,4,4096]{3,2,1,0:T(4,128)S(1)} %get-tuple-element.25.correction_ref, bf16[3,4,4096]{2,1,0:T(4,128)(2,1)S(1)} %bitcast.8, ...), custom_call_target="tpu_custom_call" | custom-call | flops 1048576 | bytes 1048576 | tf_op jit(solution)/shard_map/pallas_call | solution.py:44
  15.5 0.3 collective-permute-start.9
  15.7 1.8 %collective-permute-start.11 = (bf16[1,64,4096]{2,1,0:T(8,128)(2,1)S(1)}, bf16[1,64,4096]{2,1,0:T(8,128)(2,1)S(1)}, u32[]{:S(2)}, u32[]{:S(2)}) collective-permute-start(bf16[1,64,4096]{2,1,0:T(8,128)(2,1)S(1)} %copy-done.4), channel_id=1, source_target_pairs={{2,0},{0,2},{3,1},{1,3},{6,4},{4,6},{7,5},{5,7},{10,8},{8,10},{11,... | collective-permute-start | bytes 1572872 | tf_op jit(solution)/shard_map/ppermute | solution.py:31
  18.0 3.7 %collective-permute-start.3 = (bf16[3,4,4096]{2,1,0:T(4,128)(2,1)S(1)}, bf16[3,4,4096]{2,1,0:T(4,128)(2,1)S(1)}, u32[]{:S(2)}, u32[]{:S(2)}) collective-permute-start(bf16[3,4,4096]{2,1,0:T(4,128)(2,1)S(1)} %shard_map.127.query_ref), channel_id=1, source_target_pairs={{12,0},{8,4},{4,8},{0,12},{13,1},{9,5},{5,9},{1,13},{14,2},{10,6},... | collective-permute-start | bytes 294920 | tf_op jit(solution)/shard_map/ppermute | solution.py:31
  21.6 0.8 %collective-permute-start.7 = (bf16[3,4,4096]{2,1,0:T(4,128)(2,1)S(1)}, bf16[3,4,4096]{2,1,0:T(4,128)(2,1)S(1)}, u32[]{:S(2)}, u32[]{:S(2)}) collective-permute-start(bf16[3,4,4096]{2,1,0:T(4,128)(2,1)S(1)} %shard_map.127.query_ref), channel_id=1, source_target_pairs={{4,0},{0,4},{12,8},{8,12},{5,1},{1,5},{13,9},{9,13},{6,2},{2,6},{1... | collective-permute-start | bytes 294920 | tf_op jit(solution)/shard_map/ppermute | solution.py:31
  22.4 1.3 %shard_map.128 = (f32[3,4,4096]{2,1,0:T(4,128)S(1)}, f32[3,4,128]{2,1,0:T(4,128)S(1)}, f32[8,128]{1,0:T(8,128)S(1)}) custom-call(bf16[3,4,4096]{2,1,0:T(4,128)(2,1)S(1)} %shard_map.127.query_ref, bf16[2,1024,512]{2,1,0:T(8,128)(2,1)S(1)} %copy-done, bf16[2,4,32,512]{3,2,1,0:T(8,128)(2,1)S(1)} %get-tuple-element.30.suffix_ref, ...), custom_call_target="tpu_custom_call" | custom-call | flops 1048576 | bytes 1048576 | tf_op jit(solution)/shard_map/pallas_call | solution.py:44
  23.8 1.7 %collective-permute-done.3.query_ref = bf16[3,4,4096]{2,1,0:T(4,128)(2,1)S(1)} collective-permute-done((bf16[3,4,4096]{2,1,0:T(4,128)(2,1)S(1)}, bf16[3,4,4096]{2,1,0:T(4,128)(2,1)S(1)}, u32[]{:S(2)}, u32[]{:S(2)}) %collective-permute-start.3) | collective-permute-done | bytes 98336 | tf_op jit(solution)/shard_map/ppermute | solution.py:31
  25.5 1.2 %shard_map.129 = bf16[3,4,4224]{2,1,0:T(4,128)(2,1)S(1)} custom-call(bf16[3,4,4096]{2,1,0:T(4,128)(2,1)S(1)} %collective-permute-done.3.query_ref, bf16[2,1024,512]{2,1,0:T(8,128)(2,1)S(1)} %copy-done, f32[8,128]{1,0:T(8,128)S(1)} %get-tuple-element.33.refs_0_), custom_call_target="tpu_custom_call" | custom-call | flops 1048576 | bytes 1048576 | tf_op jit(solution)/shard_map/pallas_call | solution.py:44
  26.7 3.7 %collective-permute-start.4 = (bf16[3,4,4224]{2,1,0:T(4,128)(2,1)S(1)}, bf16[3,4,4224]{2,1,0:T(4,128)(2,1)S(1)}, u32[]{:S(2)}, u32[]{:S(2)}) collective-permute-start(bf16[3,4,4224]{2,1,0:T(4,128)(2,1)S(1)} %shard_map.129), channel_id=1, source_target_pairs={{0,12},{4,8},{8,4},{12,0},{1,13},{5,9},{9,5},{13,1},{2,14},{6,10},... | collective-permute-start | bytes 304136 | tf_op jit(solution)/shard_map/ppermute | solution.py:36
  30.4 1.3 %collective-permute-done.5.query_ref = bf16[3,4,4096]{2,1,0:T(4,128)(2,1)S(1)} collective-permute-done((bf16[3,4,4096]{2,1,0:T(4,128)(2,1)S(1)}, bf16[3,4,4096]{2,1,0:T(4,128)(2,1)S(1)}, u32[]{:S(2)}, u32[]{:S(2)}) %collective-permute-start.5) | collective-permute-done | bytes 98336 | tf_op jit(solution)/shard_map/ppermute | solution.py:31
  31.7 1.2 %shard_map.130 = bf16[3,4,4224]{2,1,0:T(4,128)(2,1)S(1)} custom-call(bf16[3,4,4096]{2,1,0:T(4,128)(2,1)S(1)} %collective-permute-done.5.query_ref, bf16[2,1024,512]{2,1,0:T(8,128)(2,1)S(1)} %copy-done), custom_call_target="tpu_custom_call" | custom-call | flops 1048576 | bytes 1048576 | tf_op jit(solution)/shard_map/pallas_call | solution.py:44
  33.0 1.2 %shard_map.131 = bf16[3,4,4224]{2,1,0:T(4,128)(2,1)S(1)} custom-call(bf16[3,4,4096]{2,1,0:T(4,128)(2,1)S(1)} %collective-permute-done.7.query_ref, bf16[2,1024,512]{2,1,0:T(8,128)(2,1)S(1)} %copy-done), custom_call_target="tpu_custom_call" | custom-call | flops 1048576 | bytes 1048576 | tf_op jit(solution)/shard_map/pallas_call | solution.py:44
  34.2 3.2 %collective-permute-start.8 = (bf16[3,4,4224]{2,1,0:T(4,128)(2,1)S(1)}, bf16[3,4,4224]{2,1,0:T(4,128)(2,1)S(1)}, u32[]{:S(2)}, u32[]{:S(2)}) collective-permute-start(bf16[3,4,4224]{2,1,0:T(4,128)(2,1)S(1)} %shard_map.131), channel_id=1, source_target_pairs={{0,4},{4,0},{8,12},{12,8},{1,5},{5,1},{9,13},{13,9},{2,6},{6,2},{1... | collective-permute-start | bytes 304136 | tf_op jit(solution)/shard_map/ppermute | solution.py:36
  37.3 2.3 %collective-permute-done.6.refs_1_ = bf16[3,4,4224]{2,1,0:T(4,128)(2,1)S(1)} collective-permute-done((bf16[3,4,4224]{2,1,0:T(4,128)(2,1)S(1)}, bf16[3,4,4224]{2,1,0:T(4,128)(2,1)S(1)}, u32[]{:S(2)}, u32[]{:S(2)}) %collective-permute-start.6) | collective-permute-done | bytes 101408 | tf_op jit(solution)/shard_map/ppermute | solution.py:36
  39.6 1.0 %collective-permute-done.8.refs_2_ = bf16[3,4,4224]{2,1,0:T(4,128)(2,1)S(1)} collective-permute-done((bf16[3,4,4224]{2,1,0:T(4,128)(2,1)S(1)}, bf16[3,4,4224]{2,1,0:T(4,128)(2,1)S(1)}, u32[]{:S(2)}, u32[]{:S(2)}) %collective-permute-start.8) | collective-permute-done | bytes 101408 | tf_op jit(solution)/shard_map/ppermute | solution.py:36
  40.6 2.1 %shard_map.132 = (bf16[3,4,4096]{2,1,0:T(4,128)(2,1)}, f32[16,128]{1,0:T(8,128)S(1)}) custom-call(bf16[3,4,4224]{2,1,0:T(4,128)(2,1)S(1)} %collective-permute-done.4.refs_0_, bf16[3,4,4224]{2,1,0:T(4,128)(2,1)S(1)} %collective-permute-done.6.refs_1_, bf16[3,4,4224]{2,1,0:T(4,128)(2,1)S(1)} %collective-permute-done.8.refs_2_, ...), custom_call_target="tpu_custom_call" | custom-call | flops 1048576 | bytes 1048576 | tf_op jit(solution)/shard_map/pallas_call | solution.py:44
  42.9 1.1 %collective-permute-done.10.refs_1_ = f32[16,128]{1,0:T(8,128)S(1)} collective-permute-done((f32[16,128]{1,0:T(8,128)S(1)}, f32[16,128]{1,0:T(8,128)S(1)}, u32[]{:S(2)}, u32[]{:S(2)}) %collective-permute-start.10) | collective-permute-done | bytes 8224 | tf_op jit(solution)/shard_map/ppermute | solution.py:31
  44.0 0.9 %shard_map.133 = bf16[3,4,4096]{2,1,0:T(4,128)(2,1)} custom-call(f32[16,128]{1,0:T(8,128)S(1)} %get-tuple-element.38.refs_0_, f32[16,128]{1,0:T(8,128)S(1)} %collective-permute-done.10.refs_1_, bf16[1,64,4096]{2,1,0:T(8,128)(2,1)S(1)} %copy-done.4, bf16[1,64,4096]{2,1,0:T(8,128)(2,1)S(1)} %collective-permute-done.11.refs_3_), custom_call_target="tpu_custom_call" | custom-call | flops 1048576 | bytes 1048576 | tf_op jit(solution)/shard_map/pallas_call | solution.py:44
  (33 shorter events, 0.8 us)
Async XLA Ops:
  0.6 21.8 %copy-start = (bf16[2,1024,512]{2,1,0:T(8,128)(2,1)S(1)}, bf16[2,1024,512]{2,1,0:T(8,128)(2,1)}, u32[]{:S(2)}) copy-start(bf16[2,1024,512]{2,1,0:T(8,128)(2,1)} %kv_ref.7) | copy-start | bytes 6291460
  0.6 6.0 %collective-permute-start = (bf16[3,4,4096]{2,1,0:T(4,128)(2,1)}, bf16[3,4,4096]{2,1,0:T(4,128)(2,1)S(1)}, u32[]{:S(2)}, u32[]{:S(2)}) collective-permute-start(bf16[3,4,4096]{2,1,0:T(4,128)(2,1)} %bitcast.6), channel_id=1, source_target_pairs={{2,0},{0,2},{3,1},{1,3},{6,4},{4,6},{7,5},{5,7},{10,8},{8,10},{11,... | collective-permute-start | bytes 294920 | tf_op jit(solution)/shard_map/ppermute | solution.py:31
  4.3 1.0 %copy-start.1 = (bf16[1,64,4096]{2,1,0:T(8,128)(2,1)S(1)}, bf16[1,64,4096]{2,1,0:T(8,128)(2,1)}, u32[]{:S(2)}) copy-start(bf16[1,64,4096]{2,1,0:T(8,128)(2,1)} %refs_1_.1) | copy-start | bytes 1572868
  5.4 0.9 %copy-start.6 = (bf16[4,3,4096]{2,0,1:T(4,128)(2,1)S(1)}, bf16[4,3,4096]{2,0,1:T(4,128)(2,1)}, u32[]{:S(2)}) copy-start(bf16[4,3,4096]{2,0,1:T(4,128)(2,1)} %param.11) | copy-start | bytes 294916
  7.6 1.2 %collective-permute-start.1 = (f32[32,64]{1,0:T(8,128)S(1)}, f32[32,64]{1,0:T(8,128)S(1)}, u32[]{:S(2)}, u32[]{:S(2)}) collective-permute-start(f32[32,64]{1,0:T(8,128)S(1)} %get-tuple-element.23.refs_0_), channel_id=1, source_target_pairs={{1,0},{0,1},{3,2},{2,3},{5,4},{4,5},{7,6},{6,7},{9,8},{8,9},{11,10... | collective-permute-start | bytes 24584 | tf_op jit(solution)/shard_map/ppermute | solution.py:31
  7.6 1.0 %copy-start.2 = (bf16[1,64,4096]{2,1,0:T(8,128)(2,1)S(1)}, bf16[1,64,4096]{2,1,0:T(8,128)(2,1)}, u32[]{:S(2)}) copy-start(bf16[1,64,4096]{2,1,0:T(8,128)(2,1)} %in_ref.1) | copy-start | bytes 1572868
  8.7 6.8 %copy-start.3 = (bf16[1,64,4096]{2,1,0:T(8,128)(2,1)S(1)}, bf16[1,64,4096]{2,1,0:T(8,128)(2,1)}, u32[]{:S(2)}) copy-start(bf16[1,64,4096]{2,1,0:T(8,128)(2,1)} %refs_5_) | copy-start | bytes 1572868
  8.7 7.1 %copy-start.4 = (bf16[1,64,4096]{2,1,0:T(8,128)(2,1)S(1)}, bf16[1,64,4096]{2,1,0:T(8,128)(2,1)}, u32[]{:S(2)}) copy-start(bf16[1,64,4096]{2,1,0:T(8,128)(2,1)} %refs_2_) | copy-start | bytes 1572868
  9.0 8.8 %collective-permute-start.2 = (f32[1,3,4,4096]{3,2,1,0:T(4,128)S(1)}, f32[1,3,4,4096]{3,2,1,0:T(4,128)S(1)}, u32[]{:S(2)}, u32[]{:S(2)}) collective-permute-start(f32[1,3,4,4096]{3,2,1,0:T(4,128)S(1)} %get-tuple-element.24), channel_id=1, source_target_pairs={{0,2},{2,0},{1,3},{3,1},{4,6},{6,4},{5,7},{7,5},{8,10},{10,8},{9,1... | collective-permute-start | bytes 589832 | tf_op jit(solution)/shard_map/ppermute | solution.py:36
  10.9 0.9 %copy-start.5 = (bf16[2,4,32,512]{3,2,1,0:T(8,128)(2,1)S(1)}, bf16[2,4,32,512]{3,2,1,0:T(8,128)(2,1)}, u32[]{:S(2)}) copy-start(bf16[2,4,32,512]{3,2,1,0:T(8,128)(2,1)} %suffix_ref.1) | copy-start | bytes 786436
  11.9 0.9 %copy-start.7 = (bf16[4,3,4096]{2,0,1:T(4,128)(2,1)S(1)}, bf16[4,3,4096]{2,0,1:T(4,128)(2,1)}, u32[]{:S(2)}) copy-start(bf16[4,3,4096]{2,0,1:T(4,128)(2,1)} %param.12) | copy-start | bytes 294916
  12.8 0.7 %copy-start.8 = (bf16[2,4,3,512]{3,1,2,0:T(4,128)(2,1)S(1)}, bf16[2,4,3,512]{3,1,2,0:T(4,128)(2,1)}, u32[]{:S(2)}) copy-start(bf16[2,4,3,512]{3,1,2,0:T(4,128)(2,1)} %param.13) | copy-start | bytes 73732
  13.5 0.7 %copy-start.9 = (s32[4,1]{0,1:T(1,128)S(1)}, s32[4,1]{0,1:T(1,128)}, u32[]{:S(2)}) copy-start(s32[4,1]{0,1:T(1,128)} %param.16) | copy-start | bytes 52
  14.1 0.7 %copy-start.11 = (s32[4]{0:T(128)S(1)}, s32[4]{0:T(128)}, u32[]{:S(2)}) copy-start(s32[4]{0:T(128)} %length_ref.1) | copy-start | bytes 52
  15.5 25.2 %collective-permute-start.9 = (bf16[1,64,4096]{2,1,0:T(8,128)(2,1)S(1)}, bf16[1,64,4096]{2,1,0:T(8,128)(2,1)S(1)}, u32[]{:S(2)}, u32[]{:S(2)}) collective-permute-start(bf16[1,64,4096]{2,1,0:T(8,128)(2,1)S(1)} %copy-done.3), channel_id=1, source_target_pairs={{2,0},{0,2},{3,1},{1,3},{6,4},{4,6},{7,5},{5,7},{10,8},{8,10},{11,... | collective-permute-start | bytes 1572872 | tf_op jit(solution)/shard_map/ppermute | solution.py:31
  15.7 27.1 %collective-permute-start.11 = (bf16[1,64,4096]{2,1,0:T(8,128)(2,1)S(1)}, bf16[1,64,4096]{2,1,0:T(8,128)(2,1)S(1)}, u32[]{:S(2)}, u32[]{:S(2)}) collective-permute-start(bf16[1,64,4096]{2,1,0:T(8,128)(2,1)S(1)} %copy-done.4), channel_id=1, source_target_pairs={{2,0},{0,2},{3,1},{1,3},{6,4},{4,6},{7,5},{5,7},{10,8},{8,10},{11,... | collective-permute-start | bytes 1572872 | tf_op jit(solution)/shard_map/ppermute | solution.py:31
  18.0 7.5 %collective-permute-start.3 = (bf16[3,4,4096]{2,1,0:T(4,128)(2,1)S(1)}, bf16[3,4,4096]{2,1,0:T(4,128)(2,1)S(1)}, u32[]{:S(2)}, u32[]{:S(2)}) collective-permute-start(bf16[3,4,4096]{2,1,0:T(4,128)(2,1)S(1)} %shard_map.127.query_ref), channel_id=1, source_target_pairs={{12,0},{8,4},{4,8},{0,12},{13,1},{9,5},{5,9},{1,13},{14,2},{10,6},... | collective-permute-start | bytes 294920 | tf_op jit(solution)/shard_map/ppermute | solution.py:31
  21.6 10.1 %collective-permute-start.5 = (bf16[3,4,4096]{2,1,0:T(4,128)(2,1)S(1)}, bf16[3,4,4096]{2,1,0:T(4,128)(2,1)S(1)}, u32[]{:S(2)}, u32[]{:S(2)}) collective-permute-start(bf16[3,4,4096]{2,1,0:T(4,128)(2,1)S(1)} %shard_map.127.query_ref), channel_id=1, source_target_pairs={{8,0},{12,4},{0,8},{4,12},{9,1},{13,5},{1,9},{5,13},{10,2},{14,6},... | collective-permute-start | bytes 294920 | tf_op jit(solution)/shard_map/ppermute | solution.py:31
  21.6 11.3 %collective-permute-start.7 = (bf16[3,4,4096]{2,1,0:T(4,128)(2,1)S(1)}, bf16[3,4,4096]{2,1,0:T(4,128)(2,1)S(1)}, u32[]{:S(2)}, u32[]{:S(2)}) collective-permute-start(bf16[3,4,4096]{2,1,0:T(4,128)(2,1)S(1)} %shard_map.127.query_ref), channel_id=1, source_target_pairs={{4,0},{0,4},{12,8},{8,12},{5,1},{1,5},{13,9},{9,13},{6,2},{2,6},{1... | collective-permute-start | bytes 294920 | tf_op jit(solution)/shard_map/ppermute | solution.py:31
  26.7 13.9 %copy-start.10 = (s32[4,1]{0,1:T(1,128)S(1)}, s32[4,1]{0,1:T(1,128)}, u32[]{:S(2)}) copy-start(s32[4,1]{0,1:T(1,128)} %param.16) | copy-start | bytes 52
  26.7 10.6 %collective-permute-start.4 = (bf16[3,4,4224]{2,1,0:T(4,128)(2,1)S(1)}, bf16[3,4,4224]{2,1,0:T(4,128)(2,1)S(1)}, u32[]{:S(2)}, u32[]{:S(2)}) collective-permute-start(bf16[3,4,4224]{2,1,0:T(4,128)(2,1)S(1)} %shard_map.129), channel_id=1, source_target_pairs={{0,12},{4,8},{8,4},{12,0},{1,13},{5,9},{9,5},{13,1},{2,14},{6,10},... | collective-permute-start | bytes 304136 | tf_op jit(solution)/shard_map/ppermute | solution.py:36
  32.9 6.7 %collective-permute-start.6 = (bf16[3,4,4224]{2,1,0:T(4,128)(2,1)S(1)}, bf16[3,4,4224]{2,1,0:T(4,128)(2,1)S(1)}, u32[]{:S(2)}, u32[]{:S(2)}) collective-permute-start(bf16[3,4,4224]{2,1,0:T(4,128)(2,1)S(1)} %shard_map.130), channel_id=1, source_target_pairs={{0,8},{4,12},{8,0},{12,4},{1,9},{5,13},{9,1},{13,5},{2,10},{6,14},... | collective-permute-start | bytes 304136 | tf_op jit(solution)/shard_map/ppermute | solution.py:36
  34.2 6.5 %collective-permute-start.8 = (bf16[3,4,4224]{2,1,0:T(4,128)(2,1)S(1)}, bf16[3,4,4224]{2,1,0:T(4,128)(2,1)S(1)}, u32[]{:S(2)}, u32[]{:S(2)}) collective-permute-start(bf16[3,4,4224]{2,1,0:T(4,128)(2,1)S(1)} %shard_map.131), channel_id=1, source_target_pairs={{0,4},{4,0},{8,12},{12,8},{1,5},{5,1},{9,13},{13,9},{2,6},{6,2},{1... | collective-permute-start | bytes 304136 | tf_op jit(solution)/shard_map/ppermute | solution.py:36
  42.8 1.2 %collective-permute-start.10 = (f32[16,128]{1,0:T(8,128)S(1)}, f32[16,128]{1,0:T(8,128)S(1)}, u32[]{:S(2)}, u32[]{:S(2)}) collective-permute-start(f32[16,128]{1,0:T(8,128)S(1)} %get-tuple-element.38.refs_0_), channel_id=1, source_target_pairs={{1,0},{0,1},{3,2},{2,3},{5,4},{4,5},{7,6},{6,7},{9,8},{8,9},{11,10... | collective-permute-start | bytes 24584 | tf_op jit(solution)/shard_map/ppermute | solution.py:31

commit v3 on v2

v3 whole, which is shorter than its diff:
```python
import functools
import math

import jax
import jax.numpy as jnp
from jax import lax
from jax.experimental import pallas as pl
from jax.experimental.pallas import tpu as pltpu
from jax.sharding import PartitionSpec as P

HEAD_SIZE = 128
LANES = 128
rope_base = 1000000.0
MASKED = -1e30
VMEM_BYTES = 8 << 20

VMEM = pl.BlockSpec(memory_space=pltpu.VMEM)
F32 = jnp.float32
BF16 = jnp.bfloat16


def peer(index, offset, size):
    if size & (size - 1) == 0:
        return index ^ offset
    return (index + offset) % size


def fetch(value, axis, offset):
    size = lax.axis_size(axis)
    return lax.ppermute(value, axis, [(peer(i, offset, size), i) for i in range(size)])


def send(value, axis, offset):
    size = lax.axis_size(axis)
    return lax.ppermute(value, axis, [(i, peer(i, offset, size)) for i in range(size)])


def dot(left, right, contract):
    return lax.dot_general(left, right, (contract, ((), ())), preferred_element_type=F32)


def call(kernel, out_shape, args, specs=None, scratch=(), flops=1 << 20, out_specs=None):
    return pl.pallas_call(
        kernel,
        out_shape=out_shape,
        in_specs=specs or [VMEM] * len(args),
        out_specs=out_specs or jax.tree.map(lambda unused: VMEM, out_shape),
        scratch_shapes=scratch,
        compiler_params=pltpu.CompilerParams(vmem_limit_bytes=VMEM_BYTES),
        cost_estimate=pl.CostEstimate(flops=flops, bytes_accessed=1 << 20, transcendentals=0),
    )(*args)


def rank_kernel(count, *refs):
    parts = refs[:count]
    down_ref = refs[count]
    earlier, out_ref, gathered = refs[count + 1 : -2], *refs[-2:]
    steps, rows, width = parts[0].shape
    resident, rank, _ = down_ref.shape
    pad_rows = gathered.shape[0] // count
    for j, ref in enumerate(parts):
        for t in range(steps):
            at = j * pad_rows + t * rows
            gathered[at : at + rows, :] = ref[t].astype(F32)
        at = j * pad_rows + steps * rows
        gathered[at : (j + 1) * pad_rows, :] = jnp.zeros((pad_rows - steps * rows, width), F32)
    result = dot(
        gathered[...].astype(BF16), down_ref[...].reshape(resident * rank, width), ((1,), (1,))
    )
    for ref in earlier:
        out_ref[: ref.shape[0], :] = ref[...]
    out_ref[out_ref.shape[0] - result.shape[0] :, :] = result


def own_rank_kernel(own_ref, down_ref, out_ref, kept_ref, gathered):
    rank_kernel(1, own_ref, down_ref, out_ref, gathered)
    kept_ref[...] = down_ref[...]


def copy_kernel(in_ref, _, out_ref):
    out_ref[...] = in_ref[...]


def query_kernel(parts, block, *refs):
    rank_refs = refs[:parts]
    up_ref, base_ref, cos_ref, sin_ref = refs[parts : parts + 4]
    out_ref, ids_ref = refs[-2:]
    resident, rank, _ = up_ref.shape
    steps, rows, width = out_ref.shape
    pad_rows = ids_ref.shape[0]
    ids_ref[...] = jnp.zeros_like(ids_ref)
    for t in range(steps):
        ids_ref[t * rows : (t + 1) * rows, :] = base_ref[t, :, width:].astype(F32)
    ids = ids_ref[:, LANES // 2 : LANES // 2 + 1].astype(jnp.int32)
    ranks = functools.reduce(
        jnp.add, [ref[block * pad_rows : (block + 1) * pad_rows, :] for ref in rank_refs]
    )
    lane = lax.broadcasted_iota(jnp.int32, ranks.shape, 1)
    owner = lax.axis_index("adapter") * resident + lane // rank
    chosen = jnp.where(owner == ids, ranks, 0.0).astype(BF16)
    correction = dot(chosen, up_ref[...].reshape(resident * rank, width), ((1,), (0,)))
    for t in range(steps):
        cos_part, sin_part = cos_ref[t], sin_ref[t]
        for h in range(width // HEAD_SIZE):
            at = slice(h * HEAD_SIZE, (h + 1) * HEAD_SIZE)
            piece = base_ref[t, :, at].astype(F32) + correction[t * rows : (t + 1) * rows, at]
            turned = piece * cos_part + pltpu.roll(piece, HEAD_SIZE // 2, 1) * sin_part
            out_ref[t, :, at] = turned.astype(BF16)


def pick_kernel(adapters, resident, *refs):
    queries = refs[:adapters]
    base_ref, _, out_ref, meta_ref = refs[adapters:]
    meta_ref[...] = base_ref[0, :, out_ref.shape[2] :].astype(F32).astype(jnp.int32)
    owner = meta_ref[:, LANES // 2 : LANES // 2 + 1] // resident
    x = lax.axis_index("adapter")
    for t in range(out_ref.shape[0]):
        picked = queries[0][t].astype(F32)
        for j in range(1, adapters):
            picked = jnp.where(owner == peer(x, j, adapters), queries[j][t].astype(F32), picked)
        out_ref[t] = picked.astype(BF16)


def load_queries(query_ref, rows_ref):
    steps, rows, _ = query_ref.shape
    rows_ref[...] = jnp.zeros_like(rows_ref)
    for t in range(steps):
        rows_ref[t * rows : (t + 1) * rows, :] = query_ref[t].astype(F32)


def group_queries(rows_ref, first, group):
    pieces = [
        rows_ref[:, first + g * HEAD_SIZE : first + (g + 1) * HEAD_SIZE] for g in range(group)
    ]
    return jnp.concatenate(pieces, axis=0).astype(BF16)


def attend(query, key, value, scale, extra=None):
    scores = dot(query, key, ((1,), (1,)))
    if extra is not None:
        more_key, more_value, bias = extra
        scores = jnp.concatenate([scores, dot(query, more_key, ((1,), (1,))) + bias], axis=1)
        value = jnp.concatenate([value, more_value], axis=0)
    peaks = jnp.max(scores, axis=1, keepdims=True)
    weight = jnp.exp2((scores - peaks) * scale).astype(BF16)
    ones = jnp.ones((value.shape[0], LANES), BF16)
    summed = dot(weight, jnp.concatenate([value, ones], axis=1), ((1,), (0,)))
    total = summed[:, HEAD_SIZE:]
    return summed[:, :HEAD_SIZE] / total, peaks * scale + jnp.log2(total)


def split_stat(stat, heads):
    first = stat.astype(BF16).astype(F32)
    second = (stat - first).astype(BF16).astype(F32)
    third = stat - first - second
    lane = lax.broadcasted_iota(jnp.int32, stat.shape, 1)
    out = jnp.where(lane < heads, first, 0.0)
    out = jnp.where((lane >= heads) & (lane < 2 * heads), pltpu.roll(second, heads, 1), out)
    out = jnp.where(
        (lane >= 2 * heads) & (lane < 3 * heads), pltpu.roll(third, 2 * heads, 1), out
    )
    return out


def far_kernel(scale, query_ref, kv_ref, *refs):
    out_ref, rows_ref, kept, stats = refs[-4:]
    steps, rows, width = query_ref.shape
    heads = width // HEAD_SIZE
    kv_heads = kv_ref.shape[2] // HEAD_SIZE
    group = heads // kv_heads
    cut = rows_ref.shape[0]
    load_queries(query_ref, rows_ref)
    lane = lax.broadcasted_iota(jnp.int32, (cut, LANES), 1)
    for kv in range(kv_heads):
        at = pl.ds(kv * HEAD_SIZE, HEAD_SIZE)
        queries = group_queries(rows_ref, kv * group * HEAD_SIZE, group)
        result, level = attend(queries, kv_ref[0, :, at], kv_ref[1, :, at], scale)
        for g in range(group):
            head = kv * group + g
            kept[:, head * HEAD_SIZE : (head + 1) * HEAD_SIZE] = result[g * cut : (g + 1) * cut]
            piece = level[g * cut : (g + 1) * cut]
            stats[...] = jnp.where(lane == head, piece, stats[...] if head else 0.0)
    packed = split_stat(stats[...], heads)
    for t in range(steps):
        at = t * rows
        out_ref[t, :, :width] = kept[at : at + rows, :].astype(BF16)
        out_ref[t, :, width:] = packed[at : at + rows, :].astype(BF16)


def near_kernel(scale, query_ref, kv_ref, suffix_ref, fresh_ref, meta_ref, *refs):
    own_ref, level_ref, rows_ref, kept, stats, fresh_rows, length_rows = refs
    load_queries(query_ref, rows_ref)
    steps, rows, width = query_ref.shape
    heads = width // HEAD_SIZE
    kv_heads = kv_ref.shape[2] // HEAD_SIZE
    group = heads // kv_heads
    cut = rows_ref.shape[0]
    fresh_rows[...] = jnp.zeros_like(fresh_rows)
    length_rows[...] = jnp.zeros_like(length_rows)
    for t in range(steps):
        length_rows[t * rows : (t + 1) * rows, :] = meta_ref[...]
        for part in range(2):
            fresh_rows[part, t * rows : (t + 1) * rows, :] = fresh_ref[part, t].astype(F32)
    slots = suffix_ref.shape[2]
    suffix_count = rows * slots
    shape = (cut, suffix_count + fresh_rows.shape[1])
    token = lax.broadcasted_iota(jnp.int32, shape, 0)
    column = lax.broadcasted_iota(jnp.int32, shape, 1)
    token_row, token_step = token % rows, token // rows
    fresh_at = column - suffix_count
    in_suffix = (column < suffix_count) & (column // slots == token_row)
    in_suffix &= column % slots < length_rows[:, 0:1]
    in_fresh = (column >= suffix_count) & (fresh_at % rows == token_row)
    in_fresh &= fresh_at // rows <= token_step
    bias = jnp.where(in_suffix | in_fresh, 0.0, MASKED)
    bias = jnp.concatenate([bias] * group, axis=0)
    lane = lax.broadcasted_iota(jnp.int32, (cut, LANES), 1)
    for kv in range(kv_heads):
        at = pl.ds(kv * HEAD_SIZE, HEAD_SIZE)
        more = [
            jnp.concatenate(
                [suffix_ref[part, r, :, at] for r in range(rows)]
                + [fresh_rows[part, :, at].astype(BF16)],
                axis=0,
            )
            for part in range(2)
        ]
        result, level = attend(
            group_queries(rows_ref, kv * group * HEAD_SIZE, group),
            kv_ref[0, :, at],
            kv_ref[1, :, at],
            scale,
            (more[0], more[1], bias),
        )
        for g in range(group):
            head = kv * group + g
            kept[:, head * HEAD_SIZE : (head + 1) * HEAD_SIZE] = result[g * cut : (g + 1) * cut]
            piece = level[g * cut : (g + 1) * cut]
            stats[...] = jnp.where(lane == head, piece, stats[...] if head else 0.0)
    for t in range(steps):
        own_ref[t] = kept[t * rows : (t + 1) * rows, :]
        level_ref[t] = stats[t * rows : (t + 1) * rows, :]


def message_levels(packed, heads):
    count = packed.shape[1]
    return (
        packed + pltpu.roll(packed, count - heads, 1) + pltpu.roll(packed, count - 2 * heads, 1)
    )


def mix(own_ref, level_ref, arrived, t, store):
    width = own_ref.shape[2]
    heads = width // HEAD_SIZE
    levels = [level_ref[t]]
    for ref in arrived:
        levels.append(message_levels(ref[t, :, width:].astype(F32), heads))
    highest = functools.reduce(jnp.maximum, levels)
    shares = [jnp.exp2(level - highest) for level in levels]
    total = functools.reduce(jnp.add, shares)
    shares = [share / total for share in shares]
    for h in range(heads):
        at = slice(h * HEAD_SIZE, (h + 1) * HEAD_SIZE)
        mixed = own_ref[t, :, at] * shares[0][:, h : h + 1]
        for ref, share in zip(arrived, shares[1:]):
            mixed += ref[t, :, at].astype(F32) * share[:, h : h + 1]
        store(at, mixed)
    return highest + jnp.log2(total)


def blend_kernel(*refs):
    arrived = refs[:-4]
    own_ref, level_ref, out_ref, out_level_ref = refs[-4:]
    for t in range(own_ref.shape[0]):

        def store(at, mixed):
            out_ref[t, :, at] = mixed

        out_level_ref[t] = mix(own_ref, level_ref, arrived, t, store)


def merge_kernel(messages, adapters, *refs):
    arrived = refs[:messages]
    own_ref, level_ref = refs[messages : messages + 2]
    downs = refs[2 + messages : 2 + messages + adapters]
    meta_ref, out_hbm, rank_ref, rows_ref, ids_ref, out_ref, sem = refs[2 + messages + adapters :]
    steps, rows, _ = own_ref.shape
    resident, rank, _ = downs[0].shape
    depth = resident * rank
    x = lax.axis_index("adapter")
    rows_ref[...] = jnp.zeros_like(rows_ref)
    ids_ref[...] = jnp.zeros_like(ids_ref)
    for t in range(steps):
        ids_ref[t * rows : (t + 1) * rows, :] = meta_ref[...]

        def store(at, mixed):
            out_ref[t, :, at] = mixed.astype(BF16)
            rows_ref[t * rows : (t + 1) * rows, at] = mixed

        mix(own_ref, level_ref, arrived, t, store)
    copy = pltpu.make_async_copy(out_ref, out_hbm, sem)
    copy.start()
    factors = jnp.concatenate([down[u] for down in downs for u in range(resident)], axis=0)
    result = dot(rows_ref[...].astype(BF16), factors, ((1,), (1,)))
    lane = lax.broadcasted_iota(jnp.int32, result.shape, 1)
    owner = peer(x, lane // depth, adapters) * resident + lane % depth // rank
    rank_ref[...] = jnp.where(owner == ids_ref[:, LANES // 2 : LANES // 2 + 1], result, 0.0)
    copy.wait()


def up_kernel(parts, adapters, *refs):
    ranks = refs[:parts]
    ups = refs[parts : parts + adapters]
    out_ref = refs[parts + adapters]
    steps, rows, width = out_ref.shape
    resident = ups[0].shape[0]
    chosen = functools.reduce(jnp.add, [ref[...] for ref in ranks]).astype(BF16)
    factors = jnp.concatenate([up[u] for up in ups for u in range(resident)], axis=0)
    result = dot(chosen, factors, ((1,), (0,)))
    for t in range(steps):
        out_ref[t] = result[t * rows : (t + 1) * rows].astype(BF16)


def rope_parts(lengths, steps, first_position):
    half_dim = HEAD_SIZE // 2
    frequency = rope_base ** (-2.0 * jnp.arange(half_dim, dtype=F32) / HEAD_SIZE)
    lengths = lengths.astype(jnp.int32)
    position = first_position + lengths + jnp.arange(steps, dtype=jnp.int32)[:, None]
    angles = position.astype(F32)[..., None] * frequency
    cos_part, sin_part = jnp.cos(angles), jnp.sin(angles)
    return (
        jnp.concatenate([cos_part, cos_part], axis=-1),
        jnp.concatenate([-sin_part, sin_part], axis=-1),
    )


def on_device(
    hidden,
    base_query_rows,
    fresh_key_value,
    suffix_key_value,
    suffix_length,
    row_adapter_index,
    prompt_key_value,
    query_down_factors,
    query_up_factors,
    output_down_factors,
    output_up_factors,
):
    rows, steps, width = hidden.shape
    seq_count, adapters, halves = (lax.axis_size(name) for name in ("seq", "adapter", "head"))
    slots = suffix_key_value.shape[2]
    resident, rank, _ = query_down_factors.shape
    depth = resident * rank
    tokens = rows * steps
    pad_rows = -(-tokens // 16) * 16
    heads = width // HEAD_SIZE
    kv_heads = prompt_key_value.shape[2] // HEAD_SIZE
    group = heads // kv_heads
    scale = math.log2(math.e) / math.sqrt(HEAD_SIZE)
    stat_lanes = -(-3 * heads // LANES) * LANES
    hidden = hidden.transpose(1, 0, 2)
    lane = jnp.arange(LANES, dtype=jnp.int32)
    facts = jnp.where(lane < LANES // 2, suffix_length[:, None], row_adapter_index).astype(BF16)
    base = jnp.concatenate([base_query_rows.transpose(1, 0, 2), jnp.broadcast_to(facts, (steps, rows, LANES))], axis=2)
    fresh = fresh_key_value.transpose(0, 2, 1, 3)

    own_rows = jax.ShapeDtypeStruct((pad_rows, depth), F32)
    factors = jax.ShapeDtypeStruct(query_down_factors.shape, BF16)
    own_ranks, own_down = call(
        own_rank_kernel,
        (own_rows, factors),
        (hidden, query_down_factors),
        scratch=[pltpu.VMEM((pad_rows, width), F32)],
    )
    hidden_of = [fetch(hidden, "adapter", j) for j in range(1, adapters)]
    ranks = call(
        functools.partial(rank_kernel, adapters - 1),
        jax.ShapeDtypeStruct((adapters * pad_rows, depth), F32),
        (*hidden_of, own_down, own_ranks),
        scratch=[pltpu.VMEM(((adapters - 1) * pad_rows, width), F32)],
    )
    rank_parts = [ranks] + [fetch(ranks, "head", j) for j in range(1, halves)]
    own_up = call(
        copy_kernel,
        jax.ShapeDtypeStruct(query_up_factors.shape, BF16),
        (query_up_factors, ranks),
    )
    first_position = prompt_key_value.shape[1] * seq_count
    block_queries = []
    for j in reversed(range(adapters)):
        block_base = fetch(base, "adapter", j) if j else base
        block_queries.insert(
            0,
            call(
                functools.partial(query_kernel, halves, j),
                jax.ShapeDtypeStruct((steps, rows, width), BF16),
                (
                    *rank_parts,
                    own_up,
                    block_base,
                    *rope_parts(block_base[0, :, width], steps, first_position),
                    *block_queries[:1],
                ),
                scratch=[pltpu.VMEM((pad_rows, LANES), F32)],
            ),
        )
    arrived = [send(part, "adapter", j) for j, part in enumerate(block_queries) if j]
    output_down_factors, output_up_factors, token = lax.optimization_barrier(
        (output_down_factors, output_up_factors, block_queries[0][0, :, :LANES])
    )
    queries, meta = call(
        functools.partial(pick_kernel, adapters, resident),
        (
            jax.ShapeDtypeStruct((steps, rows, width), BF16),
            jax.ShapeDtypeStruct((rows, LANES), jnp.int32),
        ),
        (block_queries[0], *arrived, base, token),
        flops=1 << 36,
    )
    message = jax.ShapeDtypeStruct((steps, rows, width + stat_lanes), BF16)
    query_scratch = [
        pltpu.VMEM((pad_rows, width), F32),
        pltpu.VMEM((pad_rows, width), F32),
        pltpu.VMEM((pad_rows, LANES), F32),
    ]
    piece_of = {0: queries}
    for k in range(1, seq_count):
        piece_of[k] = fetch(piece_of[k - 1], "seq", 1) if k % 2 else fetch(queries, "seq", k)
    order = list(range(2, seq_count)) + [1]
    messages = []
    for k in order:
        messages.append(
            call(
                functools.partial(far_kernel, scale),
                message,
                (piece_of[k], prompt_key_value),
                scratch=query_scratch,
            )
        )
    fresh_slots = -(-tokens // LANES) * LANES
    part_shapes = (
        jax.ShapeDtypeStruct((steps, rows, width), F32),
        jax.ShapeDtypeStruct((steps, rows, LANES), F32),
    )
    own, level = call(
        functools.partial(near_kernel, scale),
        part_shapes,
        (queries, prompt_key_value, suffix_key_value, fresh, meta),
        scratch=query_scratch
        + [
            pltpu.VMEM((2, fresh_slots, fresh.shape[3]), F32),
            pltpu.VMEM((pad_rows, LANES), jnp.int32),
        ],
    )
    output_downs = [output_down_factors] + [
        fetch(output_down_factors, "adapter", j) for j in range(1, adapters)
    ]
    output_ups = [output_up_factors] + [
        fetch(output_up_factors, "adapter", j) for j in range(1, adapters)
    ]
    partials = [send(part, "seq", k) for part, k in zip(messages, order)]
    early, partials = partials[:-2], partials[-2:]
    if early:
        own, level = call(blend_kernel, part_shapes, (*early, own, level))
    attended, out_rank = call(
        functools.partial(merge_kernel, len(partials), adapters),
        (
            jax.ShapeDtypeStruct((steps, rows, width), BF16),
            jax.ShapeDtypeStruct((pad_rows, adapters * depth), F32),
        ),
        (*partials, own, level, *output_downs, meta),
        scratch=[
            pltpu.VMEM((pad_rows, width), F32),
            pltpu.VMEM((pad_rows, LANES), jnp.int32),
            pltpu.VMEM((steps, rows, width), BF16),
            pltpu.SemaphoreType.DMA,
        ],
        out_specs=(pl.BlockSpec(memory_space=pl.ANY), VMEM),
    )
    out_ranks = [out_rank] + [fetch(out_rank, "head", j) for j in range(1, halves)]
    adapted = call(
        functools.partial(up_kernel, halves, adapters),
        jax.ShapeDtypeStruct((steps, rows, width), BF16),
        (*out_ranks, *output_ups),
    )
    return attended.transpose(1, 0, 2), adapted.transpose(1, 0, 2)


def solution(mesh):
    rows = ("groups", "seq", "adapter")
    factors = P(("groups", "adapter"), None, "head")
    placed = (
        P(rows, None, "head"),
        P(rows, None, "head"),
        P(None, rows, None, "head"),
        P(None, rows, None, "head"),
        P(rows),
        P(rows, None),
        P(None, ("groups", "seq"), "head"),
        factors,
        factors,
        factors,
        factors,
    )
    return jax.shard_map(
        on_device,
        mesh=mesh,
        in_specs=placed,
        out_specs=(P(rows, None, "head"), P(rows, None, "head")),
        check_vma=False,
    )
```

time: 45.3 us -> 41.2 us (0.909)
  local copies, waits for them, and re-layouts: 6.88 us -> 3.09 us
  other arithmetic: 0.88 us -> 2.2 us
  Pallas kernels: 10.3 us -> 9.24 us
  waiting for transfers between devices: 7.71 us -> 7.13 us
    unnamed x24 -> x16, local copies, waits for them, and re-layouts: 6.88 us -> 3.01 us
    ppermute x8 -> x9, starting transfers between devices: 9.62 us -> 11.5 us  [fetch(): lax.ppermute(value, axis, [(peer(i, offset, size), i) for i in range(size)])]
    ppermute x4, starting transfers between devices: 8.8 us -> 6.97 us  [send(): lax.ppermute(value, axis, [(i, peer(i, offset, size)) for i in range(size)])]
    pallas_call x12 -> x13, Pallas kernels: 10.3 us -> 9.24 us  [call(): pl.pallas_call(kernel, out_shape=out_shape, in_specs=specs or [VMEM] * le...]
    concatenate x0 -> x1, other arithmetic: none -> 0.96 us  [on_device(): jnp.concatenate([base_query_rows.transpose(1, 0, 2), jnp.broadcast_to(fac...]
    ppermute x8 -> x9, waiting for transfers between devices: 4.42 us -> 3.46 us  [fetch(): lax.ppermute(value, axis, [(peer(i, offset, size), i) for i in range(size)])]
    convert_element_type x0 -> x1, other arithmetic: none -> 0.75 us  [on_device(): jnp.where(lane < LANES // 2, suffix_length[:, None], row_adapter_index)]
    add x1 -> x2, other arithmetic: 0.66 us -> 0.12 us  [rope_parts(): first_position + lengths + jnp.arange(steps, dtype=jnp.int32)[:, None]]
  transfers between devices with their start and end apart: 12 -> 13, of which waited for: 7 -> 5; matrix products, arithmetic and copies ran while one was open for 2% -> 6% of each run, Pallas kernels for 18% -> 19%
where the time goes in v3:
time: 41.2 us; the launch traced here: 41 us
  starting transfers between devices  18.5 us (45%)
  Pallas kernels  9.24 us (22%)
  waiting for transfers between devices  7.13 us (17%)
  local copies, waits for them, and re-layouts  3.09 us (7%)
  other arithmetic  2.2 us (5%)
  between operations  0.81 us (2%)
    ppermute x9, starting transfers between devices, fetch(): lax.ppermute(value, axis, [(peer(i, offset, size), i) for i in range(size)])  11.5 us
    pallas_call x13, Pallas kernels, call(): pl.pallas_call(kernel, out_shape=out_shape, in_specs=specs or [VMEM] * le...  9.24 us
    ppermute x4, starting transfers between devices, send(): lax.ppermute(value, axis, [(i, peer(i, offset, size)) for i in range(size)])  6.97 us
    ppermute x4, waiting for transfers between devices, send(): lax.ppermute(value, axis, [(i, peer(i, offset, size)) for i in range(size)])  3.67 us
    ppermute x9, waiting for transfers between devices, fetch(): lax.ppermute(value, axis, [(peer(i, offset, size), i) for i in range(size)])  3.46 us
    unnamed x16, local copies, waits for them, and re-layouts  3.01 us
    concatenate x1, other arithmetic, on_device(): jnp.concatenate([base_query_rows.transpose(1, 0, 2), jnp.broadcast_to(fac...  0.96 us
  transfers between devices with their start and end apart: 13, of which 5 were waited for; matrix products, arithmetic and copies ran while one was open for 6% of the time, Pallas kernels for 19%

profile of v3, /device:TPU:0, one launch (start us, length us, event | category | flops | bytes accessed | tf_op | source)
XLA Modules:
  0.0 41.0 jit_solution(12727265545267760412)
XLA Ops:
  0.6 3.0 %collective-permute-start = (bf16[3,4,4096]{2,1,0:T(4,128)(2,1)}, bf16[3,4,4096]{2,1,0:T(4,128)(2,1)S(1)}, u32[]{:S(2)}, u32[]{:S(2)}) collective-permute-start(bf16[3,4,4096]{2,1,0:T(4,128)(2,1)} %bitcast.10), channel_id=1, source_target_pairs={{2,0},{0,2},{3,1},{1,3},{6,4},{4,6},{7,5},{5,7},{10,8},{8,10},{11,... | collective-permute-start | bytes 294920 | tf_op jit(solution)/shard_map/ppermute | solution.py:30
  3.6 0.8 %select_convert_fusion = bf16[4,128]{0,1:T(8,128)(2,1)S(1)} fusion(s32[4]{0:T(128)} %bitcast.15, s32[4]{0:T(128)} %param.15, pred[128]{0:T(512)(128)(4,1)S(1)} %iota_compare_fusion), kind=kLoop, calls=%fused_computation.1 | loop fusion | flops 1024 | bytes 1184 | tf_op jit(solution)/shard_map/convert_element_type | solution.py:364
  4.5 1.0 %pad_maximum_fusion.refs_3_.refs_2_ = bf16[3,4,4224]{2,1,0:T(4,128)(2,1)S(1)} fusion(bf16[3,4,128]{2,1,0:T(4,128)(2,1)S(1)} %broadcast_in_dim.38, bf16[3,4,4096]{2,1,0:T(4,128)(2,1)} %bitcast.14), kind=kLoop, calls=%fused_computation | loop fusion | flops 202752 | bytes 202752 | tf_op jit(solution)/shard_map/concatenate | solution.py:365
  5.6 1.0 %copy-done.1 = bf16[1,64,4096]{2,1,0:T(8,128)(2,1)S(1)} copy-done((bf16[1,64,4096]{2,1,0:T(8,128)(2,1)S(1)}, bf16[1,64,4096]{2,1,0:T(8,128)(2,1)}, u32[]{:S(2)}) %copy-start.1) | copy-done | bytes 524312
  6.6 0.9 %copy-done.6 = bf16[4,3,4096]{2,0,1:T(4,128)(2,1)S(1)} copy-done((bf16[4,3,4096]{2,0,1:T(4,128)(2,1)S(1)}, bf16[4,3,4096]{2,0,1:T(4,128)(2,1)}, u32[]{:S(2)}) %copy-start.6) | copy-done | bytes 98328
  7.5 0.3 shard_map.122
  7.8 0.3 shard_map.123._.refs_0_
  8.0 1.1 %copy-done.2 = bf16[1,64,4096]{2,1,0:T(8,128)(2,1)S(1)} copy-done((bf16[1,64,4096]{2,1,0:T(8,128)(2,1)S(1)}, bf16[1,64,4096]{2,1,0:T(8,128)(2,1)}, u32[]{:S(2)}) %copy-start.2) | copy-done | bytes 524312
  9.1 1.0 %collective-permute-done.2.refs_3_ = bf16[3,4,4224]{2,1,0:T(4,128)(2,1)S(1)} collective-permute-done((bf16[3,4,4224]{2,1,0:T(4,128)(2,1)S(1)}, bf16[3,4,4224]{2,1,0:T(4,128)(2,1)S(1)}, u32[]{:S(2)}, u32[]{:S(2)}) %collective-permute-start.2) | collective-permute-done | bytes 101408 | tf_op jit(solution)/shard_map/ppermute | solution.py:30
  10.3 0.2 fusion.3
  10.6 0.4 shard_map.125.refs_6_
  11.0 1.1 %collective-permute-start.3 = (bf16[3,4,4096]{2,1,0:T(4,128)(2,1)S(1)}, bf16[3,4,4096]{2,1,0:T(4,128)(2,1)S(1)}, u32[]{:S(2)}, u32[]{:S(2)}) collective-permute-start(bf16[3,4,4096]{2,1,0:T(4,128)(2,1)S(1)} %shard_map.125.refs_6_), channel_id=1, source_target_pairs={{0,2},{2,0},{1,3},{3,1},{4,6},{6,4},{5,7},{7,5},{8,10},{10,8},{9,1... | collective-permute-start | bytes 294920 | tf_op jit(solution)/shard_map/ppermute | solution.py:35
  12.1 0.4 shard_map.126.refs_0_
  12.5 1.1 %collective-permute-start.10 = (bf16[1,64,4096]{2,1,0:T(8,128)(2,1)S(1)}, bf16[1,64,4096]{2,1,0:T(8,128)(2,1)S(1)}, u32[]{:S(2)}, u32[]{:S(2)}) collective-permute-start(bf16[1,64,4096]{2,1,0:T(8,128)(2,1)S(1)} %copy-done.3), channel_id=1, source_target_pairs={{2,0},{0,2},{3,1},{1,3},{6,4},{4,6},{7,5},{5,7},{10,8},{8,10},{11,... | collective-permute-start | bytes 1572872 | tf_op jit(solution)/shard_map/ppermute | solution.py:30
  13.6 1.0 %collective-permute-start.12 = (bf16[1,64,4096]{2,1,0:T(8,128)(2,1)S(1)}, bf16[1,64,4096]{2,1,0:T(8,128)(2,1)S(1)}, u32[]{:S(2)}, u32[]{:S(2)}) collective-permute-start(bf16[1,64,4096]{2,1,0:T(8,128)(2,1)S(1)} %copy-done.4), channel_id=1, source_target_pairs={{2,0},{0,2},{3,1},{1,3},{6,4},{4,6},{7,5},{5,7},{10,8},{8,10},{11,... | collective-permute-start | bytes 1572872 | tf_op jit(solution)/shard_map/ppermute | solution.py:30
  14.6 1.5 %collective-permute-done.3.refs_1_ = bf16[3,4,4096]{2,1,0:T(4,128)(2,1)S(1)} collective-permute-done((bf16[3,4,4096]{2,1,0:T(4,128)(2,1)S(1)}, bf16[3,4,4096]{2,1,0:T(4,128)(2,1)S(1)}, u32[]{:S(2)}, u32[]{:S(2)}) %collective-permute-start.3) | collective-permute-done | bytes 98336 | tf_op jit(solution)/shard_map/ppermute | solution.py:35
  16.1 0.1 shard_map.127
  16.2 2.8 %collective-permute-start.4 = (bf16[3,4,4096]{2,1,0:T(4,128)(2,1)S(1)}, bf16[3,4,4096]{2,1,0:T(4,128)(2,1)S(1)}, u32[]{:S(2)}, u32[]{:S(2)}) collective-permute-start(bf16[3,4,4096]{2,1,0:T(4,128)(2,1)S(1)} %get-tuple-element.18.query_ref), channel_id=1, source_target_pairs={{8,0},{12,4},{0,8},{4,12},{9,1},{13,5},{1,9},{5,13},{10,2},{14,6},... | collective-permute-start | bytes 294920 | tf_op jit(solution)/shard_map/ppermute | solution.py:30
  19.0 1.6 %collective-permute-start.7 = (bf16[3,4,4096]{2,1,0:T(4,128)(2,1)S(1)}, bf16[3,4,4096]{2,1,0:T(4,128)(2,1)S(1)}, u32[]{:S(2)}, u32[]{:S(2)}) collective-permute-start(bf16[3,4,4096]{2,1,0:T(4,128)(2,1)S(1)} %get-tuple-element.18.query_ref), channel_id=1, source_target_pairs={{4,0},{0,4},{12,8},{8,12},{5,1},{1,5},{13,9},{9,13},{6,2},{2,6},{1... | collective-permute-start | bytes 294920 | tf_op jit(solution)/shard_map/ppermute | solution.py:30
  20.6 1.3 %collective-permute-done.4.query_ref = bf16[3,4,4096]{2,1,0:T(4,128)(2,1)S(1)} collective-permute-done((bf16[3,4,4096]{2,1,0:T(4,128)(2,1)S(1)}, bf16[3,4,4096]{2,1,0:T(4,128)(2,1)S(1)}, u32[]{:S(2)}, u32[]{:S(2)}) %collective-permute-start.4) | collective-permute-done | bytes 98336 | tf_op jit(solution)/shard_map/ppermute | solution.py:30
  21.9 1.8 %collective-permute-start.5 = (bf16[3,4,4096]{2,1,0:T(4,128)(2,1)S(1)}, bf16[3,4,4096]{2,1,0:T(4,128)(2,1)S(1)}, u32[]{:S(2)}, u32[]{:S(2)}) collective-permute-start(bf16[3,4,4096]{2,1,0:T(4,128)(2,1)S(1)} %collective-permute-done.4.query_ref), channel_id=1, source_target_pairs={{4,0},{0,4},{12,8},{8,12},{5,1},{1,5},{13,9},{9,13},{6,2},{2,6},{1... | collective-permute-start | bytes 294920 | tf_op jit(solution)/shard_map/ppermute | solution.py:30
  23.7 1.2 %shard_map.130 = bf16[3,4,4224]{2,1,0:T(4,128)(2,1)S(1)} custom-call(bf16[3,4,4096]{2,1,0:T(4,128)(2,1)S(1)} %collective-permute-done.4.query_ref, bf16[2,1024,512]{2,1,0:T(8,128)(2,1)S(1)} %copy-done), custom_call_target="tpu_custom_call" | custom-call | flops 1048576 | bytes 1048576 | tf_op jit(solution)/shard_map/pallas_call | solution.py:43
  24.9 3.4 %collective-permute-start.9 = (bf16[3,4,4224]{2,1,0:T(4,128)(2,1)S(1)}, bf16[3,4,4224]{2,1,0:T(4,128)(2,1)S(1)}, u32[]{:S(2)}, u32[]{:S(2)}) collective-permute-start(bf16[3,4,4224]{2,1,0:T(4,128)(2,1)S(1)} %shard_map.130), channel_id=1, source_target_pairs={{0,8},{4,12},{8,0},{12,4},{1,9},{5,13},{9,1},{13,5},{2,10},{6,14},... | collective-permute-start | bytes 304136 | tf_op jit(solution)/shard_map/ppermute | solution.py:35
  28.4 1.2 %shard_map.129 = bf16[3,4,4224]{2,1,0:T(4,128)(2,1)S(1)} custom-call(bf16[3,4,4096]{2,1,0:T(4,128)(2,1)S(1)} %collective-permute-done.7.query_ref, bf16[2,1024,512]{2,1,0:T(8,128)(2,1)S(1)} %copy-done), custom_call_target="tpu_custom_call" | custom-call | flops 1048576 | bytes 1048576 | tf_op jit(solution)/shard_map/pallas_call | solution.py:43
  29.6 1.2 %shard_map.128 = bf16[3,4,4224]{2,1,0:T(4,128)(2,1)S(1)} custom-call(bf16[3,4,4096]{2,1,0:T(4,128)(2,1)S(1)} %collective-permute-done.5.query_ref, bf16[2,1024,512]{2,1,0:T(8,128)(2,1)S(1)} %copy-done), custom_call_target="tpu_custom_call" | custom-call | flops 1048576 | bytes 1048576 | tf_op jit(solution)/shard_map/pallas_call | solution.py:43
  30.8 2.5 %collective-permute-start.6 = (bf16[3,4,4224]{2,1,0:T(4,128)(2,1)S(1)}, bf16[3,4,4224]{2,1,0:T(4,128)(2,1)S(1)}, u32[]{:S(2)}, u32[]{:S(2)}) collective-permute-start(bf16[3,4,4224]{2,1,0:T(4,128)(2,1)S(1)} %shard_map.128), channel_id=1, source_target_pairs={{0,12},{4,8},{8,4},{12,0},{1,13},{5,9},{9,5},{13,1},{2,14},{6,10},... | collective-permute-start | bytes 304136 | tf_op jit(solution)/shard_map/ppermute | solution.py:35
  33.3 1.3 %shard_map.131 = (f32[3,4,4096]{2,1,0:T(4,128)S(1)}, f32[3,4,128]{2,1,0:T(4,128)S(1)}) custom-call(bf16[3,4,4096]{2,1,0:T(4,128)(2,1)S(1)} %get-tuple-element.18.query_ref, bf16[2,1024,512]{2,1,0:T(8,128)(2,1)S(1)} %copy-done, bf16[2,4,32,512]{3,2,1,0:T(8,128)(2,1)S(1)} %copy-done.5, bf16[2,3,4,512]{3,2,1,0:T(4,128)(2,1)S(1)} %bitcast.12, ...), custom_call_target="tpu_custom_call" | custom-call | flops 1048576 | bytes 1048576 | tf_op jit(solution)/shard_map/pallas_call | solution.py:43
  34.6 0.6 %shard_map.132 = (f32[3,4,4096]{2,1,0:T(4,128)S(1)}, f32[3,4,128]{2,1,0:T(4,128)S(1)}) custom-call(bf16[3,4,4224]{2,1,0:T(4,128)(2,1)S(1)} %collective-permute-done.9.refs_0_, f32[3,4,4096]{2,1,0:T(4,128)S(1)} %get-tuple-element.20.refs_1_, f32[3,4,128]{2,1,0:T(4,128)S(1)} %get-tuple-element.21.refs_2_), custom_call_target="tpu_custom_call" | custom-call | flops 1048576 | bytes 1048576 | tf_op jit(solution)/shard_map/pallas_call | solution.py:43
  35.2 2.2 %collective-permute-done.6.refs_0_ = bf16[3,4,4224]{2,1,0:T(4,128)(2,1)S(1)} collective-permute-done((bf16[3,4,4224]{2,1,0:T(4,128)(2,1)S(1)}, bf16[3,4,4224]{2,1,0:T(4,128)(2,1)S(1)}, u32[]{:S(2)}, u32[]{:S(2)}) %collective-permute-start.6) | collective-permute-done | bytes 101408 | tf_op jit(solution)/shard_map/ppermute | solution.py:35
  37.4 1.4 %shard_map.133 = (bf16[3,4,4096]{2,1,0:T(4,128)(2,1)}, f32[16,128]{1,0:T(8,128)S(1)}) custom-call(bf16[3,4,4224]{2,1,0:T(4,128)(2,1)S(1)} %collective-permute-done.6.refs_0_, bf16[3,4,4224]{2,1,0:T(4,128)(2,1)S(1)} %collective-permute-done.8.refs_1_, f32[3,4,4096]{2,1,0:T(4,128)S(1)} %get-tuple-element.22.refs_2_, ...), custom_call_target="tpu_custom_call" | custom-call | flops 1048576 | bytes 1048576 | tf_op jit(solution)/shard_map/pallas_call | solution.py:43
  38.9 1.1 %collective-permute-done.11.refs_1_ = f32[16,128]{1,0:T(8,128)S(1)} collective-permute-done((f32[16,128]{1,0:T(8,128)S(1)}, f32[16,128]{1,0:T(8,128)S(1)}, u32[]{:S(2)}, u32[]{:S(2)}) %collective-permute-start.11) | collective-permute-done | bytes 8224 | tf_op jit(solution)/shard_map/ppermute | solution.py:30
  40.0 0.9 %shard_map.134 = bf16[3,4,4096]{2,1,0:T(4,128)(2,1)} custom-call(f32[16,128]{1,0:T(8,128)S(1)} %get-tuple-element.26.refs_0_, f32[16,128]{1,0:T(8,128)S(1)} %collective-permute-done.11.refs_1_, bf16[1,64,4096]{2,1,0:T(8,128)(2,1)S(1)} %copy-done.4, bf16[1,64,4096]{2,1,0:T(8,128)(2,1)S(1)} %collective-permute-done.12.refs_3_), custom_call_target="tpu_custom_call" | custom-call | flops 1048576 | bytes 1048576 | tf_op jit(solution)/shard_map/pallas_call | solution.py:43
  (37 shorter events, 0.7 us)
Async XLA Ops:
  0.6 7.1 %collective-permute-start = (bf16[3,4,4096]{2,1,0:T(4,128)(2,1)}, bf16[3,4,4096]{2,1,0:T(4,128)(2,1)S(1)}, u32[]{:S(2)}, u32[]{:S(2)}) collective-permute-start(bf16[3,4,4096]{2,1,0:T(4,128)(2,1)} %bitcast.10), channel_id=1, source_target_pairs={{2,0},{0,2},{3,1},{1,3},{6,4},{4,6},{7,5},{5,7},{10,8},{8,10},{11,... | collective-permute-start | bytes 294920 | tf_op jit(solution)/shard_map/ppermute | solution.py:30
  5.4 4.7 %collective-permute-start.2 = (bf16[3,4,4224]{2,1,0:T(4,128)(2,1)S(1)}, bf16[3,4,4224]{2,1,0:T(4,128)(2,1)S(1)}, u32[]{:S(2)}, u32[]{:S(2)}) collective-permute-start(bf16[3,4,4224]{2,1,0:T(4,128)(2,1)S(1)} %pad_maximum_fusion.refs_3_.refs_2_), channel_id=1, source_target_pairs={{2,0},{0,2},{3,1},{1,3},{6,4},{4,6},{7,5},{5,7},{10,8},{8,10},{11,... | collective-permute-start | bytes 304136 | tf_op jit(solution)/shard_map/ppermute | solution.py:30
  5.5 1.0 %copy-start.1 = (bf16[1,64,4096]{2,1,0:T(8,128)(2,1)S(1)}, bf16[1,64,4096]{2,1,0:T(8,128)(2,1)}, u32[]{:S(2)}) copy-start(bf16[1,64,4096]{2,1,0:T(8,128)(2,1)} %down_ref.1) | copy-start | bytes 1572868
  6.6 0.9 %copy-start.6 = (bf16[4,3,4096]{2,0,1:T(4,128)(2,1)S(1)}, bf16[4,3,4096]{2,0,1:T(4,128)(2,1)}, u32[]{:S(2)}) copy-start(bf16[4,3,4096]{2,0,1:T(4,128)(2,1)} %param.11) | copy-start | bytes 294916
  7.5 5.0 %copy-start.3 = (bf16[1,64,4096]{2,1,0:T(8,128)(2,1)S(1)}, bf16[1,64,4096]{2,1,0:T(8,128)(2,1)}, u32[]{:S(2)}) copy-start(bf16[1,64,4096]{2,1,0:T(8,128)(2,1)} %refs_4_) | copy-start | bytes 1572868
  7.5 6.1 %copy-start.4 = (bf16[1,64,4096]{2,1,0:T(8,128)(2,1)S(1)}, bf16[1,64,4096]{2,1,0:T(8,128)(2,1)}, u32[]{:S(2)}) copy-start(bf16[1,64,4096]{2,1,0:T(8,128)(2,1)} %refs_2_) | copy-start | bytes 1572868
  8.0 2.6 %collective-permute-start.1 = (f32[32,64]{1,0:T(8,128)S(1)}, f32[32,64]{1,0:T(8,128)S(1)}, u32[]{:S(2)}, u32[]{:S(2)}) collective-permute-start(f32[32,64]{1,0:T(8,128)S(1)} %shard_map.123._.refs_0_), channel_id=1, source_target_pairs={{1,0},{0,1},{3,2},{2,3},{5,4},{4,5},{7,6},{6,7},{9,8},{8,9},{11,10... | collective-permute-start | bytes 24584 | tf_op jit(solution)/shard_map/ppermute | solution.py:30
  8.0 1.1 %copy-start.2 = (bf16[1,64,4096]{2,1,0:T(8,128)(2,1)S(1)}, bf16[1,64,4096]{2,1,0:T(8,128)(2,1)}, u32[]{:S(2)}) copy-start(bf16[1,64,4096]{2,1,0:T(8,128)(2,1)} %in_ref.1) | copy-start | bytes 1572868
  11.0 5.0 %collective-permute-start.3 = (bf16[3,4,4096]{2,1,0:T(4,128)(2,1)S(1)}, bf16[3,4,4096]{2,1,0:T(4,128)(2,1)S(1)}, u32[]{:S(2)}, u32[]{:S(2)}) collective-permute-start(bf16[3,4,4096]{2,1,0:T(4,128)(2,1)S(1)} %shard_map.125.refs_6_), channel_id=1, source_target_pairs={{0,2},{2,0},{1,3},{3,1},{4,6},{6,4},{5,7},{7,5},{8,10},{10,8},{9,1... | collective-permute-start | bytes 294920 | tf_op jit(solution)/shard_map/ppermute | solution.py:35
  12.5 11.3 %copy-start = (bf16[2,1024,512]{2,1,0:T(8,128)(2,1)S(1)}, bf16[2,1024,512]{2,1,0:T(8,128)(2,1)}, u32[]{:S(2)}) copy-start(bf16[2,1024,512]{2,1,0:T(8,128)(2,1)} %kv_ref.7) | copy-start | bytes 6291460
  12.5 24.9 %collective-permute-start.10 = (bf16[1,64,4096]{2,1,0:T(8,128)(2,1)S(1)}, bf16[1,64,4096]{2,1,0:T(8,128)(2,1)S(1)}, u32[]{:S(2)}, u32[]{:S(2)}) collective-permute-start(bf16[1,64,4096]{2,1,0:T(8,128)(2,1)S(1)} %copy-done.3), channel_id=1, source_target_pairs={{2,0},{0,2},{3,1},{1,3},{6,4},{4,6},{7,5},{5,7},{10,8},{8,10},{11,... | collective-permute-start | bytes 1572872 | tf_op jit(solution)/shard_map/ppermute | solution.py:30
  13.6 25.3 %collective-permute-start.12 = (bf16[1,64,4096]{2,1,0:T(8,128)(2,1)S(1)}, bf16[1,64,4096]{2,1,0:T(8,128)(2,1)S(1)}, u32[]{:S(2)}, u32[]{:S(2)}) collective-permute-start(bf16[1,64,4096]{2,1,0:T(8,128)(2,1)S(1)} %copy-done.4), channel_id=1, source_target_pairs={{2,0},{0,2},{3,1},{1,3},{6,4},{4,6},{7,5},{5,7},{10,8},{8,10},{11,... | collective-permute-start | bytes 1572872 | tf_op jit(solution)/shard_map/ppermute | solution.py:30
  16.2 5.7 %collective-permute-start.4 = (bf16[3,4,4096]{2,1,0:T(4,128)(2,1)S(1)}, bf16[3,4,4096]{2,1,0:T(4,128)(2,1)S(1)}, u32[]{:S(2)}, u32[]{:S(2)}) collective-permute-start(bf16[3,4,4096]{2,1,0:T(4,128)(2,1)S(1)} %get-tuple-element.18.query_ref), channel_id=1, source_target_pairs={{8,0},{12,4},{0,8},{4,12},{9,1},{13,5},{1,9},{5,13},{10,2},{14,6},... | collective-permute-start | bytes 294920 | tf_op jit(solution)/shard_map/ppermute | solution.py:30
  19.0 9.4 %collective-permute-start.7 = (bf16[3,4,4096]{2,1,0:T(4,128)(2,1)S(1)}, bf16[3,4,4096]{2,1,0:T(4,128)(2,1)S(1)}, u32[]{:S(2)}, u32[]{:S(2)}) collective-permute-start(bf16[3,4,4096]{2,1,0:T(4,128)(2,1)S(1)} %get-tuple-element.18.query_ref), channel_id=1, source_target_pairs={{4,0},{0,4},{12,8},{8,12},{5,1},{1,5},{13,9},{9,13},{6,2},{2,6},{1... | collective-permute-start | bytes 294920 | tf_op jit(solution)/shard_map/ppermute | solution.py:30
  21.9 7.7 %collective-permute-start.5 = (bf16[3,4,4096]{2,1,0:T(4,128)(2,1)S(1)}, bf16[3,4,4096]{2,1,0:T(4,128)(2,1)S(1)}, u32[]{:S(2)}, u32[]{:S(2)}) collective-permute-start(bf16[3,4,4096]{2,1,0:T(4,128)(2,1)S(1)} %collective-permute-done.4.query_ref), channel_id=1, source_target_pairs={{4,0},{0,4},{12,8},{8,12},{5,1},{1,5},{13,9},{9,13},{6,2},{2,6},{1... | collective-permute-start | bytes 294920 | tf_op jit(solution)/shard_map/ppermute | solution.py:30
  24.9 8.3 %copy-start.5 = (bf16[2,4,32,512]{3,2,1,0:T(8,128)(2,1)S(1)}, bf16[2,4,32,512]{3,2,1,0:T(8,128)(2,1)}, u32[]{:S(2)}) copy-start(bf16[2,4,32,512]{3,2,1,0:T(8,128)(2,1)} %suffix_ref.1) | copy-start | bytes 786436
  24.9 8.3 %copy-start.7 = (bf16[2,4,3,512]{3,1,2,0:T(4,128)(2,1)S(1)}, bf16[2,4,3,512]{3,1,2,0:T(4,128)(2,1)}, u32[]{:S(2)}) copy-start(bf16[2,4,3,512]{3,1,2,0:T(4,128)(2,1)} %param.13) | copy-start | bytes 73732
  24.9 9.7 %collective-permute-start.9 = (bf16[3,4,4224]{2,1,0:T(4,128)(2,1)S(1)}, bf16[3,4,4224]{2,1,0:T(4,128)(2,1)S(1)}, u32[]{:S(2)}, u32[]{:S(2)}) collective-permute-start(bf16[3,4,4224]{2,1,0:T(4,128)(2,1)S(1)} %shard_map.130), channel_id=1, source_target_pairs={{0,8},{4,12},{8,0},{12,4},{1,9},{5,13},{9,1},{13,5},{2,10},{6,14},... | collective-permute-start | bytes 304136 | tf_op jit(solution)/shard_map/ppermute | solution.py:35
  29.6 5.6 %collective-permute-start.8 = (bf16[3,4,4224]{2,1,0:T(4,128)(2,1)S(1)}, bf16[3,4,4224]{2,1,0:T(4,128)(2,1)S(1)}, u32[]{:S(2)}, u32[]{:S(2)}) collective-permute-start(bf16[3,4,4224]{2,1,0:T(4,128)(2,1)S(1)} %shard_map.129), channel_id=1, source_target_pairs={{0,4},{4,0},{8,12},{12,8},{1,5},{5,1},{9,13},{13,9},{2,6},{6,2},{1... | collective-permute-start | bytes 304136 | tf_op jit(solution)/shard_map/ppermute | solution.py:35
  30.8 6.6 %collective-permute-start.6 = (bf16[3,4,4224]{2,1,0:T(4,128)(2,1)S(1)}, bf16[3,4,4224]{2,1,0:T(4,128)(2,1)S(1)}, u32[]{:S(2)}, u32[]{:S(2)}) collective-permute-start(bf16[3,4,4224]{2,1,0:T(4,128)(2,1)S(1)} %shard_map.128), channel_id=1, source_target_pairs={{0,12},{4,8},{8,4},{12,0},{1,13},{5,9},{9,5},{13,1},{2,14},{6,10},... | collective-permute-start | bytes 304136 | tf_op jit(solution)/shard_map/ppermute | solution.py:35
  38.8 1.2 %collective-permute-start.11 = (f32[16,128]{1,0:T(8,128)S(1)}, f32[16,128]{1,0:T(8,128)S(1)}, u32[]{:S(2)}, u32[]{:S(2)}) collective-permute-start(f32[16,128]{1,0:T(8,128)S(1)} %get-tuple-element.26.refs_0_), channel_id=1, source_target_pairs={{1,0},{0,1},{3,2},{2,3},{5,4},{4,5},{7,6},{6,7},{9,8},{8,9},{11,10... | collective-permute-start | bytes 24584 | tf_op jit(solution)/shard_map/ppermute | solution.py:30

commit v4 on v3

--- a/solution.py
+++ b/solution.py
@@ -72,7 +72,17 @@
     out_ref[out_ref.shape[0] - result.shape[0] :, :] = result
 
 
-def own_rank_kernel(own_ref, down_ref, out_ref, kept_ref, gathered):
+def first_kernel(out_ref):
+    out_ref[...] = jnp.zeros_like(out_ref)
+
+
+def own_rank_kernel(own_ref, down_ref, table_ref, _, out_ref, kept_ref, split_ref, gathered):
+    width = table_ref.shape[1]
+    rest = table_ref[...]
+    for i in range(3):
+        part = rest.astype(BF16)
+        split_ref[:, i * width : (i + 1) * width] = part
+        rest = rest - part.astype(F32)
     rank_kernel(1, own_ref, down_ref, out_ref, gathered)
     kept_ref[...] = down_ref[...]
 
@@ -83,15 +93,21 @@
 
 def query_kernel(parts, block, *refs):
     rank_refs = refs[:parts]
-    up_ref, base_ref, cos_ref, sin_ref = refs[parts : parts + 4]
-    out_ref, ids_ref = refs[-2:]
+    up_ref, base_ref, table_ref = refs[parts : parts + 3]
+    out_ref, facts_ref, angles_ref = refs[-3:]
     resident, rank, _ = up_ref.shape
     steps, rows, width = out_ref.shape
-    pad_rows = ids_ref.shape[0]
-    ids_ref[...] = jnp.zeros_like(ids_ref)
-    for t in range(steps):
-        ids_ref[t * rows : (t + 1) * rows, :] = base_ref[t, :, width:].astype(F32)
-    ids = ids_ref[:, LANES // 2 : LANES // 2 + 1].astype(jnp.int32)
+    pad_rows = facts_ref.shape[0]
+    facts_ref[...] = jnp.zeros_like(facts_ref)
+    for t in range(steps):
+        facts_ref[t * rows : (t + 1) * rows, :] = base_ref[t, :, width:].astype(F32)
+    ids = facts_ref[:, LANES // 2 : LANES // 2 + 1].astype(jnp.int32)
+    shape = (pad_rows, table_ref.shape[0])
+    step = lax.broadcasted_iota(jnp.int32, shape, 0) // rows
+    place = (lax.broadcasted_iota(jnp.int32, shape, 1) - step).astype(F32)
+    picked = (place == facts_ref[:, 0:1]).astype(F32).astype(BF16)
+    found = dot(picked, table_ref[...], ((1,), (0,)))
+    angles_ref[...] = found[:, : 2 * LANES] + found[:, 2 * LANES : 4 * LANES] + found[:, 4 * LANES :]
     ranks = functools.reduce(
         jnp.add, [ref[block * pad_rows : (block + 1) * pad_rows, :] for ref in rank_refs]
     )
@@ -100,7 +116,8 @@
     chosen = jnp.where(owner == ids, ranks, 0.0).astype(BF16)
     correction = dot(chosen, up_ref[...].reshape(resident * rank, width), ((1,), (0,)))
     for t in range(steps):
-        cos_part, sin_part = cos_ref[t], sin_ref[t]
+        cos_part = angles_ref[t * rows : (t + 1) * rows, :LANES]
+        sin_part = angles_ref[t * rows : (t + 1) * rows, LANES:]
         for h in range(width // HEAD_SIZE):
             at = slice(h * HEAD_SIZE, (h + 1) * HEAD_SIZE)
             piece = base_ref[t, :, at].astype(F32) + correction[t * rows : (t + 1) * rows, at]
@@ -135,18 +152,22 @@
     return jnp.concatenate(pieces, axis=0).astype(BF16)
 
 
-def attend(query, key, value, scale, extra=None):
-    scores = dot(query, key, ((1,), (1,)))
-    if extra is not None:
-        more_key, more_value, bias = extra
-        scores = jnp.concatenate([scores, dot(query, more_key, ((1,), (1,))) + bias], axis=1)
-        value = jnp.concatenate([value, more_value], axis=0)
-    peaks = jnp.max(scores, axis=1, keepdims=True)
-    weight = jnp.exp2((scores - peaks) * scale).astype(BF16)
-    ones = jnp.ones((value.shape[0], LANES), BF16)
-    summed = dot(weight, jnp.concatenate([value, ones], axis=1), ((1,), (0,)))
-    total = summed[:, HEAD_SIZE:]
-    return summed[:, :HEAD_SIZE] / total, peaks * scale + jnp.log2(total)
+def attend(queries, keys, values, scale):
+    scores = []
+    for query, parts in zip(queries, keys):
+        found = []
+        for key, bias in parts:
+            part = dot(query, key, ((1,), (1,)))
+            found.append(part if bias is None else part + bias)
+        scores.append(found[0] if len(found) == 1 else jnp.concatenate(found, axis=1))
+    peaks = [jnp.max(score, axis=1, keepdims=True) * scale for score in scores]
+    weights = [jnp.exp2(s * scale - p).astype(BF16) for s, p in zip(scores, peaks)]
+    for weight, peak, parts in zip(weights, peaks, values):
+        value = parts[0] if len(parts) == 1 else jnp.concatenate(parts, axis=0)
+        ones = jnp.ones((value.shape[0], LANES), BF16)
+        summed = dot(weight, jnp.concatenate([value, ones], axis=1), ((1,), (0,)))
+        total = summed[:, HEAD_SIZE:]
+        yield summed[:, :HEAD_SIZE] * (1.0 / total), peak + jnp.log2(total)
 
 
 def split_stat(stat, heads):
@@ -162,29 +183,36 @@
     return out
 
 
-def far_kernel(scale, query_ref, kv_ref, *refs):
-    out_ref, rows_ref, kept, stats = refs[-4:]
+def far_kernel(scale, query_ref, kv_ref, out_ref, rows_ref, kept, stats_ref):
     steps, rows, width = query_ref.shape
     heads = width // HEAD_SIZE
     kv_heads = kv_ref.shape[2] // HEAD_SIZE
     group = heads // kv_heads
     cut = rows_ref.shape[0]
     load_queries(query_ref, rows_ref)
+    columns = [slice(kv * HEAD_SIZE, (kv + 1) * HEAD_SIZE) for kv in range(kv_heads)]
+    found = attend(
+        [group_queries(rows_ref, kv * group * HEAD_SIZE, group) for kv in range(kv_heads)],
+        [[(kv_ref[0, :, at], None)] for at in columns],
+        [[kv_ref[1, :, at]] for at in columns],
+        scale,
+    )
+    stats_ref[...] = split_stat(collect(found, kept, cut, group), heads)
+    for t in range(steps):
+        at = t * rows
+        out_ref[t, :, :width] = kept[at : at + rows, :].astype(BF16)
+        out_ref[t, :, width:] = stats_ref[at : at + rows, :].astype(BF16)
+
+
+def collect(found, kept, cut, group):
     lane = lax.broadcasted_iota(jnp.int32, (cut, LANES), 1)
-    for kv in range(kv_heads):
-        at = pl.ds(kv * HEAD_SIZE, HEAD_SIZE)
-        queries = group_queries(rows_ref, kv * group * HEAD_SIZE, group)
-        result, level = attend(queries, kv_ref[0, :, at], kv_ref[1, :, at], scale)
+    stats = jnp.zeros((cut, LANES), F32)
+    for kv, (result, level) in enumerate(found):
         for g in range(group):
             head = kv * group + g
             kept[:, head * HEAD_SIZE : (head + 1) * HEAD_SIZE] = result[g * cut : (g + 1) * cut]
-            piece = level[g * cut : (g + 1) * cut]
-            stats[...] = jnp.where(lane == head, piece, stats[...] if head else 0.0)
-    packed = split_stat(stats[...], heads)
-    for t in range(steps):
-        at = t * rows
-        out_ref[t, :, :width] = kept[at : at + rows, :].astype(BF16)
-        out_ref[t, :, width:] = packed[at : at + rows, :].astype(BF16)
+            stats = jnp.where(lane == head, level[g * cut : (g + 1) * cut], stats)
+    return stats
 
 
 def near_kernel(scale, query_ref, kv_ref, suffix_ref, fresh_ref, meta_ref, *refs):
@@ -214,29 +242,19 @@
     in_fresh &= fresh_at // rows <= token_step
     bias = jnp.where(in_suffix | in_fresh, 0.0, MASKED)
     bias = jnp.concatenate([bias] * group, axis=0)
-    lane = lax.broadcasted_iota(jnp.int32, (cut, LANES), 1)
-    for kv in range(kv_heads):
-        at = pl.ds(kv * HEAD_SIZE, HEAD_SIZE)
-        more = [
-            jnp.concatenate(
-                [suffix_ref[part, r, :, at] for r in range(rows)]
-                + [fresh_rows[part, :, at].astype(BF16)],
-                axis=0,
-            )
-            for part in range(2)
-        ]
-        result, level = attend(
-            group_queries(rows_ref, kv * group * HEAD_SIZE, group),
-            kv_ref[0, :, at],
-            kv_ref[1, :, at],
-            scale,
-            (more[0], more[1], bias),
-        )
-        for g in range(group):
-            head = kv * group + g
-            kept[:, head * HEAD_SIZE : (head + 1) * HEAD_SIZE] = result[g * cut : (g + 1) * cut]
-            piece = level[g * cut : (g + 1) * cut]
-            stats[...] = jnp.where(lane == head, piece, stats[...] if head else 0.0)
+    columns = [slice(kv * HEAD_SIZE, (kv + 1) * HEAD_SIZE) for kv in range(kv_heads)]
+
+    def local(part, at):
+        pieces = [suffix_ref[part, r, :, at] for r in range(rows)]
+        return jnp.concatenate(pieces + [fresh_rows[part, :, at].astype(BF16)], axis=0)
+
+    found = attend(
+        [group_queries(rows_ref, kv * group * HEAD_SIZE, group) for kv in range(kv_heads)],
+        [[(kv_ref[0, :, at], None), (local(0, at), bias)] for at in columns],
+        [[kv_ref[1, :, at], local(1, at)] for at in columns],
+        scale,
+    )
+    stats[...] = collect(found, kept, cut, group)
     for t in range(steps):
         own_ref[t] = kept[t * rows : (t + 1) * rows, :]
         level_ref[t] = stats[t * rows : (t + 1) * rows, :]
@@ -321,17 +339,13 @@
         out_ref[t] = result[t * rows : (t + 1) * rows].astype(BF16)
 
 
-def rope_parts(lengths, steps, first_position):
+def rope_table(slots, first_position):
     half_dim = HEAD_SIZE // 2
     frequency = rope_base ** (-2.0 * jnp.arange(half_dim, dtype=F32) / HEAD_SIZE)
-    lengths = lengths.astype(jnp.int32)
-    position = first_position + lengths + jnp.arange(steps, dtype=jnp.int32)[:, None]
-    angles = position.astype(F32)[..., None] * frequency
+    position = (first_position + jnp.arange(slots, dtype=jnp.int32)).astype(F32)
+    angles = position[:, None] * frequency
     cos_part, sin_part = jnp.cos(angles), jnp.sin(angles)
-    return (
-        jnp.concatenate([cos_part, cos_part], axis=-1),
-        jnp.concatenate([-sin_part, sin_part], axis=-1),
-    )
+    return jnp.concatenate([cos_part, cos_part, -sin_part, sin_part], axis=1)
 
 
 def on_device(
@@ -360,17 +374,21 @@
     scale = math.log2(math.e) / math.sqrt(HEAD_SIZE)
     stat_lanes = -(-3 * heads // LANES) * LANES
     hidden = hidden.transpose(1, 0, 2)
-    lane = jnp.arange(LANES, dtype=jnp.int32)
-    facts = jnp.where(lane < LANES // 2, suffix_length[:, None], row_adapter_index).astype(BF16)
-    base = jnp.concatenate([base_query_rows.transpose(1, 0, 2), jnp.broadcast_to(facts, (steps, rows, LANES))], axis=2)
+    lane = lax.broadcasted_iota(jnp.int32, (steps, rows, width + LANES), 2)
+    facts = jnp.where(lane < width + LANES // 2, suffix_length[:, None], row_adapter_index)
+    base = jnp.pad(base_query_rows.transpose(1, 0, 2), ((0, 0), (0, 0), (0, LANES)))
+    base = jnp.where(lane < width, base, facts.astype(BF16))
     fresh = fresh_key_value.transpose(0, 2, 1, 3)
 
     own_rows = jax.ShapeDtypeStruct((pad_rows, depth), F32)
     factors = jax.ShapeDtypeStruct(query_down_factors.shape, BF16)
-    own_ranks, own_down = call(
+    first = call(first_kernel, jax.ShapeDtypeStruct((8, LANES), F32), (), flops=1 << 34)
+    table_slots = -(-(slots + steps) // 16) * 16
+    table = rope_table(table_slots, prompt_key_value.shape[1] * seq_count)
+    own_ranks, own_down, table = call(
         own_rank_kernel,
-        (own_rows, factors),
-        (hidden, query_down_factors),
+        (own_rows, factors, jax.ShapeDtypeStruct((table_slots, 6 * LANES), BF16)),
+        (hidden, query_down_factors, table, first),
         scratch=[pltpu.VMEM((pad_rows, width), F32)],
     )
     hidden_of = [fetch(hidden, "adapter", j) for j in range(1, adapters)]
@@ -386,7 +404,6 @@
         jax.ShapeDtypeStruct(query_up_factors.shape, BF16),
         (query_up_factors, ranks),
     )
-    first_position = prompt_key_value.shape[1] * seq_count
     block_queries = []
     for j in reversed(range(adapters)):
         block_base = fetch(base, "adapter", j) if j else base
@@ -399,10 +416,13 @@
                     *rank_parts,
                     own_up,
                     block_base,
-                    *rope_parts(block_base[0, :, width], steps, first_position),
+                    table,
                     *block_queries[:1],
                 ),
-                scratch=[pltpu.VMEM((pad_rows, LANES), F32)],
+                scratch=[
+                    pltpu.VMEM((pad_rows, LANES), F32),
+                    pltpu.VMEM((pad_rows, 2 * LANES), F32),
+                ],
             ),
         )
     arrived = [send(part, "adapter", j) for j, part in enumerate(block_queries) if j]
@@ -460,7 +480,8 @@
         fetch(output_up_factors, "adapter", j) for j in range(1, adapters)
     ]
     partials = [send(part, "seq", k) for part, k in zip(messages, order)]
-    early, partials = partials[:-2], partials[-2:]
+    last = max(seq_count - 3, 0)
+    early, partials = partials[:last] + partials[last + 1 :], partials[last : last + 1]
     if early:
         own, level = call(blend_kernel, part_shapes, (*early, own, level))
     attended, out_rank = call(

time: 41.2 us -> 38.8 us (0.942)
  local copies, waits for them, and re-layouts: 3.09 us -> 0.78 us
  waiting for transfers between devices: 7.13 us -> 8.1 us
  other arithmetic: 2.2 us -> 1.31 us
  Pallas kernels: 9.24 us -> 8.57 us
  starting transfers between devices: 18.5 us -> 19.1 us
    unnamed x16, local copies, waits for them, and re-layouts: 3.01 us -> 0.77 us
    ppermute x9, waiting for transfers between devices: 3.46 us -> 5.62 us  [fetch(): lax.ppermute(value, axis, [(peer(i, offset, size), i) for i in range(size)])]
    ppermute x4, waiting for transfers between devices: 3.67 us -> 2.48 us  [send(): lax.ppermute(value, axis, [(i, peer(i, offset, size)) for i in range(size)])]
    select_n x0 -> x1, other arithmetic: none -> 1.04 us  [on_device(): base = jnp.where(lane < width, base, facts.astype(BF16))]
    concatenate x3 -> x1, other arithmetic: 1.12 us -> 0.09 us  [rope_table(): return jnp.concatenate([cos_part, cos_part, -sin_part, sin_part], axis=1)]
    ppermute x4, starting transfers between devices: 6.97 us -> 7.93 us  [send(): lax.ppermute(value, axis, [(i, peer(i, offset, size)) for i in range(size)])]
    convert_element_type x3 -> x1, other arithmetic: 0.77 us -> 0.01 us  [rope_table(): position = (first_position + jnp.arange(slots, dtype=jnp.int32)).astype(F32)]
    pallas_call x13 -> x14, Pallas kernels: 9.24 us -> 8.57 us  [call(): pl.pallas_call(kernel, out_shape=out_shape, in_specs=specs or [VMEM] * le...]
  transfers between devices with their start and end apart: 13 -> 13, of which waited for: 5 -> 8; matrix products, arithmetic and copies ran while one was open for 6% -> 3% of each run, Pallas kernels for 19% -> 19%
where the time goes in v4:
time: 38.8 us; the launch traced here: 38.7 us
  starting transfers between devices  19.1 us (49%)
  Pallas kernels  8.57 us (22%)
  waiting for transfers between devices  8.1 us (21%)
  other arithmetic  1.31 us (3%)
  between operations  0.81 us (2%)
  local copies, waits for them, and re-layouts  0.78 us (2%)
    ppermute x9, starting transfers between devices, fetch(): lax.ppermute(value, axis, [(peer(i, offset, size), i) for i in range(size)])  11.2 us
    pallas_call x14, Pallas kernels, call(): pl.pallas_call(kernel, out_shape=out_shape, in_specs=specs or [VMEM] * le...  8.57 us
    ppermute x4, starting transfers between devices, send(): lax.ppermute(value, axis, [(i, peer(i, offset, size)) for i in range(size)])  7.93 us
    ppermute x9, waiting for transfers between devices, fetch(): lax.ppermute(value, axis, [(peer(i, offset, size), i) for i in range(size)])  5.62 us
    ppermute x4, waiting for transfers between devices, send(): lax.ppermute(value, axis, [(i, peer(i, offset, size)) for i in range(size)])  2.48 us
    select_n x1, other arithmetic, on_device(): base = jnp.where(lane < width, base, facts.astype(BF16))  1.04 us
  transfers between devices with their start and end apart: 13, of which 8 were waited for; matrix products, arithmetic and copies ran while one was open for 3% of the time, Pallas kernels for 19%

profile of v4, /device:TPU:0, one launch (start us, length us, event | category | flops | bytes accessed | tf_op | source)
XLA Modules:
  0.0 38.7 jit_solution(4556539498750016010)
XLA Ops:
  0.6 3.0 %collective-permute-start = (bf16[3,4,4096]{2,1,0:T(4,128)(2,1)}, bf16[3,4,4096]{2,1,0:T(4,128)(2,1)S(1)}, u32[]{:S(2)}, u32[]{:S(2)}) collective-permute-start(bf16[3,4,4096]{2,1,0:T(4,128)(2,1)} %bitcast.8), channel_id=1, source_target_pairs={{2,0},{0,2},{3,1},{1,3},{6,4},{4,6},{7,5},{5,7},{10,8},{8,10},{11,... | collective-permute-start | bytes 294920 | tf_op jit(solution)/shard_map/ppermute | solution.py:30
  3.6 1.0 %fusion.refs_3_.refs_2_ = bf16[3,4,4224]{2,1,0:T(4,128)(2,1)S(1)} fusion(s32[4]{0:T(128)} %bitcast.13, s32[4]{0:T(128)} %param.15, bf16[3,4,4096]{2,1,0:T(4,128)(2,1)} %bitcast.12, pred[4224]{0:T(1024)(128)(4,1)S(1)} %get-tuple-element.33, pred[4224]{0:T(1024)(128)(4,1)S(1)} %get-tuple-element.34), kind=kLoop, calls=%fused_computation.1 | loop fusion | flops 152064 | bytes 208160 | tf_op jit(solution)/shard_map/jit(_where)/select_n | solution.py:380
  4.7 0.1 collective-permute-start.2
  4.8 0.2 multiply_cosine_fusion
  5.1 0.7 %copy-done.1 = bf16[1,64,4096]{2,1,0:T(8,128)(2,1)S(1)} copy-done((bf16[1,64,4096]{2,1,0:T(8,128)(2,1)S(1)}, bf16[1,64,4096]{2,1,0:T(8,128)(2,1)}, u32[]{:S(2)}) %copy-start.1) | copy-done | bytes 524312
  5.9 0.3 shard_map.126
  6.1 1.0 %collective-permute-done.refs_0_ = bf16[3,4,4096]{2,1,0:T(4,128)(2,1)S(1)} collective-permute-done((bf16[3,4,4096]{2,1,0:T(4,128)(2,1)}, bf16[3,4,4096]{2,1,0:T(4,128)(2,1)S(1)}, u32[]{:S(2)}, u32[]{:S(2)}) %collective-permute-start) | collective-permute-done | bytes 98336 | tf_op jit(solution)/shard_map/ppermute | solution.py:30
  7.1 0.3 shard_map.127._.refs_0_
  7.4 2.0 %collective-permute-done.2.refs_3_ = bf16[3,4,4224]{2,1,0:T(4,128)(2,1)S(1)} collective-permute-done((bf16[3,4,4224]{2,1,0:T(4,128)(2,1)S(1)}, bf16[3,4,4224]{2,1,0:T(4,128)(2,1)S(1)}, u32[]{:S(2)}, u32[]{:S(2)}) %collective-permute-start.2) | collective-permute-done | bytes 101408 | tf_op jit(solution)/shard_map/ppermute | solution.py:30
  9.4 0.4 shard_map.129.refs_5_
  9.8 1.6 %collective-permute-start.3 = (bf16[3,4,4096]{2,1,0:T(4,128)(2,1)S(1)}, bf16[3,4,4096]{2,1,0:T(4,128)(2,1)S(1)}, u32[]{:S(2)}, u32[]{:S(2)}) collective-permute-start(bf16[3,4,4096]{2,1,0:T(4,128)(2,1)S(1)} %shard_map.129.refs_5_), channel_id=1, source_target_pairs={{0,2},{2,0},{1,3},{3,1},{4,6},{6,4},{5,7},{7,5},{8,10},{10,8},{9,1... | collective-permute-start | bytes 294920 | tf_op jit(solution)/shard_map/ppermute | solution.py:35
  11.4 0.4 shard_map.130.refs_0_
  11.8 0.6 %collective-permute-start.10 = (bf16[1,64,4096]{2,1,0:T(8,128)(2,1)S(1)}, bf16[1,64,4096]{2,1,0:T(8,128)(2,1)S(1)}, u32[]{:S(2)}, u32[]{:S(2)}) collective-permute-start(bf16[1,64,4096]{2,1,0:T(8,128)(2,1)S(1)} %copy-done.3), channel_id=1, source_target_pairs={{2,0},{0,2},{3,1},{1,3},{6,4},{4,6},{7,5},{5,7},{10,8},{8,10},{11,... | collective-permute-start | bytes 1572872 | tf_op jit(solution)/shard_map/ppermute | solution.py:30
  12.4 1.5 %collective-permute-start.12 = (bf16[1,64,4096]{2,1,0:T(8,128)(2,1)S(1)}, bf16[1,64,4096]{2,1,0:T(8,128)(2,1)S(1)}, u32[]{:S(2)}, u32[]{:S(2)}) collective-permute-start(bf16[1,64,4096]{2,1,0:T(8,128)(2,1)S(1)} %copy-done.4), channel_id=1, source_target_pairs={{2,0},{0,2},{3,1},{1,3},{6,4},{4,6},{7,5},{5,7},{10,8},{8,10},{11,... | collective-permute-start | bytes 1572872 | tf_op jit(solution)/shard_map/ppermute | solution.py:30
  13.9 0.8 %collective-permute-done.3.refs_1_ = bf16[3,4,4096]{2,1,0:T(4,128)(2,1)S(1)} collective-permute-done((bf16[3,4,4096]{2,1,0:T(4,128)(2,1)S(1)}, bf16[3,4,4096]{2,1,0:T(4,128)(2,1)S(1)}, u32[]{:S(2)}, u32[]{:S(2)}) %collective-permute-start.3) | collective-permute-done | bytes 98336 | tf_op jit(solution)/shard_map/ppermute | solution.py:35
  14.7 0.1 shard_map.131
  14.8 2.7 %collective-permute-start.4 = (bf16[3,4,4096]{2,1,0:T(4,128)(2,1)S(1)}, bf16[3,4,4096]{2,1,0:T(4,128)(2,1)S(1)}, u32[]{:S(2)}, u32[]{:S(2)}) collective-permute-start(bf16[3,4,4096]{2,1,0:T(4,128)(2,1)S(1)} %get-tuple-element.20.query_ref), channel_id=1, source_target_pairs={{8,0},{12,4},{0,8},{4,12},{9,1},{13,5},{1,9},{5,13},{10,2},{14,6},... | collective-permute-start | bytes 294920 | tf_op jit(solution)/shard_map/ppermute | solution.py:30
  17.5 1.6 %collective-permute-start.8 = (bf16[3,4,4096]{2,1,0:T(4,128)(2,1)S(1)}, bf16[3,4,4096]{2,1,0:T(4,128)(2,1)S(1)}, u32[]{:S(2)}, u32[]{:S(2)}) collective-permute-start(bf16[3,4,4096]{2,1,0:T(4,128)(2,1)S(1)} %get-tuple-element.20.query_ref), channel_id=1, source_target_pairs={{4,0},{0,4},{12,8},{8,12},{5,1},{1,5},{13,9},{9,13},{6,2},{2,6},{1... | collective-permute-start | bytes 294920 | tf_op jit(solution)/shard_map/ppermute | solution.py:30
  19.0 1.5 %collective-permute-done.4.query_ref = bf16[3,4,4096]{2,1,0:T(4,128)(2,1)S(1)} collective-permute-done((bf16[3,4,4096]{2,1,0:T(4,128)(2,1)S(1)}, bf16[3,4,4096]{2,1,0:T(4,128)(2,1)S(1)}, u32[]{:S(2)}, u32[]{:S(2)}) %collective-permute-start.4) | collective-permute-done | bytes 98336 | tf_op jit(solution)/shard_map/ppermute | solution.py:30
  20.5 1.7 %collective-permute-start.5 = (bf16[3,4,4096]{2,1,0:T(4,128)(2,1)S(1)}, bf16[3,4,4096]{2,1,0:T(4,128)(2,1)S(1)}, u32[]{:S(2)}, u32[]{:S(2)}) collective-permute-start(bf16[3,4,4096]{2,1,0:T(4,128)(2,1)S(1)} %collective-permute-done.4.query_ref), channel_id=1, source_target_pairs={{4,0},{0,4},{12,8},{8,12},{5,1},{1,5},{13,9},{9,13},{6,2},{2,6},{1... | collective-permute-start | bytes 294920 | tf_op jit(solution)/shard_map/ppermute | solution.py:30
  22.2 1.0 %shard_map.133 = bf16[3,4,4224]{2,1,0:T(4,128)(2,1)S(1)} custom-call(bf16[3,4,4096]{2,1,0:T(4,128)(2,1)S(1)} %collective-permute-done.4.query_ref, bf16[2,1024,512]{2,1,0:T(8,128)(2,1)S(1)} %copy-done), custom_call_target="tpu_custom_call" | custom-call | flops 1048576 | bytes 1048576 | tf_op jit(solution)/shard_map/pallas_call | solution.py:43
  23.2 3.4 %collective-permute-start.7 = (bf16[3,4,4224]{2,1,0:T(4,128)(2,1)S(1)}, bf16[3,4,4224]{2,1,0:T(4,128)(2,1)S(1)}, u32[]{:S(2)}, u32[]{:S(2)}) collective-permute-start(bf16[3,4,4224]{2,1,0:T(4,128)(2,1)S(1)} %shard_map.133), channel_id=1, source_target_pairs={{0,8},{4,12},{8,0},{12,4},{1,9},{5,13},{9,1},{13,5},{2,10},{6,14},... | collective-permute-start | bytes 304136 | tf_op jit(solution)/shard_map/ppermute | solution.py:35
  26.7 1.0 %shard_map.134 = bf16[3,4,4224]{2,1,0:T(4,128)(2,1)S(1)} custom-call(bf16[3,4,4096]{2,1,0:T(4,128)(2,1)S(1)} %collective-permute-done.8.query_ref, bf16[2,1024,512]{2,1,0:T(8,128)(2,1)S(1)} %copy-done), custom_call_target="tpu_custom_call" | custom-call | flops 1048576 | bytes 1048576 | tf_op jit(solution)/shard_map/pallas_call | solution.py:43
  27.7 1.0 %shard_map.132 = bf16[3,4,4224]{2,1,0:T(4,128)(2,1)S(1)} custom-call(bf16[3,4,4096]{2,1,0:T(4,128)(2,1)S(1)} %collective-permute-done.5.query_ref, bf16[2,1024,512]{2,1,0:T(8,128)(2,1)S(1)} %copy-done), custom_call_target="tpu_custom_call" | custom-call | flops 1048576 | bytes 1048576 | tf_op jit(solution)/shard_map/pallas_call | solution.py:43
  28.8 2.9 %collective-permute-start.6 = (bf16[3,4,4224]{2,1,0:T(4,128)(2,1)S(1)}, bf16[3,4,4224]{2,1,0:T(4,128)(2,1)S(1)}, u32[]{:S(2)}, u32[]{:S(2)}) collective-permute-start(bf16[3,4,4224]{2,1,0:T(4,128)(2,1)S(1)} %shard_map.132), channel_id=1, source_target_pairs={{0,12},{4,8},{8,4},{12,0},{1,13},{5,9},{9,5},{13,1},{2,14},{6,10},... | collective-permute-start | bytes 304136 | tf_op jit(solution)/shard_map/ppermute | solution.py:35
  31.7 1.1 %shard_map.135 = (f32[3,4,4096]{2,1,0:T(4,128)S(1)}, f32[3,4,128]{2,1,0:T(4,128)S(1)}) custom-call(bf16[3,4,4096]{2,1,0:T(4,128)(2,1)S(1)} %get-tuple-element.20.query_ref, bf16[2,1024,512]{2,1,0:T(8,128)(2,1)S(1)} %copy-done, bf16[2,4,32,512]{3,2,1,0:T(8,128)(2,1)S(1)} %copy-done.5, bf16[2,3,4,512]{3,2,1,0:T(4,128)(2,1)S(1)} %bitcast.10, ...), custom_call_target="tpu_custom_call" | custom-call | flops 1048576 | bytes 1048576 | tf_op jit(solution)/shard_map/pallas_call | solution.py:43
  32.9 0.8 %shard_map.136 = (f32[3,4,4096]{2,1,0:T(4,128)S(1)}, f32[3,4,128]{2,1,0:T(4,128)S(1)}) custom-call(bf16[3,4,4224]{2,1,0:T(4,128)(2,1)S(1)} %collective-permute-done.7.refs_0_, bf16[3,4,4224]{2,1,0:T(4,128)(2,1)S(1)} %collective-permute-done.9.refs_1_, f32[3,4,4096]{2,1,0:T(4,128)S(1)} %get-tuple-element.22.refs_2_, f32[3,4,128]{2,1,0:T(4,128)S(1)} %get-tuple-element.23.refs_3_), custom_call_target="tpu_custom_call" | custom-call | flops 1048576 | bytes 1048576 | tf_op jit(solution)/shard_map/pallas_call | solution.py:43
  33.7 1.6 %collective-permute-done.6.refs_0_ = bf16[3,4,4224]{2,1,0:T(4,128)(2,1)S(1)} collective-permute-done((bf16[3,4,4224]{2,1,0:T(4,128)(2,1)S(1)}, bf16[3,4,4224]{2,1,0:T(4,128)(2,1)S(1)}, u32[]{:S(2)}, u32[]{:S(2)}) %collective-permute-start.6) | collective-permute-done | bytes 101408 | tf_op jit(solution)/shard_map/ppermute | solution.py:35
  35.3 1.2 %shard_map.137 = (bf16[3,4,4096]{2,1,0:T(4,128)(2,1)}, f32[16,128]{1,0:T(8,128)S(1)}) custom-call(bf16[3,4,4224]{2,1,0:T(4,128)(2,1)S(1)} %collective-permute-done.6.refs_0_, f32[3,4,4096]{2,1,0:T(4,128)S(1)} %get-tuple-element.24.refs_1_, f32[3,4,128]{2,1,0:T(4,128)S(1)} %get-tuple-element.25.refs_2_, bf16[1,64,4096]{2,1,0:T(8,128)(2,1)S(1)} %copy-done.3, ...), custom_call_target="tpu_custom_call" | custom-call | flops 1048576 | bytes 1048576 | tf_op jit(solution)/shard_map/pallas_call | solution.py:43
  36.6 0.4 collective-permute-done.12.refs_3_
  37.0 0.8 %collective-permute-done.11.refs_1_ = f32[16,128]{1,0:T(8,128)S(1)} collective-permute-done((f32[16,128]{1,0:T(8,128)S(1)}, f32[16,128]{1,0:T(8,128)S(1)}, u32[]{:S(2)}, u32[]{:S(2)}) %collective-permute-start.11) | collective-permute-done | bytes 8224 | tf_op jit(solution)/shard_map/ppermute | solution.py:30
  37.8 0.9 %shard_map.138 = bf16[3,4,4096]{2,1,0:T(4,128)(2,1)} custom-call(f32[16,128]{1,0:T(8,128)S(1)} %get-tuple-element.28.refs_0_, f32[16,128]{1,0:T(8,128)S(1)} %collective-permute-done.11.refs_1_, bf16[1,64,4096]{2,1,0:T(8,128)(2,1)S(1)} %copy-done.4, bf16[1,64,4096]{2,1,0:T(8,128)(2,1)S(1)} %collective-permute-done.12.refs_3_), custom_call_target="tpu_custom_call" | custom-call | flops 1048576 | bytes 1048576 | tf_op jit(solution)/shard_map/pallas_call | solution.py:43
  (31 shorter events, 0.4 us)
Async XLA Ops:
  0.6 6.5 %collective-permute-start = (bf16[3,4,4096]{2,1,0:T(4,128)(2,1)}, bf16[3,4,4096]{2,1,0:T(4,128)(2,1)S(1)}, u32[]{:S(2)}, u32[]{:S(2)}) collective-permute-start(bf16[3,4,4096]{2,1,0:T(4,128)(2,1)} %bitcast.8), channel_id=1, source_target_pairs={{2,0},{0,2},{3,1},{1,3},{6,4},{4,6},{7,5},{5,7},{10,8},{8,10},{11,... | collective-permute-start | bytes 294920 | tf_op jit(solution)/shard_map/ppermute | solution.py:30
  4.7 4.7 %collective-permute-start.2 = (bf16[3,4,4224]{2,1,0:T(4,128)(2,1)S(1)}, bf16[3,4,4224]{2,1,0:T(4,128)(2,1)S(1)}, u32[]{:S(2)}, u32[]{:S(2)}) collective-permute-start(bf16[3,4,4224]{2,1,0:T(4,128)(2,1)S(1)} %fusion.refs_3_.refs_2_), channel_id=1, source_target_pairs={{2,0},{0,2},{3,1},{1,3},{6,4},{4,6},{7,5},{5,7},{10,8},{8,10},{11,... | collective-permute-start | bytes 304136 | tf_op jit(solution)/shard_map/ppermute | solution.py:30
  4.8 1.0 %copy-start.1 = (bf16[1,64,4096]{2,1,0:T(8,128)(2,1)S(1)}, bf16[1,64,4096]{2,1,0:T(8,128)(2,1)}, u32[]{:S(2)}) copy-start(bf16[1,64,4096]{2,1,0:T(8,128)(2,1)} %down_ref.1) | copy-start | bytes 1572868
  4.8 1.0 %copy-start.6 = (bf16[4,3,4096]{2,0,1:T(4,128)(2,1)S(1)}, bf16[4,3,4096]{2,0,1:T(4,128)(2,1)}, u32[]{:S(2)}) copy-start(bf16[4,3,4096]{2,0,1:T(4,128)(2,1)} %param.11) | copy-start | bytes 294916
  4.8 2.5 %copy-start.2 = (bf16[1,64,4096]{2,1,0:T(8,128)(2,1)S(1)}, bf16[1,64,4096]{2,1,0:T(8,128)(2,1)}, u32[]{:S(2)}) copy-start(bf16[1,64,4096]{2,1,0:T(8,128)(2,1)} %in_ref.1) | copy-start | bytes 1572868
  5.8 5.9 %copy-start.3 = (bf16[1,64,4096]{2,1,0:T(8,128)(2,1)S(1)}, bf16[1,64,4096]{2,1,0:T(8,128)(2,1)}, u32[]{:S(2)}) copy-start(bf16[1,64,4096]{2,1,0:T(8,128)(2,1)} %refs_3_) | copy-start | bytes 1572868
  5.8 6.5 %copy-start.4 = (bf16[1,64,4096]{2,1,0:T(8,128)(2,1)S(1)}, bf16[1,64,4096]{2,1,0:T(8,128)(2,1)}, u32[]{:S(2)}) copy-start(bf16[1,64,4096]{2,1,0:T(8,128)(2,1)} %refs_2_) | copy-start | bytes 1572868
  7.3 2.1 %collective-permute-start.1 = (f32[32,64]{1,0:T(8,128)S(1)}, f32[32,64]{1,0:T(8,128)S(1)}, u32[]{:S(2)}, u32[]{:S(2)}) collective-permute-start(f32[32,64]{1,0:T(8,128)S(1)} %shard_map.127._.refs_0_), channel_id=1, source_target_pairs={{1,0},{0,1},{3,2},{2,3},{5,4},{4,5},{7,6},{6,7},{9,8},{8,9},{11,10... | collective-permute-start | bytes 24584 | tf_op jit(solution)/shard_map/ppermute | solution.py:30
  9.8 4.9 %collective-permute-start.3 = (bf16[3,4,4096]{2,1,0:T(4,128)(2,1)S(1)}, bf16[3,4,4096]{2,1,0:T(4,128)(2,1)S(1)}, u32[]{:S(2)}, u32[]{:S(2)}) collective-permute-start(bf16[3,4,4096]{2,1,0:T(4,128)(2,1)S(1)} %shard_map.129.refs_5_), channel_id=1, source_target_pairs={{0,2},{2,0},{1,3},{3,1},{4,6},{6,4},{5,7},{7,5},{8,10},{10,8},{9,1... | collective-permute-start | bytes 294920 | tf_op jit(solution)/shard_map/ppermute | solution.py:35
  11.8 10.4 %copy-start = (bf16[2,1024,512]{2,1,0:T(8,128)(2,1)S(1)}, bf16[2,1024,512]{2,1,0:T(8,128)(2,1)}, u32[]{:S(2)}) copy-start(bf16[2,1024,512]{2,1,0:T(8,128)(2,1)} %kv_ref.7) | copy-start | bytes 6291460
  11.8 23.5 %collective-permute-start.10 = (bf16[1,64,4096]{2,1,0:T(8,128)(2,1)S(1)}, bf16[1,64,4096]{2,1,0:T(8,128)(2,1)S(1)}, u32[]{:S(2)}, u32[]{:S(2)}) collective-permute-start(bf16[1,64,4096]{2,1,0:T(8,128)(2,1)S(1)} %copy-done.3), channel_id=1, source_target_pairs={{2,0},{0,2},{3,1},{1,3},{6,4},{4,6},{7,5},{5,7},{10,8},{8,10},{11,... | collective-permute-start | bytes 1572872 | tf_op jit(solution)/shard_map/ppermute | solution.py:30
  12.4 24.6 %collective-permute-start.12 = (bf16[1,64,4096]{2,1,0:T(8,128)(2,1)S(1)}, bf16[1,64,4096]{2,1,0:T(8,128)(2,1)S(1)}, u32[]{:S(2)}, u32[]{:S(2)}) collective-permute-start(bf16[1,64,4096]{2,1,0:T(8,128)(2,1)S(1)} %copy-done.4), channel_id=1, source_target_pairs={{2,0},{0,2},{3,1},{1,3},{6,4},{4,6},{7,5},{5,7},{10,8},{8,10},{11,... | collective-permute-start | bytes 1572872 | tf_op jit(solution)/shard_map/ppermute | solution.py:30
  14.8 5.7 %collective-permute-start.4 = (bf16[3,4,4096]{2,1,0:T(4,128)(2,1)S(1)}, bf16[3,4,4096]{2,1,0:T(4,128)(2,1)S(1)}, u32[]{:S(2)}, u32[]{:S(2)}) collective-permute-start(bf16[3,4,4096]{2,1,0:T(4,128)(2,1)S(1)} %get-tuple-element.20.query_ref), channel_id=1, source_target_pairs={{8,0},{12,4},{0,8},{4,12},{9,1},{13,5},{1,9},{5,13},{10,2},{14,6},... | collective-permute-start | bytes 294920 | tf_op jit(solution)/shard_map/ppermute | solution.py:30
  17.5 9.2 %collective-permute-start.8 = (bf16[3,4,4096]{2,1,0:T(4,128)(2,1)S(1)}, bf16[3,4,4096]{2,1,0:T(4,128)(2,1)S(1)}, u32[]{:S(2)}, u32[]{:S(2)}) collective-permute-start(bf16[3,4,4096]{2,1,0:T(4,128)(2,1)S(1)} %get-tuple-element.20.query_ref), channel_id=1, source_target_pairs={{4,0},{0,4},{12,8},{8,12},{5,1},{1,5},{13,9},{9,13},{6,2},{2,6},{1... | collective-permute-start | bytes 294920 | tf_op jit(solution)/shard_map/ppermute | solution.py:30
  20.5 7.2 %collective-permute-start.5 = (bf16[3,4,4096]{2,1,0:T(4,128)(2,1)S(1)}, bf16[3,4,4096]{2,1,0:T(4,128)(2,1)S(1)}, u32[]{:S(2)}, u32[]{:S(2)}) collective-permute-start(bf16[3,4,4096]{2,1,0:T(4,128)(2,1)S(1)} %collective-permute-done.4.query_ref), channel_id=1, source_target_pairs={{4,0},{0,4},{12,8},{8,12},{5,1},{1,5},{13,9},{9,13},{6,2},{2,6},{1... | collective-permute-start | bytes 294920 | tf_op jit(solution)/shard_map/ppermute | solution.py:30
  23.2 8.4 %copy-start.5 = (bf16[2,4,32,512]{3,2,1,0:T(8,128)(2,1)S(1)}, bf16[2,4,32,512]{3,2,1,0:T(8,128)(2,1)}, u32[]{:S(2)}) copy-start(bf16[2,4,32,512]{3,2,1,0:T(8,128)(2,1)} %suffix_ref.1) | copy-start | bytes 786436
  23.2 8.4 %copy-start.7 = (bf16[2,4,3,512]{3,1,2,0:T(4,128)(2,1)S(1)}, bf16[2,4,3,512]{3,1,2,0:T(4,128)(2,1)}, u32[]{:S(2)}) copy-start(bf16[2,4,3,512]{3,1,2,0:T(4,128)(2,1)} %param.13) | copy-start | bytes 73732
  23.2 9.6 %collective-permute-start.7 = (bf16[3,4,4224]{2,1,0:T(4,128)(2,1)S(1)}, bf16[3,4,4224]{2,1,0:T(4,128)(2,1)S(1)}, u32[]{:S(2)}, u32[]{:S(2)}) collective-permute-start(bf16[3,4,4224]{2,1,0:T(4,128)(2,1)S(1)} %shard_map.133), channel_id=1, source_target_pairs={{0,8},{4,12},{8,0},{12,4},{1,9},{5,13},{9,1},{13,5},{2,10},{6,14},... | collective-permute-start | bytes 304136 | tf_op jit(solution)/shard_map/ppermute | solution.py:35
  27.7 5.2 %collective-permute-start.9 = (bf16[3,4,4224]{2,1,0:T(4,128)(2,1)S(1)}, bf16[3,4,4224]{2,1,0:T(4,128)(2,1)S(1)}, u32[]{:S(2)}, u32[]{:S(2)}) collective-permute-start(bf16[3,4,4224]{2,1,0:T(4,128)(2,1)S(1)} %shard_map.134), channel_id=1, source_target_pairs={{0,4},{4,0},{8,12},{12,8},{1,5},{5,1},{9,13},{13,9},{2,6},{6,2},{1... | collective-permute-start | bytes 304136 | tf_op jit(solution)/shard_map/ppermute | solution.py:35
  28.8 6.6 %collective-permute-start.6 = (bf16[3,4,4224]{2,1,0:T(4,128)(2,1)S(1)}, bf16[3,4,4224]{2,1,0:T(4,128)(2,1)S(1)}, u32[]{:S(2)}, u32[]{:S(2)}) collective-permute-start(bf16[3,4,4224]{2,1,0:T(4,128)(2,1)S(1)} %shard_map.132), channel_id=1, source_target_pairs={{0,12},{4,8},{8,4},{12,0},{1,13},{5,9},{9,5},{13,1},{2,14},{6,10},... | collective-permute-start | bytes 304136 | tf_op jit(solution)/shard_map/ppermute | solution.py:35
  36.5 1.2 %collective-permute-start.11 = (f32[16,128]{1,0:T(8,128)S(1)}, f32[16,128]{1,0:T(8,128)S(1)}, u32[]{:S(2)}, u32[]{:S(2)}) collective-permute-start(f32[16,128]{1,0:T(8,128)S(1)} %get-tuple-element.28.refs_0_), channel_id=1, source_target_pairs={{1,0},{0,1},{3,2},{2,3},{5,4},{4,5},{7,6},{6,7},{9,8},{8,9},{11,10... | collective-permute-start | bytes 24584 | tf_op jit(solution)/shard_map/ppermute | solution.py:30

commit v5 on v4

--- a/solution.py
+++ b/solution.py
@@ -33,6 +33,10 @@
 def send(value, axis, offset):
     size = lax.axis_size(axis)
     return lax.ppermute(value, axis, [(i, peer(i, offset, size)) for i in range(size)])
+
+
+def padded(tokens):
+    return -(-tokens // 16) * 16
 
 
 def dot(left, right, contract):
@@ -91,51 +95,69 @@
     out_ref[...] = in_ref[...]
 
 
-def query_kernel(parts, block, *refs):
+def total_ranks(rank_refs, block, pad_rows):
+    parts = [ref[block * pad_rows : (block + 1) * pad_rows, :] for ref in rank_refs]
+    return functools.reduce(jnp.add, parts).astype(BF16)
+
+
+def correction_kernel(parts, block, *refs):
+    up_ref = refs[parts]
+    out_ref = refs[-1]
+    resident, rank, _ = up_ref.shape
+    _, steps, rows, _ = out_ref.shape
+    ranks = total_ranks(refs[:parts], block, padded(steps * rows))
+    for u in range(resident):
+        result = dot(ranks[:, u * rank : (u + 1) * rank], up_ref[u], ((1,), (0,)))
+        for t in range(steps):
+            out_ref[u, t] = result[t * rows : (t + 1) * rows].astype(BF16)
+
+
+def prepare_kernel(parts, *refs):
     rank_refs = refs[:parts]
-    up_ref, base_ref, table_ref = refs[parts : parts + 3]
-    out_ref, facts_ref, angles_ref = refs[-3:]
+    up_ref, base_ref, facts_ref, table_ref = refs[parts : parts + 4]
+    sum_ref, angles_ref, token_ref, column_ref = refs[-4:]
     resident, rank, _ = up_ref.shape
-    steps, rows, width = out_ref.shape
-    pad_rows = facts_ref.shape[0]
-    facts_ref[...] = jnp.zeros_like(facts_ref)
-    for t in range(steps):
-        facts_ref[t * rows : (t + 1) * rows, :] = base_ref[t, :, width:].astype(F32)
-    ids = facts_ref[:, LANES // 2 : LANES // 2 + 1].astype(jnp.int32)
+    steps, rows, width = base_ref.shape
+    pad_rows = column_ref.shape[0]
+    column_ref[...] = jnp.zeros_like(column_ref)
+    for t in range(steps):
+        column_ref[t * rows : (t + 1) * rows, :] = facts_ref[...]
+    ids = column_ref[:, LANES // 2 : LANES // 2 + 1]
     shape = (pad_rows, table_ref.shape[0])
     step = lax.broadcasted_iota(jnp.int32, shape, 0) // rows
-    place = (lax.broadcasted_iota(jnp.int32, shape, 1) - step).astype(F32)
-    picked = (place == facts_ref[:, 0:1]).astype(F32).astype(BF16)
+    place = lax.broadcasted_iota(jnp.int32, shape, 1) - step
+    picked = (place == column_ref[:, 0:1]).astype(F32).astype(BF16)
     found = dot(picked, table_ref[...], ((1,), (0,)))
     angles_ref[...] = found[:, : 2 * LANES] + found[:, 2 * LANES : 4 * LANES] + found[:, 4 * LANES :]
-    ranks = functools.reduce(
-        jnp.add, [ref[block * pad_rows : (block + 1) * pad_rows, :] for ref in rank_refs]
-    )
+    ranks = total_ranks(rank_refs, 0, pad_rows)
     lane = lax.broadcasted_iota(jnp.int32, ranks.shape, 1)
     owner = lax.axis_index("adapter") * resident + lane // rank
-    chosen = jnp.where(owner == ids, ranks, 0.0).astype(BF16)
+    chosen = jnp.where(owner == ids, ranks.astype(F32), 0.0).astype(BF16)
     correction = dot(chosen, up_ref[...].reshape(resident * rank, width), ((1,), (0,)))
+    for t in range(steps):
+        sum_ref[t] = base_ref[t].astype(F32) + correction[t * rows : (t + 1) * rows]
+    token_ref[...] = jnp.zeros_like(token_ref)
+
+
+def rotate_kernel(others, *refs):
+    corrections = refs[:others]
+    sum_ref, angles_ref, facts_ref, _, out_ref = refs[others:]
+    steps, rows, width = sum_ref.shape
+    x = lax.axis_index("adapter")
+    ids = facts_ref[:, LANES // 2 : LANES // 2 + 1]
     for t in range(steps):
         cos_part = angles_ref[t * rows : (t + 1) * rows, :LANES]
         sin_part = angles_ref[t * rows : (t + 1) * rows, LANES:]
         for h in range(width // HEAD_SIZE):
             at = slice(h * HEAD_SIZE, (h + 1) * HEAD_SIZE)
-            piece = base_ref[t, :, at].astype(F32) + correction[t * rows : (t + 1) * rows, at]
+            piece = sum_ref[t, :, at]
+            for j, ref in enumerate(corrections):
+                resident = ref.shape[0]
+                for u in range(resident):
+                    owner = peer(x, j + 1, others + 1) * resident + u
+                    piece += jnp.where(ids == owner, ref[u, t, :, at].astype(F32), 0.0)
             turned = piece * cos_part + pltpu.roll(piece, HEAD_SIZE // 2, 1) * sin_part
             out_ref[t, :, at] = turned.astype(BF16)
-
-
-def pick_kernel(adapters, resident, *refs):
-    queries = refs[:adapters]
-    base_ref, _, out_ref, meta_ref = refs[adapters:]
-    meta_ref[...] = base_ref[0, :, out_ref.shape[2] :].astype(F32).astype(jnp.int32)
-    owner = meta_ref[:, LANES // 2 : LANES // 2 + 1] // resident
-    x = lax.axis_index("adapter")
-    for t in range(out_ref.shape[0]):
-        picked = queries[0][t].astype(F32)
-        for j in range(1, adapters):
-            picked = jnp.where(owner == peer(x, j, adapters), queries[j][t].astype(F32), picked)
-        out_ref[t] = picked.astype(BF16)
 
 
 def load_queries(query_ref, rows_ref):
@@ -267,41 +289,49 @@
     )
 
 
-def mix(own_ref, level_ref, arrived, t, store):
-    width = own_ref.shape[2]
+def mix(own_ref, level_ref, arrived, store, finish=None):
+    steps, _, width = own_ref.shape
     heads = width // HEAD_SIZE
-    levels = [level_ref[t]]
-    for ref in arrived:
-        levels.append(message_levels(ref[t, :, width:].astype(F32), heads))
-    highest = functools.reduce(jnp.maximum, levels)
-    shares = [jnp.exp2(level - highest) for level in levels]
-    total = functools.reduce(jnp.add, shares)
-    shares = [share / total for share in shares]
+    shares, levels = [], []
+    for t in range(steps):
+        parts = [level_ref[t]]
+        for ref in arrived:
+            parts.append(message_levels(ref[t, :, width:].astype(F32), heads))
+        highest = functools.reduce(jnp.maximum, parts)
+        weights = [jnp.exp2(part - highest) for part in parts]
+        total = functools.reduce(jnp.add, weights)
+        inverse = 1.0 / total
+        shares.append([weight * inverse for weight in weights])
+        levels.append(highest + jnp.log2(total))
+    quarter = heads // 4 if heads % 4 == 0 else heads
     for h in range(heads):
         at = slice(h * HEAD_SIZE, (h + 1) * HEAD_SIZE)
-        mixed = own_ref[t, :, at] * shares[0][:, h : h + 1]
-        for ref, share in zip(arrived, shares[1:]):
-            mixed += ref[t, :, at].astype(F32) * share[:, h : h + 1]
-        store(at, mixed)
-    return highest + jnp.log2(total)
+        for t in range(steps):
+            mixed = own_ref[t, :, at] * shares[t][0][:, h : h + 1]
+            for ref, share in zip(arrived, shares[t][1:]):
+                mixed += ref[t, :, at].astype(F32) * share[:, h : h + 1]
+            store(t, at, mixed)
+        if finish and (h + 1) % quarter == 0:
+            finish(slice((h + 1 - quarter) * HEAD_SIZE, (h + 1) * HEAD_SIZE))
+    return levels
 
 
 def blend_kernel(*refs):
     arrived = refs[:-4]
     own_ref, level_ref, out_ref, out_level_ref = refs[-4:]
-    for t in range(own_ref.shape[0]):
-
-        def store(at, mixed):
-            out_ref[t, :, at] = mixed
-
-        out_level_ref[t] = mix(own_ref, level_ref, arrived, t, store)
+
+    def store(t, at, mixed):
+        out_ref[t, :, at] = mixed
+
+    for t, level in enumerate(mix(own_ref, level_ref, arrived, store)):
+        out_level_ref[t] = level
 
 
 def merge_kernel(messages, adapters, *refs):
     arrived = refs[:messages]
     own_ref, level_ref = refs[messages : messages + 2]
     downs = refs[2 + messages : 2 + messages + adapters]
-    meta_ref, out_hbm, rank_ref, rows_ref, ids_ref, out_ref, sem = refs[2 + messages + adapters :]
+    meta_ref, out_ref, rank_ref, rows_ref, ids_ref = refs[2 + messages + adapters :]
     steps, rows, _ = own_ref.shape
     resident, rank, _ = downs[0].shape
     depth = resident * rank
@@ -310,33 +340,46 @@
     ids_ref[...] = jnp.zeros_like(ids_ref)
     for t in range(steps):
         ids_ref[t * rows : (t + 1) * rows, :] = meta_ref[...]
-
-        def store(at, mixed):
-            out_ref[t, :, at] = mixed.astype(BF16)
-            rows_ref[t * rows : (t + 1) * rows, at] = mixed
-
-        mix(own_ref, level_ref, arrived, t, store)
-    copy = pltpu.make_async_copy(out_ref, out_hbm, sem)
-    copy.start()
-    factors = jnp.concatenate([down[u] for down in downs for u in range(resident)], axis=0)
-    result = dot(rows_ref[...].astype(BF16), factors, ((1,), (1,)))
+    products = []
+
+    def store(t, at, mixed):
+        out_ref[t, :, at] = mixed.astype(BF16)
+        rows_ref[t * rows : (t + 1) * rows, at] = mixed
+
+    def finish(at):
+        factors = [down[u, :, at] for down in downs for u in range(resident)]
+        products.append(
+            dot(rows_ref[:, at].astype(BF16), jnp.concatenate(factors, axis=0), ((1,), (1,)))
+        )
+
+    mix(own_ref, level_ref, arrived, store, finish)
+    result = functools.reduce(jnp.add, products)
     lane = lax.broadcasted_iota(jnp.int32, result.shape, 1)
     owner = peer(x, lane // depth, adapters) * resident + lane % depth // rank
     rank_ref[...] = jnp.where(owner == ids_ref[:, LANES // 2 : LANES // 2 + 1], result, 0.0)
-    copy.wait()
 
 
 def up_kernel(parts, adapters, *refs):
     ranks = refs[:parts]
     ups = refs[parts : parts + adapters]
-    out_ref = refs[parts + adapters]
+    attended_ref, attended_hbm, out_hbm, out_ref, sems = refs[parts + adapters :]
+    copies = [pltpu.make_async_copy(attended_ref, attended_hbm, sems.at[4])]
+    copies[0].start()
     steps, rows, width = out_ref.shape
     resident = ups[0].shape[0]
     chosen = functools.reduce(jnp.add, [ref[...] for ref in ranks]).astype(BF16)
-    factors = jnp.concatenate([up[u] for up in ups for u in range(resident)], axis=0)
-    result = dot(chosen, factors, ((1,), (0,)))
-    for t in range(steps):
-        out_ref[t] = result[t * rows : (t + 1) * rows].astype(BF16)
+    quarter = width // 4
+    for i in range(4):
+        at = slice(i * quarter, (i + 1) * quarter)
+        factors = jnp.concatenate([up[u, :, at] for up in ups for u in range(resident)], axis=0)
+        result = dot(chosen, factors, ((1,), (0,)))
+        for t in range(steps):
+            out_ref[t, :, at] = result[t * rows : (t + 1) * rows].astype(BF16)
+        copy = pltpu.make_async_copy(out_ref.at[:, :, at], out_hbm.at[:, :, at], sems.at[i])
+        copy.start()
+        copies.append(copy)
+    for copy in copies:
+        copy.wait()
 
 
 def rope_table(slots, first_position):
@@ -367,17 +410,16 @@
     resident, rank, _ = query_down_factors.shape
     depth = resident * rank
     tokens = rows * steps
-    pad_rows = -(-tokens // 16) * 16
+    pad_rows = padded(tokens)
     heads = width // HEAD_SIZE
     kv_heads = prompt_key_value.shape[2] // HEAD_SIZE
     group = heads // kv_heads
     scale = math.log2(math.e) / math.sqrt(HEAD_SIZE)
     stat_lanes = -(-3 * heads // LANES) * LANES
     hidden = hidden.transpose(1, 0, 2)
-    lane = lax.broadcasted_iota(jnp.int32, (steps, rows, width + LANES), 2)
-    facts = jnp.where(lane < width + LANES // 2, suffix_length[:, None], row_adapter_index)
-    base = jnp.pad(base_query_rows.transpose(1, 0, 2), ((0, 0), (0, 0), (0, LANES)))
-    base = jnp.where(lane < width, base, facts.astype(BF16))
+    base = base_query_rows.transpose(1, 0, 2)
+    lane = jnp.arange(LANES, dtype=jnp.int32)
+    facts = jnp.where(lane < LANES // 2, suffix_length[:, None], row_adapter_index)
     fresh = fresh_key_value.transpose(0, 2, 1, 3)
 
     own_rows = jax.ShapeDtypeStruct((pad_rows, depth), F32)
@@ -404,38 +446,32 @@
         jax.ShapeDtypeStruct(query_up_factors.shape, BF16),
         (query_up_factors, ranks),
     )
-    block_queries = []
-    for j in reversed(range(adapters)):
-        block_base = fetch(base, "adapter", j) if j else base
-        block_queries.insert(
-            0,
-            call(
-                functools.partial(query_kernel, halves, j),
-                jax.ShapeDtypeStruct((steps, rows, width), BF16),
-                (
-                    *rank_parts,
-                    own_up,
-                    block_base,
-                    table,
-                    *block_queries[:1],
-                ),
-                scratch=[
-                    pltpu.VMEM((pad_rows, LANES), F32),
-                    pltpu.VMEM((pad_rows, 2 * LANES), F32),
-                ],
-            ),
+    corrections = [
+        call(
+            functools.partial(correction_kernel, halves, j),
+            jax.ShapeDtypeStruct((resident, steps, rows, width), BF16),
+            (*rank_parts, own_up),
         )
-    arrived = [send(part, "adapter", j) for j, part in enumerate(block_queries) if j]
+        for j in range(1, adapters)
+    ]
+    arrived = [send(part, "adapter", j + 1) for j, part in enumerate(corrections)]
+    query_sum, angles, token = call(
+        functools.partial(prepare_kernel, halves),
+        (
+            jax.ShapeDtypeStruct((steps, rows, width), F32),
+            jax.ShapeDtypeStruct((pad_rows, 2 * LANES), F32),
+            jax.ShapeDtypeStruct((8, LANES), F32),
+        ),
+        (*rank_parts, own_up, base, facts, table, *corrections),
+        scratch=[pltpu.VMEM((pad_rows, LANES), jnp.int32)],
+    )
     output_down_factors, output_up_factors, token = lax.optimization_barrier(
-        (output_down_factors, output_up_factors, block_queries[0][0, :, :LANES])
-    )
-    queries, meta = call(
-        functools.partial(pick_kernel, adapters, resident),
-        (
-            jax.ShapeDtypeStruct((steps, rows, width), BF16),
-            jax.ShapeDtypeStruct((rows, LANES), jnp.int32),
-        ),
-        (block_queries[0], *arrived, base, token),
+        (output_down_factors, output_up_factors, token)
+    )
+    queries = call(
+        functools.partial(rotate_kernel, adapters - 1),
+        jax.ShapeDtypeStruct((steps, rows, width), BF16),
+        (*arrived, query_sum, angles, facts, token),
         flops=1 << 36,
     )
     message = jax.ShapeDtypeStruct((steps, rows, width + stat_lanes), BF16)
@@ -466,7 +502,7 @@
     own, level = call(
         functools.partial(near_kernel, scale),
         part_shapes,
-        (queries, prompt_key_value, suffix_key_value, fresh, meta),
+        (queries, prompt_key_value, suffix_key_value, fresh, facts),
         scratch=query_scratch
         + [
             pltpu.VMEM((2, fresh_slots, fresh.shape[3]), F32),
@@ -490,20 +526,19 @@
             jax.ShapeDtypeStruct((steps, rows, width), BF16),
             jax.ShapeDtypeStruct((pad_rows, adapters * depth), F32),
         ),
-        (*partials, own, level, *output_downs, meta),
+        (*partials, own, level, *output_downs, facts),
         scratch=[
             pltpu.VMEM((pad_rows, width), F32),
             pltpu.VMEM((pad_rows, LANES), jnp.int32),
-            pltpu.VMEM((steps, rows, width), BF16),
-            pltpu.SemaphoreType.DMA,
         ],
-        out_specs=(pl.BlockSpec(memory_space=pl.ANY), VMEM),
     )
     out_ranks = [out_rank] + [fetch(out_rank, "head", j) for j in range(1, halves)]
-    adapted = call(
+    attended, adapted = call(
         functools.partial(up_kernel, halves, adapters),
-        jax.ShapeDtypeStruct((steps, rows, width), BF16),
-        (*out_ranks, *output_ups),
+        (jax.ShapeDtypeStruct((steps, rows, width), BF16),) * 2,
+        (*out_ranks, *output_ups, attended),
+        scratch=[pltpu.VMEM((steps, rows, width), BF16), pltpu.SemaphoreType.DMA((5,))],
+        out_specs=(pl.BlockSpec(memory_space=pl.ANY),) * 2,
     )
     return attended.transpose(1, 0, 2), adapted.transpose(1, 0, 2)
 

time: 38.8 us -> 37.7 us (0.972)
  Pallas kernels: 8.57 us -> 7.55 us
  other arithmetic: 1.31 us -> 0.35 us
  starting transfers between devices: 19.1 us -> 19.7 us
    pallas_call x14, Pallas kernels: 8.57 us -> 7.55 us  [call(): pl.pallas_call(kernel, out_shape=out_shape, in_specs=specs or [VMEM] * le...]
    select_n x1, other arithmetic: 1.04 us -> 0.07 us  [on_device(): jnp.where(lane < LANES // 2, suffix_length[:, None], row_adapter_index)]
    ppermute x4, waiting for transfers between devices: 2.48 us -> 2.93 us  [send(): lax.ppermute(value, axis, [(i, peer(i, offset, size)) for i in range(size)])]
    ppermute x9 -> x8, starting transfers between devices: 11.2 us -> 11.6 us  [fetch(): lax.ppermute(value, axis, [(peer(i, offset, size), i) for i in range(size)])]
    ppermute x9 -> x8, waiting for transfers between devices: 5.62 us -> 5.38 us  [fetch(): lax.ppermute(value, axis, [(peer(i, offset, size), i) for i in range(size)])]
  transfers between devices with their start and end apart: 13 -> 12, of which waited for: 8 -> 8; matrix products, arithmetic and copies ran while one was open for 3% -> 1% of each run, Pallas kernels for 19% -> 17%
where the time goes in v5:
time: 37.7 us; the launch traced here: 37.5 us
  starting transfers between devices  19.7 us (52%)
  waiting for transfers between devices  8.32 us (22%)
  Pallas kernels  7.55 us (20%)
  between operations  0.83 us (2%)
  local copies, waits for them, and re-layouts  0.74 us (2%)
    ppermute x8, starting transfers between devices, fetch(): lax.ppermute(value, axis, [(peer(i, offset, size), i) for i in range(size)])  11.6 us
    ppermute x4, starting transfers between devices, send(): lax.ppermute(value, axis, [(i, peer(i, offset, size)) for i in range(size)])  8.15 us
    pallas_call x14, Pallas kernels, call(): pl.pallas_call(kernel, out_shape=out_shape, in_specs=specs or [VMEM] * le...  7.55 us
    ppermute x8, waiting for transfers between devices, fetch(): lax.ppermute(value, axis, [(peer(i, offset, size), i) for i in range(size)])  5.38 us
    ppermute x4, waiting for transfers between devices, send(): lax.ppermute(value, axis, [(i, peer(i, offset, size)) for i in range(size)])  2.93 us
  transfers between devices with their start and end apart: 12, of which 8 were waited for; matrix products, arithmetic and copies ran while one was open for 1% of the time, Pallas kernels for 17%

profile of v5, /device:TPU:0, one launch (start us, length us, event | category | flops | bytes accessed | tf_op | source)
XLA Modules:
  0.0 37.5 jit_solution(9894015050345311518)
XLA Ops:
  0.6 3.0 %collective-permute-start = (bf16[3,4,4096]{2,1,0:T(4,128)(2,1)}, bf16[3,4,4096]{2,1,0:T(4,128)(2,1)S(1)}, u32[]{:S(2)}, u32[]{:S(2)}) collective-permute-start(bf16[3,4,4096]{2,1,0:T(4,128)(2,1)} %bitcast.7), channel_id=1, source_target_pairs={{2,0},{0,2},{3,1},{1,3},{6,4},{4,6},{7,5},{5,7},{10,8},{8,10},{11,... | collective-permute-start | bytes 294920 | tf_op jit(solution)/shard_map/ppermute | solution.py:30
  3.8 0.2 multiply_cosine_fusion
  3.9 0.1 pad_maximum_fusion.table_ref
  4.0 0.7 %copy-done.1 = bf16[1,64,4096]{2,1,0:T(8,128)(2,1)S(1)} copy-done((bf16[1,64,4096]{2,1,0:T(8,128)(2,1)S(1)}, bf16[1,64,4096]{2,1,0:T(8,128)(2,1)}, u32[]{:S(2)}) %copy-start.1) | copy-done | bytes 524312
  4.7 0.3 shard_map.123
  5.0 1.7 %collective-permute-done.refs_0_ = bf16[3,4,4096]{2,1,0:T(4,128)(2,1)S(1)} collective-permute-done((bf16[3,4,4096]{2,1,0:T(4,128)(2,1)}, bf16[3,4,4096]{2,1,0:T(4,128)(2,1)S(1)}, u32[]{:S(2)}, u32[]{:S(2)}) %collective-permute-start) | collective-permute-done | bytes 98336 | tf_op jit(solution)/shard_map/ppermute | solution.py:30
  6.6 0.3 shard_map.124._.refs_0_
  7.0 1.1 %collective-permute-done.1.refs_1_ = f32[32,64]{1,0:T(8,128)S(1)} collective-permute-done((f32[32,64]{1,0:T(8,128)S(1)}, f32[32,64]{1,0:T(8,128)S(1)}, u32[]{:S(2)}, u32[]{:S(2)}) %collective-permute-start.1) | collective-permute-done | bytes 8224 | tf_op jit(solution)/shard_map/ppermute | solution.py:30
  8.1 0.2 shard_map.126.refs_6_
  8.3 1.9 %collective-permute-start.2 = (bf16[1,3,4,4096]{3,2,1,0:T(4,128)(2,1)S(1)}, bf16[1,3,4,4096]{3,2,1,0:T(4,128)(2,1)S(1)}, u32[]{:S(2)}, u32[]{:S(2)}) collective-permute-start(bf16[1,3,4,4096]{3,2,1,0:T(4,128)(2,1)S(1)} %shard_map.126.refs_6_), channel_id=1, source_target_pairs={{0,2},{2,0},{1,3},{3,1},{4,6},{6,4},{5,7},{7,5},{8,10},{10,8},{9,1... | collective-permute-start | bytes 294920 | tf_op jit(solution)/shard_map/ppermute | solution.py:35
  10.2 0.3 shard_map.127
  10.5 0.3 collective-permute-start.9
  10.8 1.8 %collective-permute-start.11 = (bf16[1,64,4096]{2,1,0:T(8,128)(2,1)S(1)}, bf16[1,64,4096]{2,1,0:T(8,128)(2,1)S(1)}, u32[]{:S(2)}, u32[]{:S(2)}) collective-permute-start(bf16[1,64,4096]{2,1,0:T(8,128)(2,1)S(1)} %copy-done.4), channel_id=1, source_target_pairs={{2,0},{0,2},{3,1},{1,3},{6,4},{4,6},{7,5},{5,7},{10,8},{8,10},{11,... | collective-permute-start | bytes 1572872 | tf_op jit(solution)/shard_map/ppermute | solution.py:30
  12.6 0.8 %collective-permute-done.2.refs_0_ = bf16[1,3,4,4096]{3,2,1,0:T(4,128)(2,1)S(1)} collective-permute-done((bf16[1,3,4,4096]{3,2,1,0:T(4,128)(2,1)S(1)}, bf16[1,3,4,4096]{3,2,1,0:T(4,128)(2,1)S(1)}, u32[]{:S(2)}, u32[]{:S(2)}) %collective-permute-start.2) | collective-permute-done | bytes 98336 | tf_op jit(solution)/shard_map/ppermute | solution.py:35
  13.5 0.3 shard_map.128.query_ref
  13.8 3.2 %collective-permute-start.3 = (bf16[3,4,4096]{2,1,0:T(4,128)(2,1)S(1)}, bf16[3,4,4096]{2,1,0:T(4,128)(2,1)S(1)}, u32[]{:S(2)}, u32[]{:S(2)}) collective-permute-start(bf16[3,4,4096]{2,1,0:T(4,128)(2,1)S(1)} %shard_map.128.query_ref), channel_id=1, source_target_pairs={{8,0},{12,4},{0,8},{4,12},{9,1},{13,5},{1,9},{5,13},{10,2},{14,6},... | collective-permute-start | bytes 294920 | tf_op jit(solution)/shard_map/ppermute | solution.py:30
  17.0 1.6 %collective-permute-start.7 = (bf16[3,4,4096]{2,1,0:T(4,128)(2,1)S(1)}, bf16[3,4,4096]{2,1,0:T(4,128)(2,1)S(1)}, u32[]{:S(2)}, u32[]{:S(2)}) collective-permute-start(bf16[3,4,4096]{2,1,0:T(4,128)(2,1)S(1)} %shard_map.128.query_ref), channel_id=1, source_target_pairs={{4,0},{0,4},{12,8},{8,12},{5,1},{1,5},{13,9},{9,13},{6,2},{2,6},{1... | collective-permute-start | bytes 294920 | tf_op jit(solution)/shard_map/ppermute | solution.py:30
  18.5 1.4 %collective-permute-done.3.query_ref = bf16[3,4,4096]{2,1,0:T(4,128)(2,1)S(1)} collective-permute-done((bf16[3,4,4096]{2,1,0:T(4,128)(2,1)S(1)}, bf16[3,4,4096]{2,1,0:T(4,128)(2,1)S(1)}, u32[]{:S(2)}, u32[]{:S(2)}) %collective-permute-start.3) | collective-permute-done | bytes 98336 | tf_op jit(solution)/shard_map/ppermute | solution.py:30
  19.9 1.7 %collective-permute-start.4 = (bf16[3,4,4096]{2,1,0:T(4,128)(2,1)S(1)}, bf16[3,4,4096]{2,1,0:T(4,128)(2,1)S(1)}, u32[]{:S(2)}, u32[]{:S(2)}) collective-permute-start(bf16[3,4,4096]{2,1,0:T(4,128)(2,1)S(1)} %collective-permute-done.3.query_ref), channel_id=1, source_target_pairs={{4,0},{0,4},{12,8},{8,12},{5,1},{1,5},{13,9},{9,13},{6,2},{2,6},{1... | collective-permute-start | bytes 294920 | tf_op jit(solution)/shard_map/ppermute | solution.py:30
  21.7 1.0 %shard_map.130 = bf16[3,4,4224]{2,1,0:T(4,128)(2,1)S(1)} custom-call(bf16[3,4,4096]{2,1,0:T(4,128)(2,1)S(1)} %collective-permute-done.3.query_ref, bf16[2,1024,512]{2,1,0:T(8,128)(2,1)S(1)} %copy-done), custom_call_target="tpu_custom_call" | custom-call | flops 1048576 | bytes 1048576 | tf_op jit(solution)/shard_map/pallas_call | solution.py:47
  22.7 3.4 %collective-permute-start.6 = (bf16[3,4,4224]{2,1,0:T(4,128)(2,1)S(1)}, bf16[3,4,4224]{2,1,0:T(4,128)(2,1)S(1)}, u32[]{:S(2)}, u32[]{:S(2)}) collective-permute-start(bf16[3,4,4224]{2,1,0:T(4,128)(2,1)S(1)} %shard_map.130), channel_id=1, source_target_pairs={{0,8},{4,12},{8,0},{12,4},{1,9},{5,13},{9,1},{13,5},{2,10},{6,14},... | collective-permute-start | bytes 304136 | tf_op jit(solution)/shard_map/ppermute | solution.py:35
  26.1 1.0 %shard_map.131 = bf16[3,4,4224]{2,1,0:T(4,128)(2,1)S(1)} custom-call(bf16[3,4,4096]{2,1,0:T(4,128)(2,1)S(1)} %collective-permute-done.7.query_ref, bf16[2,1024,512]{2,1,0:T(8,128)(2,1)S(1)} %copy-done), custom_call_target="tpu_custom_call" | custom-call | flops 1048576 | bytes 1048576 | tf_op jit(solution)/shard_map/pallas_call | solution.py:47
  27.2 1.0 %shard_map.129 = bf16[3,4,4224]{2,1,0:T(4,128)(2,1)S(1)} custom-call(bf16[3,4,4096]{2,1,0:T(4,128)(2,1)S(1)} %collective-permute-done.4.query_ref, bf16[2,1024,512]{2,1,0:T(8,128)(2,1)S(1)} %copy-done), custom_call_target="tpu_custom_call" | custom-call | flops 1048576 | bytes 1048576 | tf_op jit(solution)/shard_map/pallas_call | solution.py:47
  28.2 2.8 %collective-permute-start.5 = (bf16[3,4,4224]{2,1,0:T(4,128)(2,1)S(1)}, bf16[3,4,4224]{2,1,0:T(4,128)(2,1)S(1)}, u32[]{:S(2)}, u32[]{:S(2)}) collective-permute-start(bf16[3,4,4224]{2,1,0:T(4,128)(2,1)S(1)} %shard_map.129), channel_id=1, source_target_pairs={{0,12},{4,8},{8,4},{12,0},{1,13},{5,9},{9,5},{13,1},{2,14},{6,10},... | collective-permute-start | bytes 304136 | tf_op jit(solution)/shard_map/ppermute | solution.py:35
  31.0 1.1 %shard_map.132 = (f32[3,4,4096]{2,1,0:T(4,128)S(1)}, f32[3,4,128]{2,1,0:T(4,128)S(1)}) custom-call(bf16[3,4,4096]{2,1,0:T(4,128)(2,1)S(1)} %shard_map.128.query_ref, bf16[2,1024,512]{2,1,0:T(8,128)(2,1)S(1)} %copy-done, bf16[2,4,32,512]{3,2,1,0:T(8,128)(2,1)S(1)} %copy-done.5, bf16[2,3,4,512]{3,2,1,0:T(4,128)(2,1)S(1)} %bitcast.9, ...), custom_call_target="tpu_custom_call" | custom-call | flops 1048576 | bytes 1048576 | tf_op jit(solution)/shard_map/pallas_call | solution.py:47
  32.2 0.1 collective-permute-done.8.refs_1_
  32.3 0.5 %shard_map.133 = (f32[3,4,4096]{2,1,0:T(4,128)S(1)}, f32[3,4,128]{2,1,0:T(4,128)S(1)}) custom-call(bf16[3,4,4224]{2,1,0:T(4,128)(2,1)S(1)} %collective-permute-done.6.refs_0_, bf16[3,4,4224]{2,1,0:T(4,128)(2,1)S(1)} %collective-permute-done.8.refs_1_, f32[3,4,4096]{2,1,0:T(4,128)S(1)} %get-tuple-element.26.refs_2_, f32[3,4,128]{2,1,0:T(4,128)S(1)} %get-tuple-element.27.refs_3_), custom_call_target="tpu_custom_call" | custom-call | flops 1048576 | bytes 1048576 | tf_op jit(solution)/shard_map/pallas_call | solution.py:47
  32.8 2.0 %collective-permute-done.5.refs_0_ = bf16[3,4,4224]{2,1,0:T(4,128)(2,1)S(1)} collective-permute-done((bf16[3,4,4224]{2,1,0:T(4,128)(2,1)S(1)}, bf16[3,4,4224]{2,1,0:T(4,128)(2,1)S(1)}, u32[]{:S(2)}, u32[]{:S(2)}) %collective-permute-start.5) | collective-permute-done | bytes 101408 | tf_op jit(solution)/shard_map/ppermute | solution.py:35
  34.8 0.6 %shard_map.134 = (bf16[3,4,4096]{2,1,0:T(4,128)(2,1)S(1)}, f32[16,128]{1,0:T(8,128)S(1)}) custom-call(bf16[3,4,4224]{2,1,0:T(4,128)(2,1)S(1)} %collective-permute-done.5.refs_0_, f32[3,4,4096]{2,1,0:T(4,128)S(1)} %get-tuple-element.28.refs_1_, f32[3,4,128]{2,1,0:T(4,128)S(1)} %get-tuple-element.29.refs_2_, bf16[1,64,4096]{2,1,0:T(8,128)(2,1)S(1)} %copy-done.3, ...), custom_call_target="tpu_custom_call" | custom-call | flops 1048576 | bytes 1048576 | tf_op jit(solution)/shard_map/pallas_call | solution.py:47
  35.4 0.3 collective-permute-done.11.refs_3_
  35.8 0.8 %collective-permute-done.10.refs_1_ = f32[16,128]{1,0:T(8,128)S(1)} collective-permute-done((f32[16,128]{1,0:T(8,128)S(1)}, f32[16,128]{1,0:T(8,128)S(1)}, u32[]{:S(2)}, u32[]{:S(2)}) %collective-permute-start.10) | collective-permute-done | bytes 8224 | tf_op jit(solution)/shard_map/ppermute | solution.py:30
  36.6 0.9 %shard_map.135 = (bf16[3,4,4096]{2,1,0:T(4,128)(2,1)}, bf16[3,4,4096]{2,1,0:T(4,128)(2,1)}) custom-call(f32[16,128]{1,0:T(8,128)S(1)} %get-tuple-element.31.refs_0_, f32[16,128]{1,0:T(8,128)S(1)} %collective-permute-done.10.refs_1_, bf16[1,64,4096]{2,1,0:T(8,128)(2,1)S(1)} %copy-done.4, bf16[1,64,4096]{2,1,0:T(8,128)(2,1)S(1)} %collective-permute-done.11.refs_3_, ...), custom_call_target="tpu_custom_call" | custom-call | flops 1048576 | bytes 1048576 | tf_op jit(solution)/shard_map/pallas_call | solution.py:47
  (34 shorter events, 0.2 us)
Async XLA Ops:
  0.6 6.0 %collective-permute-start = (bf16[3,4,4096]{2,1,0:T(4,128)(2,1)}, bf16[3,4,4096]{2,1,0:T(4,128)(2,1)S(1)}, u32[]{:S(2)}, u32[]{:S(2)}) collective-permute-start(bf16[3,4,4096]{2,1,0:T(4,128)(2,1)} %bitcast.7), channel_id=1, source_target_pairs={{2,0},{0,2},{3,1},{1,3},{6,4},{4,6},{7,5},{5,7},{10,8},{8,10},{11,... | collective-permute-start | bytes 294920 | tf_op jit(solution)/shard_map/ppermute | solution.py:30
  3.6 1.0 %copy-start.1 = (bf16[1,64,4096]{2,1,0:T(8,128)(2,1)S(1)}, bf16[1,64,4096]{2,1,0:T(8,128)(2,1)}, u32[]{:S(2)}) copy-start(bf16[1,64,4096]{2,1,0:T(8,128)(2,1)} %down_ref.1) | copy-start | bytes 1572868
  3.7 1.0 %copy-start.7 = (bf16[4,3,4096]{2,0,1:T(4,128)(2,1)S(1)}, bf16[4,3,4096]{2,0,1:T(4,128)(2,1)}, u32[]{:S(2)}) copy-start(bf16[4,3,4096]{2,0,1:T(4,128)(2,1)} %param.11) | copy-start | bytes 294916
  3.7 3.3 %copy-start.2 = (bf16[1,64,4096]{2,1,0:T(8,128)(2,1)S(1)}, bf16[1,64,4096]{2,1,0:T(8,128)(2,1)}, u32[]{:S(2)}) copy-start(bf16[1,64,4096]{2,1,0:T(8,128)(2,1)} %in_ref.1) | copy-start | bytes 1572868
  3.7 6.5 %copy-start.9 = (s32[4,1]{0,1:T(1,128)S(1)}, s32[4,1]{0,1:T(1,128)}, u32[]{:S(2)}) copy-start(s32[4,1]{0,1:T(1,128)} %param.16) | copy-start | bytes 52
  3.7 6.5 %copy-start.10 = (s32[4]{0:T(128)S(1)}, s32[4]{0:T(128)}, u32[]{:S(2)}) copy-start(s32[4]{0:T(128)} %param.15) | copy-start | bytes 52
  3.7 6.5 %copy-start.6 = (bf16[4,3,4096]{2,0,1:T(4,128)(2,1)S(1)}, bf16[4,3,4096]{2,0,1:T(4,128)(2,1)}, u32[]{:S(2)}) copy-start(bf16[4,3,4096]{2,0,1:T(4,128)(2,1)} %param.12) | copy-start | bytes 294916
  3.7 6.8 %copy-start.3 = (bf16[1,64,4096]{2,1,0:T(8,128)(2,1)S(1)}, bf16[1,64,4096]{2,1,0:T(8,128)(2,1)}, u32[]{:S(2)}) copy-start(bf16[1,64,4096]{2,1,0:T(8,128)(2,1)} %refs_3_) | copy-start | bytes 1572868
  3.7 7.1 %copy-start.4 = (bf16[1,64,4096]{2,1,0:T(8,128)(2,1)S(1)}, bf16[1,64,4096]{2,1,0:T(8,128)(2,1)}, u32[]{:S(2)}) copy-start(bf16[1,64,4096]{2,1,0:T(8,128)(2,1)} %refs_2_) | copy-start | bytes 1572868
  6.9 1.2 %collective-permute-start.1 = (f32[32,64]{1,0:T(8,128)S(1)}, f32[32,64]{1,0:T(8,128)S(1)}, u32[]{:S(2)}, u32[]{:S(2)}) collective-permute-start(f32[32,64]{1,0:T(8,128)S(1)} %shard_map.124._.refs_0_), channel_id=1, source_target_pairs={{1,0},{0,1},{3,2},{2,3},{5,4},{4,5},{7,6},{6,7},{9,8},{8,9},{11,10... | collective-permute-start | bytes 24584 | tf_op jit(solution)/shard_map/ppermute | solution.py:30
  8.3 5.2 %collective-permute-start.2 = (bf16[1,3,4,4096]{3,2,1,0:T(4,128)(2,1)S(1)}, bf16[1,3,4,4096]{3,2,1,0:T(4,128)(2,1)S(1)}, u32[]{:S(2)}, u32[]{:S(2)}) collective-permute-start(bf16[1,3,4,4096]{3,2,1,0:T(4,128)(2,1)S(1)} %shard_map.126.refs_6_), channel_id=1, source_target_pairs={{0,2},{2,0},{1,3},{3,1},{4,6},{6,4},{5,7},{7,5},{8,10},{10,8},{9,1... | collective-permute-start | bytes 294920 | tf_op jit(solution)/shard_map/ppermute | solution.py:35
  10.5 24.3 %collective-permute-start.9 = (bf16[1,64,4096]{2,1,0:T(8,128)(2,1)S(1)}, bf16[1,64,4096]{2,1,0:T(8,128)(2,1)S(1)}, u32[]{:S(2)}, u32[]{:S(2)}) collective-permute-start(bf16[1,64,4096]{2,1,0:T(8,128)(2,1)S(1)} %copy-done.3), channel_id=1, source_target_pairs={{2,0},{0,2},{3,1},{1,3},{6,4},{4,6},{7,5},{5,7},{10,8},{8,10},{11,... | collective-permute-start | bytes 1572872 | tf_op jit(solution)/shard_map/ppermute | solution.py:30
  10.8 25.0 %collective-permute-start.11 = (bf16[1,64,4096]{2,1,0:T(8,128)(2,1)S(1)}, bf16[1,64,4096]{2,1,0:T(8,128)(2,1)S(1)}, u32[]{:S(2)}, u32[]{:S(2)}) collective-permute-start(bf16[1,64,4096]{2,1,0:T(8,128)(2,1)S(1)} %copy-done.4), channel_id=1, source_target_pairs={{2,0},{0,2},{3,1},{1,3},{6,4},{4,6},{7,5},{5,7},{10,8},{8,10},{11,... | collective-permute-start | bytes 1572872 | tf_op jit(solution)/shard_map/ppermute | solution.py:30
  13.5 8.2 %copy-start = (bf16[2,1024,512]{2,1,0:T(8,128)(2,1)S(1)}, bf16[2,1024,512]{2,1,0:T(8,128)(2,1)}, u32[]{:S(2)}) copy-start(bf16[2,1024,512]{2,1,0:T(8,128)(2,1)} %kv_ref.7) | copy-start | bytes 6291460
  13.8 6.2 %collective-permute-start.3 = (bf16[3,4,4096]{2,1,0:T(4,128)(2,1)S(1)}, bf16[3,4,4096]{2,1,0:T(4,128)(2,1)S(1)}, u32[]{:S(2)}, u32[]{:S(2)}) collective-permute-start(bf16[3,4,4096]{2,1,0:T(4,128)(2,1)S(1)} %shard_map.128.query_ref), channel_id=1, source_target_pairs={{8,0},{12,4},{0,8},{4,12},{9,1},{13,5},{1,9},{5,13},{10,2},{14,6},... | collective-permute-start | bytes 294920 | tf_op jit(solution)/shard_map/ppermute | solution.py:30
  17.0 9.2 %collective-permute-start.7 = (bf16[3,4,4096]{2,1,0:T(4,128)(2,1)S(1)}, bf16[3,4,4096]{2,1,0:T(4,128)(2,1)S(1)}, u32[]{:S(2)}, u32[]{:S(2)}) collective-permute-start(bf16[3,4,4096]{2,1,0:T(4,128)(2,1)S(1)} %shard_map.128.query_ref), channel_id=1, source_target_pairs={{4,0},{0,4},{12,8},{8,12},{5,1},{1,5},{13,9},{9,13},{6,2},{2,6},{1... | collective-permute-start | bytes 294920 | tf_op jit(solution)/shard_map/ppermute | solution.py:30
  19.9 7.3 %collective-permute-start.4 = (bf16[3,4,4096]{2,1,0:T(4,128)(2,1)S(1)}, bf16[3,4,4096]{2,1,0:T(4,128)(2,1)S(1)}, u32[]{:S(2)}, u32[]{:S(2)}) collective-permute-start(bf16[3,4,4096]{2,1,0:T(4,128)(2,1)S(1)} %collective-permute-done.3.query_ref), channel_id=1, source_target_pairs={{4,0},{0,4},{12,8},{8,12},{5,1},{1,5},{13,9},{9,13},{6,2},{2,6},{1... | collective-permute-start | bytes 294920 | tf_op jit(solution)/shard_map/ppermute | solution.py:30
  22.7 8.4 %copy-start.5 = (bf16[2,4,32,512]{3,2,1,0:T(8,128)(2,1)S(1)}, bf16[2,4,32,512]{3,2,1,0:T(8,128)(2,1)}, u32[]{:S(2)}) copy-start(bf16[2,4,32,512]{3,2,1,0:T(8,128)(2,1)} %suffix_ref.1) | copy-start | bytes 786436
  22.7 8.4 %copy-start.8 = (bf16[2,4,3,512]{3,1,2,0:T(4,128)(2,1)S(1)}, bf16[2,4,3,512]{3,1,2,0:T(4,128)(2,1)}, u32[]{:S(2)}) copy-start(bf16[2,4,3,512]{3,1,2,0:T(4,128)(2,1)} %param.13) | copy-start | bytes 73732
  22.7 9.5 %collective-permute-start.6 = (bf16[3,4,4224]{2,1,0:T(4,128)(2,1)S(1)}, bf16[3,4,4224]{2,1,0:T(4,128)(2,1)S(1)}, u32[]{:S(2)}, u32[]{:S(2)}) collective-permute-start(bf16[3,4,4224]{2,1,0:T(4,128)(2,1)S(1)} %shard_map.130), channel_id=1, source_target_pairs={{0,8},{4,12},{8,0},{12,4},{1,9},{5,13},{9,1},{13,5},{2,10},{6,14},... | collective-permute-start | bytes 304136 | tf_op jit(solution)/shard_map/ppermute | solution.py:35
  27.2 5.1 %collective-permute-start.8 = (bf16[3,4,4224]{2,1,0:T(4,128)(2,1)S(1)}, bf16[3,4,4224]{2,1,0:T(4,128)(2,1)S(1)}, u32[]{:S(2)}, u32[]{:S(2)}) collective-permute-start(bf16[3,4,4224]{2,1,0:T(4,128)(2,1)S(1)} %shard_map.131), channel_id=1, source_target_pairs={{0,4},{4,0},{8,12},{12,8},{1,5},{5,1},{9,13},{13,9},{2,6},{6,2},{1... | collective-permute-start | bytes 304136 | tf_op jit(solution)/shard_map/ppermute | solution.py:35
  28.2 6.6 %collective-permute-start.5 = (bf16[3,4,4224]{2,1,0:T(4,128)(2,1)S(1)}, bf16[3,4,4224]{2,1,0:T(4,128)(2,1)S(1)}, u32[]{:S(2)}, u32[]{:S(2)}) collective-permute-start(bf16[3,4,4224]{2,1,0:T(4,128)(2,1)S(1)} %shard_map.129), channel_id=1, source_target_pairs={{0,12},{4,8},{8,4},{12,0},{1,13},{5,9},{9,5},{13,1},{2,14},{6,10},... | collective-permute-start | bytes 304136 | tf_op jit(solution)/shard_map/ppermute | solution.py:35
  35.4 1.2 %collective-permute-start.10 = (f32[16,128]{1,0:T(8,128)S(1)}, f32[16,128]{1,0:T(8,128)S(1)}, u32[]{:S(2)}, u32[]{:S(2)}) collective-permute-start(f32[16,128]{1,0:T(8,128)S(1)} %get-tuple-element.31.refs_0_), channel_id=1, source_target_pairs={{1,0},{0,1},{3,2},{2,3},{5,4},{4,5},{7,6},{6,7},{9,8},{8,9},{11,10... | collective-permute-start | bytes 24584 | tf_op jit(solution)/shard_map/ppermute | solution.py:30

commit v6 on v4

--- a/solution.py
+++ b/solution.py
@@ -267,41 +267,49 @@
     )
 
 
-def mix(own_ref, level_ref, arrived, t, store):
-    width = own_ref.shape[2]
+def mix(own_ref, level_ref, arrived, store, finish=None):
+    steps, _, width = own_ref.shape
     heads = width // HEAD_SIZE
-    levels = [level_ref[t]]
-    for ref in arrived:
-        levels.append(message_levels(ref[t, :, width:].astype(F32), heads))
-    highest = functools.reduce(jnp.maximum, levels)
-    shares = [jnp.exp2(level - highest) for level in levels]
-    total = functools.reduce(jnp.add, shares)
-    shares = [share / total for share in shares]
+    shares, levels = [], []
+    for t in range(steps):
+        parts = [level_ref[t]]
+        for ref in arrived:
+            parts.append(message_levels(ref[t, :, width:].astype(F32), heads))
+        highest = functools.reduce(jnp.maximum, parts)
+        weights = [jnp.exp2(part - highest) for part in parts]
+        total = functools.reduce(jnp.add, weights)
+        inverse = 1.0 / total
+        shares.append([weight * inverse for weight in weights])
+        levels.append(highest + jnp.log2(total))
+    quarter = heads // 4 if heads % 4 == 0 else heads
     for h in range(heads):
         at = slice(h * HEAD_SIZE, (h + 1) * HEAD_SIZE)
-        mixed = own_ref[t, :, at] * shares[0][:, h : h + 1]
-        for ref, share in zip(arrived, shares[1:]):
-            mixed += ref[t, :, at].astype(F32) * share[:, h : h + 1]
-        store(at, mixed)
-    return highest + jnp.log2(total)
+        for t in range(steps):
+            mixed = own_ref[t, :, at] * shares[t][0][:, h : h + 1]
+            for ref, share in zip(arrived, shares[t][1:]):
+                mixed += ref[t, :, at].astype(F32) * share[:, h : h + 1]
+            store(t, at, mixed)
+        if finish and (h + 1) % quarter == 0:
+            finish(slice((h + 1 - quarter) * HEAD_SIZE, (h + 1) * HEAD_SIZE))
+    return levels
 
 
 def blend_kernel(*refs):
     arrived = refs[:-4]
     own_ref, level_ref, out_ref, out_level_ref = refs[-4:]
-    for t in range(own_ref.shape[0]):
-
-        def store(at, mixed):
-            out_ref[t, :, at] = mixed
-
-        out_level_ref[t] = mix(own_ref, level_ref, arrived, t, store)
+
+    def store(t, at, mixed):
+        out_ref[t, :, at] = mixed
+
+    for t, level in enumerate(mix(own_ref, level_ref, arrived, store)):
+        out_level_ref[t] = level
 
 
 def merge_kernel(messages, adapters, *refs):
     arrived = refs[:messages]
     own_ref, level_ref = refs[messages : messages + 2]
     downs = refs[2 + messages : 2 + messages + adapters]
-    meta_ref, out_hbm, rank_ref, rows_ref, ids_ref, out_ref, sem = refs[2 + messages + adapters :]
+    meta_ref, out_ref, rank_ref, rows_ref, ids_ref = refs[2 + messages + adapters :]
     steps, rows, _ = own_ref.shape
     resident, rank, _ = downs[0].shape
     depth = resident * rank
@@ -310,33 +318,46 @@
     ids_ref[...] = jnp.zeros_like(ids_ref)
     for t in range(steps):
         ids_ref[t * rows : (t + 1) * rows, :] = meta_ref[...]
-
-        def store(at, mixed):
-            out_ref[t, :, at] = mixed.astype(BF16)
-            rows_ref[t * rows : (t + 1) * rows, at] = mixed
-
-        mix(own_ref, level_ref, arrived, t, store)
-    copy = pltpu.make_async_copy(out_ref, out_hbm, sem)
-    copy.start()
-    factors = jnp.concatenate([down[u] for down in downs for u in range(resident)], axis=0)
-    result = dot(rows_ref[...].astype(BF16), factors, ((1,), (1,)))
+    products = []
+
+    def store(t, at, mixed):
+        out_ref[t, :, at] = mixed.astype(BF16)
+        rows_ref[t * rows : (t + 1) * rows, at] = mixed
+
+    def finish(at):
+        factors = [down[u, :, at] for down in downs for u in range(resident)]
+        products.append(
+            dot(rows_ref[:, at].astype(BF16), jnp.concatenate(factors, axis=0), ((1,), (1,)))
+        )
+
+    mix(own_ref, level_ref, arrived, store, finish)
+    result = functools.reduce(jnp.add, products)
     lane = lax.broadcasted_iota(jnp.int32, result.shape, 1)
     owner = peer(x, lane // depth, adapters) * resident + lane % depth // rank
     rank_ref[...] = jnp.where(owner == ids_ref[:, LANES // 2 : LANES // 2 + 1], result, 0.0)
-    copy.wait()
 
 
 def up_kernel(parts, adapters, *refs):
     ranks = refs[:parts]
     ups = refs[parts : parts + adapters]
-    out_ref = refs[parts + adapters]
+    attended_ref, attended_hbm, out_hbm, out_ref, sems = refs[parts + adapters :]
+    copies = [pltpu.make_async_copy(attended_ref, attended_hbm, sems.at[4])]
+    copies[0].start()
     steps, rows, width = out_ref.shape
     resident = ups[0].shape[0]
     chosen = functools.reduce(jnp.add, [ref[...] for ref in ranks]).astype(BF16)
-    factors = jnp.concatenate([up[u] for up in ups for u in range(resident)], axis=0)
-    result = dot(chosen, factors, ((1,), (0,)))
-    for t in range(steps):
-        out_ref[t] = result[t * rows : (t + 1) * rows].astype(BF16)
+    quarter = width // 4
+    for i in range(4):
+        at = slice(i * quarter, (i + 1) * quarter)
+        factors = jnp.concatenate([up[u, :, at] for up in ups for u in range(resident)], axis=0)
+        result = dot(chosen, factors, ((1,), (0,)))
+        for t in range(steps):
+            out_ref[t, :, at] = result[t * rows : (t + 1) * rows].astype(BF16)
+        copy = pltpu.make_async_copy(out_ref.at[:, :, at], out_hbm.at[:, :, at], sems.at[i])
+        copy.start()
+        copies.append(copy)
+    for copy in copies:
+        copy.wait()
 
 
 def rope_table(slots, first_position):
@@ -494,16 +515,15 @@
         scratch=[
             pltpu.VMEM((pad_rows, width), F32),
             pltpu.VMEM((pad_rows, LANES), jnp.int32),
-            pltpu.VMEM((steps, rows, width), BF16),
-            pltpu.SemaphoreType.DMA,
         ],
-        out_specs=(pl.BlockSpec(memory_space=pl.ANY), VMEM),
     )
     out_ranks = [out_rank] + [fetch(out_rank, "head", j) for j in range(1, halves)]
-    adapted = call(
+    attended, adapted = call(
         functools.partial(up_kernel, halves, adapters),
-        jax.ShapeDtypeStruct((steps, rows, width), BF16),
-        (*out_ranks, *output_ups),
+        (jax.ShapeDtypeStruct((steps, rows, width), BF16),) * 2,
+        (*out_ranks, *output_ups, attended),
+        scratch=[pltpu.VMEM((steps, rows, width), BF16), pltpu.SemaphoreType.DMA((5,))],
+        out_specs=(pl.BlockSpec(memory_space=pl.ANY),) * 2,
     )
     return attended.transpose(1, 0, 2), adapted.transpose(1, 0, 2)
 

time: 38.8 us -> 38.2 us (0.985)
  Pallas kernels: 8.57 us -> 7.7 us
    pallas_call x14, Pallas kernels: 8.57 us -> 7.7 us  [call(): pl.pallas_call(kernel, out_shape=out_shape, in_specs=specs or [VMEM] * le...]
  transfers between devices with their start and end apart: 13 -> 13, of which waited for: 8 -> 8; matrix products, arithmetic and copies ran while one was open for 3% -> 3% of each run, Pallas kernels for 19% -> 17%
where the time goes in v6:
time: 38.2 us; the launch traced here: 38.1 us
  starting transfers between devices  19 us (50%)
  waiting for transfers between devices  8.43 us (22%)
  Pallas kernels  7.7 us (20%)
  other arithmetic  1.31 us (3%)
  between operations  0.79 us (2%)
  local copies, waits for them, and re-layouts  0.78 us (2%)
    ppermute x9, starting transfers between devices, fetch(): lax.ppermute(value, axis, [(peer(i, offset, size), i) for i in range(size)])  11.1 us
    ppermute x4, starting transfers between devices, send(): lax.ppermute(value, axis, [(i, peer(i, offset, size)) for i in range(size)])  7.94 us
    pallas_call x14, Pallas kernels, call(): pl.pallas_call(kernel, out_shape=out_shape, in_specs=specs or [VMEM] * le...  7.7 us
    ppermute x9, waiting for transfers between devices, fetch(): lax.ppermute(value, axis, [(peer(i, offset, size), i) for i in range(size)])  5.64 us
    ppermute x4, waiting for transfers between devices, send(): lax.ppermute(value, axis, [(i, peer(i, offset, size)) for i in range(size)])  2.79 us
    select_n x1, other arithmetic, on_device(): base = jnp.where(lane < width, base, facts.astype(BF16))  1.04 us
    unnamed x16, local copies, waits for them, and re-layouts  0.77 us
  transfers between devices with their start and end apart: 13, of which 8 were waited for; matrix products, arithmetic and copies ran while one was open for 3% of the time, Pallas kernels for 17%

profile of v6, /device:TPU:0, one launch (start us, length us, event | category | flops | bytes accessed | tf_op | source)
XLA Modules:
  0.0 38.1 jit_solution(17007048204873587661)
XLA Ops:
  0.6 3.0 %collective-permute-start = (bf16[3,4,4096]{2,1,0:T(4,128)(2,1)}, bf16[3,4,4096]{2,1,0:T(4,128)(2,1)S(1)}, u32[]{:S(2)}, u32[]{:S(2)}) collective-permute-start(bf16[3,4,4096]{2,1,0:T(4,128)(2,1)} %bitcast.8), channel_id=1, source_target_pairs={{2,0},{0,2},{3,1},{1,3},{6,4},{4,6},{7,5},{5,7},{10,8},{8,10},{11,... | collective-permute-start | bytes 294920 | tf_op jit(solution)/shard_map/ppermute | solution.py:30
  3.6 1.0 %fusion.refs_3_.refs_2_ = bf16[3,4,4224]{2,1,0:T(4,128)(2,1)S(1)} fusion(s32[4]{0:T(128)} %bitcast.12, s32[4]{0:T(128)} %param.15, bf16[3,4,4096]{2,1,0:T(4,128)(2,1)} %bitcast.11, pred[4224]{0:T(1024)(128)(4,1)S(1)} %get-tuple-element.37, pred[4224]{0:T(1024)(128)(4,1)S(1)} %get-tuple-element.38), kind=kLoop, calls=%fused_computation.1 | loop fusion | flops 152064 | bytes 208160 | tf_op jit(solution)/shard_map/jit(_where)/select_n | solution.py:401
  4.7 0.1 collective-permute-start.2
  4.8 0.2 multiply_cosine_fusion
  5.1 0.7 %copy-done.1 = bf16[1,64,4096]{2,1,0:T(8,128)(2,1)S(1)} copy-done((bf16[1,64,4096]{2,1,0:T(8,128)(2,1)S(1)}, bf16[1,64,4096]{2,1,0:T(8,128)(2,1)}, u32[]{:S(2)}) %copy-start.1) | copy-done | bytes 524312
  5.9 0.3 shard_map.126
  6.1 1.0 %collective-permute-done.refs_0_ = bf16[3,4,4096]{2,1,0:T(4,128)(2,1)S(1)} collective-permute-done((bf16[3,4,4096]{2,1,0:T(4,128)(2,1)}, bf16[3,4,4096]{2,1,0:T(4,128)(2,1)S(1)}, u32[]{:S(2)}, u32[]{:S(2)}) %collective-permute-start) | collective-permute-done | bytes 98336 | tf_op jit(solution)/shard_map/ppermute | solution.py:30
  7.1 0.3 shard_map.127._.refs_0_
  7.4 2.0 %collective-permute-done.2.refs_3_ = bf16[3,4,4224]{2,1,0:T(4,128)(2,1)S(1)} collective-permute-done((bf16[3,4,4224]{2,1,0:T(4,128)(2,1)S(1)}, bf16[3,4,4224]{2,1,0:T(4,128)(2,1)S(1)}, u32[]{:S(2)}, u32[]{:S(2)}) %collective-permute-start.2) | collective-permute-done | bytes 101408 | tf_op jit(solution)/shard_map/ppermute | solution.py:30
  9.4 0.4 shard_map.129.refs_5_
  9.8 1.6 %collective-permute-start.3 = (bf16[3,4,4096]{2,1,0:T(4,128)(2,1)S(1)}, bf16[3,4,4096]{2,1,0:T(4,128)(2,1)S(1)}, u32[]{:S(2)}, u32[]{:S(2)}) collective-permute-start(bf16[3,4,4096]{2,1,0:T(4,128)(2,1)S(1)} %shard_map.129.refs_5_), channel_id=1, source_target_pairs={{0,2},{2,0},{1,3},{3,1},{4,6},{6,4},{5,7},{7,5},{8,10},{10,8},{9,1... | collective-permute-start | bytes 294920 | tf_op jit(solution)/shard_map/ppermute | solution.py:35
  11.4 0.4 shard_map.130.refs_0_
  11.8 0.6 %collective-permute-start.10 = (bf16[1,64,4096]{2,1,0:T(8,128)(2,1)S(1)}, bf16[1,64,4096]{2,1,0:T(8,128)(2,1)S(1)}, u32[]{:S(2)}, u32[]{:S(2)}) collective-permute-start(bf16[1,64,4096]{2,1,0:T(8,128)(2,1)S(1)} %copy-done.3), channel_id=1, source_target_pairs={{2,0},{0,2},{3,1},{1,3},{6,4},{4,6},{7,5},{5,7},{10,8},{8,10},{11,... | collective-permute-start | bytes 1572872 | tf_op jit(solution)/shard_map/ppermute | solution.py:30
  12.4 1.5 %collective-permute-start.12 = (bf16[1,64,4096]{2,1,0:T(8,128)(2,1)S(1)}, bf16[1,64,4096]{2,1,0:T(8,128)(2,1)S(1)}, u32[]{:S(2)}, u32[]{:S(2)}) collective-permute-start(bf16[1,64,4096]{2,1,0:T(8,128)(2,1)S(1)} %copy-done.4), channel_id=1, source_target_pairs={{2,0},{0,2},{3,1},{1,3},{6,4},{4,6},{7,5},{5,7},{10,8},{8,10},{11,... | collective-permute-start | bytes 1572872 | tf_op jit(solution)/shard_map/ppermute | solution.py:30
  13.9 0.8 %collective-permute-done.3.refs_1_ = bf16[3,4,4096]{2,1,0:T(4,128)(2,1)S(1)} collective-permute-done((bf16[3,4,4096]{2,1,0:T(4,128)(2,1)S(1)}, bf16[3,4,4096]{2,1,0:T(4,128)(2,1)S(1)}, u32[]{:S(2)}, u32[]{:S(2)}) %collective-permute-start.3) | collective-permute-done | bytes 98336 | tf_op jit(solution)/shard_map/ppermute | solution.py:35
  14.7 0.1 shard_map.131
  14.8 2.7 %collective-permute-start.4 = (bf16[3,4,4096]{2,1,0:T(4,128)(2,1)S(1)}, bf16[3,4,4096]{2,1,0:T(4,128)(2,1)S(1)}, u32[]{:S(2)}, u32[]{:S(2)}) collective-permute-start(bf16[3,4,4096]{2,1,0:T(4,128)(2,1)S(1)} %get-tuple-element.22.query_ref), channel_id=1, source_target_pairs={{8,0},{12,4},{0,8},{4,12},{9,1},{13,5},{1,9},{5,13},{10,2},{14,6},... | collective-permute-start | bytes 294920 | tf_op jit(solution)/shard_map/ppermute | solution.py:30
  17.5 1.6 %collective-permute-start.8 = (bf16[3,4,4096]{2,1,0:T(4,128)(2,1)S(1)}, bf16[3,4,4096]{2,1,0:T(4,128)(2,1)S(1)}, u32[]{:S(2)}, u32[]{:S(2)}) collective-permute-start(bf16[3,4,4096]{2,1,0:T(4,128)(2,1)S(1)} %get-tuple-element.22.query_ref), channel_id=1, source_target_pairs={{4,0},{0,4},{12,8},{8,12},{5,1},{1,5},{13,9},{9,13},{6,2},{2,6},{1... | collective-permute-start | bytes 294920 | tf_op jit(solution)/shard_map/ppermute | solution.py:30
  19.0 1.5 %collective-permute-done.4.query_ref = bf16[3,4,4096]{2,1,0:T(4,128)(2,1)S(1)} collective-permute-done((bf16[3,4,4096]{2,1,0:T(4,128)(2,1)S(1)}, bf16[3,4,4096]{2,1,0:T(4,128)(2,1)S(1)}, u32[]{:S(2)}, u32[]{:S(2)}) %collective-permute-start.4) | collective-permute-done | bytes 98336 | tf_op jit(solution)/shard_map/ppermute | solution.py:30
  20.5 1.7 %collective-permute-start.5 = (bf16[3,4,4096]{2,1,0:T(4,128)(2,1)S(1)}, bf16[3,4,4096]{2,1,0:T(4,128)(2,1)S(1)}, u32[]{:S(2)}, u32[]{:S(2)}) collective-permute-start(bf16[3,4,4096]{2,1,0:T(4,128)(2,1)S(1)} %collective-permute-done.4.query_ref), channel_id=1, source_target_pairs={{4,0},{0,4},{12,8},{8,12},{5,1},{1,5},{13,9},{9,13},{6,2},{2,6},{1... | collective-permute-start | bytes 294920 | tf_op jit(solution)/shard_map/ppermute | solution.py:30
  22.2 1.0 %shard_map.133 = bf16[3,4,4224]{2,1,0:T(4,128)(2,1)S(1)} custom-call(bf16[3,4,4096]{2,1,0:T(4,128)(2,1)S(1)} %collective-permute-done.4.query_ref, bf16[2,1024,512]{2,1,0:T(8,128)(2,1)S(1)} %copy-done), custom_call_target="tpu_custom_call" | custom-call | flops 1048576 | bytes 1048576 | tf_op jit(solution)/shard_map/pallas_call | solution.py:43
  23.2 3.4 %collective-permute-start.7 = (bf16[3,4,4224]{2,1,0:T(4,128)(2,1)S(1)}, bf16[3,4,4224]{2,1,0:T(4,128)(2,1)S(1)}, u32[]{:S(2)}, u32[]{:S(2)}) collective-permute-start(bf16[3,4,4224]{2,1,0:T(4,128)(2,1)S(1)} %shard_map.133), channel_id=1, source_target_pairs={{0,8},{4,12},{8,0},{12,4},{1,9},{5,13},{9,1},{13,5},{2,10},{6,14},... | collective-permute-start | bytes 304136 | tf_op jit(solution)/shard_map/ppermute | solution.py:35
  26.7 1.0 %shard_map.134 = bf16[3,4,4224]{2,1,0:T(4,128)(2,1)S(1)} custom-call(bf16[3,4,4096]{2,1,0:T(4,128)(2,1)S(1)} %collective-permute-done.8.query_ref, bf16[2,1024,512]{2,1,0:T(8,128)(2,1)S(1)} %copy-done), custom_call_target="tpu_custom_call" | custom-call | flops 1048576 | bytes 1048576 | tf_op jit(solution)/shard_map/pallas_call | solution.py:43
  27.7 1.0 %shard_map.132 = bf16[3,4,4224]{2,1,0:T(4,128)(2,1)S(1)} custom-call(bf16[3,4,4096]{2,1,0:T(4,128)(2,1)S(1)} %collective-permute-done.5.query_ref, bf16[2,1024,512]{2,1,0:T(8,128)(2,1)S(1)} %copy-done), custom_call_target="tpu_custom_call" | custom-call | flops 1048576 | bytes 1048576 | tf_op jit(solution)/shard_map/pallas_call | solution.py:43
  28.8 2.9 %collective-permute-start.6 = (bf16[3,4,4224]{2,1,0:T(4,128)(2,1)S(1)}, bf16[3,4,4224]{2,1,0:T(4,128)(2,1)S(1)}, u32[]{:S(2)}, u32[]{:S(2)}) collective-permute-start(bf16[3,4,4224]{2,1,0:T(4,128)(2,1)S(1)} %shard_map.132), channel_id=1, source_target_pairs={{0,12},{4,8},{8,4},{12,0},{1,13},{5,9},{9,5},{13,1},{2,14},{6,10},... | collective-permute-start | bytes 304136 | tf_op jit(solution)/shard_map/ppermute | solution.py:35
  31.7 1.1 %shard_map.135 = (f32[3,4,4096]{2,1,0:T(4,128)S(1)}, f32[3,4,128]{2,1,0:T(4,128)S(1)}) custom-call(bf16[3,4,4096]{2,1,0:T(4,128)(2,1)S(1)} %get-tuple-element.22.query_ref, bf16[2,1024,512]{2,1,0:T(8,128)(2,1)S(1)} %copy-done, bf16[2,4,32,512]{3,2,1,0:T(8,128)(2,1)S(1)} %copy-done.5, bf16[2,3,4,512]{3,2,1,0:T(4,128)(2,1)S(1)} %bitcast.10, ...), custom_call_target="tpu_custom_call" | custom-call | flops 1048576 | bytes 1048576 | tf_op jit(solution)/shard_map/pallas_call | solution.py:43
  32.9 0.5 %shard_map.136 = (f32[3,4,4096]{2,1,0:T(4,128)S(1)}, f32[3,4,128]{2,1,0:T(4,128)S(1)}) custom-call(bf16[3,4,4224]{2,1,0:T(4,128)(2,1)S(1)} %collective-permute-done.7.refs_0_, bf16[3,4,4224]{2,1,0:T(4,128)(2,1)S(1)} %collective-permute-done.9.refs_1_, f32[3,4,4096]{2,1,0:T(4,128)S(1)} %get-tuple-element.24.refs_2_, f32[3,4,128]{2,1,0:T(4,128)S(1)} %get-tuple-element.25.refs_3_), custom_call_target="tpu_custom_call" | custom-call | flops 1048576 | bytes 1048576 | tf_op jit(solution)/shard_map/pallas_call | solution.py:43
  33.4 1.9 %collective-permute-done.6.refs_0_ = bf16[3,4,4224]{2,1,0:T(4,128)(2,1)S(1)} collective-permute-done((bf16[3,4,4224]{2,1,0:T(4,128)(2,1)S(1)}, bf16[3,4,4224]{2,1,0:T(4,128)(2,1)S(1)}, u32[]{:S(2)}, u32[]{:S(2)}) %collective-permute-start.6) | collective-permute-done | bytes 101408 | tf_op jit(solution)/shard_map/ppermute | solution.py:35
  35.3 0.6 %shard_map.137 = (bf16[3,4,4096]{2,1,0:T(4,128)(2,1)S(1)}, f32[16,128]{1,0:T(8,128)S(1)}) custom-call(bf16[3,4,4224]{2,1,0:T(4,128)(2,1)S(1)} %collective-permute-done.6.refs_0_, f32[3,4,4096]{2,1,0:T(4,128)S(1)} %get-tuple-element.26.refs_1_, f32[3,4,128]{2,1,0:T(4,128)S(1)} %get-tuple-element.27.refs_2_, bf16[1,64,4096]{2,1,0:T(8,128)(2,1)S(1)} %copy-done.3, ...), custom_call_target="tpu_custom_call" | custom-call | flops 1048576 | bytes 1048576 | tf_op jit(solution)/shard_map/pallas_call | solution.py:43
  36.0 1.0 %collective-permute-done.12.refs_3_ = bf16[1,64,4096]{2,1,0:T(8,128)(2,1)S(1)} collective-permute-done((bf16[1,64,4096]{2,1,0:T(8,128)(2,1)S(1)}, bf16[1,64,4096]{2,1,0:T(8,128)(2,1)S(1)}, u32[]{:S(2)}, u32[]{:S(2)}) %collective-permute-start.12) | collective-permute-done | bytes 524320 | tf_op jit(solution)/shard_map/ppermute | solution.py:30
  37.0 0.2 collective-permute-done.11.refs_1_
  37.1 0.9 %shard_map.138 = (bf16[3,4,4096]{2,1,0:T(4,128)(2,1)}, bf16[3,4,4096]{2,1,0:T(4,128)(2,1)}) custom-call(f32[16,128]{1,0:T(8,128)S(1)} %get-tuple-element.29.refs_0_, f32[16,128]{1,0:T(8,128)S(1)} %collective-permute-done.11.refs_1_, bf16[1,64,4096]{2,1,0:T(8,128)(2,1)S(1)} %copy-done.4, bf16[1,64,4096]{2,1,0:T(8,128)(2,1)S(1)} %collective-permute-done.12.refs_3_, ...), custom_call_target="tpu_custom_call" | custom-call | flops 1048576 | bytes 1048576 | tf_op jit(solution)/shard_map/pallas_call | solution.py:43
  (31 shorter events, 0.3 us)
Async XLA Ops:
  0.6 6.5 %collective-permute-start = (bf16[3,4,4096]{2,1,0:T(4,128)(2,1)}, bf16[3,4,4096]{2,1,0:T(4,128)(2,1)S(1)}, u32[]{:S(2)}, u32[]{:S(2)}) collective-permute-start(bf16[3,4,4096]{2,1,0:T(4,128)(2,1)} %bitcast.8), channel_id=1, source_target_pairs={{2,0},{0,2},{3,1},{1,3},{6,4},{4,6},{7,5},{5,7},{10,8},{8,10},{11,... | collective-permute-start | bytes 294920 | tf_op jit(solution)/shard_map/ppermute | solution.py:30
  4.7 4.7 %collective-permute-start.2 = (bf16[3,4,4224]{2,1,0:T(4,128)(2,1)S(1)}, bf16[3,4,4224]{2,1,0:T(4,128)(2,1)S(1)}, u32[]{:S(2)}, u32[]{:S(2)}) collective-permute-start(bf16[3,4,4224]{2,1,0:T(4,128)(2,1)S(1)} %fusion.refs_3_.refs_2_), channel_id=1, source_target_pairs={{2,0},{0,2},{3,1},{1,3},{6,4},{4,6},{7,5},{5,7},{10,8},{8,10},{11,... | collective-permute-start | bytes 304136 | tf_op jit(solution)/shard_map/ppermute | solution.py:30
  4.8 1.0 %copy-start.1 = (bf16[1,64,4096]{2,1,0:T(8,128)(2,1)S(1)}, bf16[1,64,4096]{2,1,0:T(8,128)(2,1)}, u32[]{:S(2)}) copy-start(bf16[1,64,4096]{2,1,0:T(8,128)(2,1)} %down_ref.1) | copy-start | bytes 1572868
  4.8 1.0 %copy-start.6 = (bf16[4,3,4096]{2,0,1:T(4,128)(2,1)S(1)}, bf16[4,3,4096]{2,0,1:T(4,128)(2,1)}, u32[]{:S(2)}) copy-start(bf16[4,3,4096]{2,0,1:T(4,128)(2,1)} %param.11) | copy-start | bytes 294916
  4.8 2.5 %copy-start.2 = (bf16[1,64,4096]{2,1,0:T(8,128)(2,1)S(1)}, bf16[1,64,4096]{2,1,0:T(8,128)(2,1)}, u32[]{:S(2)}) copy-start(bf16[1,64,4096]{2,1,0:T(8,128)(2,1)} %in_ref.1) | copy-start | bytes 1572868
  5.8 5.9 %copy-start.3 = (bf16[1,64,4096]{2,1,0:T(8,128)(2,1)S(1)}, bf16[1,64,4096]{2,1,0:T(8,128)(2,1)}, u32[]{:S(2)}) copy-start(bf16[1,64,4096]{2,1,0:T(8,128)(2,1)} %refs_3_) | copy-start | bytes 1572868
  5.8 6.5 %copy-start.4 = (bf16[1,64,4096]{2,1,0:T(8,128)(2,1)S(1)}, bf16[1,64,4096]{2,1,0:T(8,128)(2,1)}, u32[]{:S(2)}) copy-start(bf16[1,64,4096]{2,1,0:T(8,128)(2,1)} %refs_2_) | copy-start | bytes 1572868
  7.3 2.1 %collective-permute-start.1 = (f32[32,64]{1,0:T(8,128)S(1)}, f32[32,64]{1,0:T(8,128)S(1)}, u32[]{:S(2)}, u32[]{:S(2)}) collective-permute-start(f32[32,64]{1,0:T(8,128)S(1)} %shard_map.127._.refs_0_), channel_id=1, source_target_pairs={{1,0},{0,1},{3,2},{2,3},{5,4},{4,5},{7,6},{6,7},{9,8},{8,9},{11,10... | collective-permute-start | bytes 24584 | tf_op jit(solution)/shard_map/ppermute | solution.py:30
  9.8 4.9 %collective-permute-start.3 = (bf16[3,4,4096]{2,1,0:T(4,128)(2,1)S(1)}, bf16[3,4,4096]{2,1,0:T(4,128)(2,1)S(1)}, u32[]{:S(2)}, u32[]{:S(2)}) collective-permute-start(bf16[3,4,4096]{2,1,0:T(4,128)(2,1)S(1)} %shard_map.129.refs_5_), channel_id=1, source_target_pairs={{0,2},{2,0},{1,3},{3,1},{4,6},{6,4},{5,7},{7,5},{8,10},{10,8},{9,1... | collective-permute-start | bytes 294920 | tf_op jit(solution)/shard_map/ppermute | solution.py:35
  11.8 10.4 %copy-start = (bf16[2,1024,512]{2,1,0:T(8,128)(2,1)S(1)}, bf16[2,1024,512]{2,1,0:T(8,128)(2,1)}, u32[]{:S(2)}) copy-start(bf16[2,1024,512]{2,1,0:T(8,128)(2,1)} %kv_ref.7) | copy-start | bytes 6291460
  11.8 23.5 %collective-permute-start.10 = (bf16[1,64,4096]{2,1,0:T(8,128)(2,1)S(1)}, bf16[1,64,4096]{2,1,0:T(8,128)(2,1)S(1)}, u32[]{:S(2)}, u32[]{:S(2)}) collective-permute-start(bf16[1,64,4096]{2,1,0:T(8,128)(2,1)S(1)} %copy-done.3), channel_id=1, source_target_pairs={{2,0},{0,2},{3,1},{1,3},{6,4},{4,6},{7,5},{5,7},{10,8},{8,10},{11,... | collective-permute-start | bytes 1572872 | tf_op jit(solution)/shard_map/ppermute | solution.py:30
  12.4 24.6 %collective-permute-start.12 = (bf16[1,64,4096]{2,1,0:T(8,128)(2,1)S(1)}, bf16[1,64,4096]{2,1,0:T(8,128)(2,1)S(1)}, u32[]{:S(2)}, u32[]{:S(2)}) collective-permute-start(bf16[1,64,4096]{2,1,0:T(8,128)(2,1)S(1)} %copy-done.4), channel_id=1, source_target_pairs={{2,0},{0,2},{3,1},{1,3},{6,4},{4,6},{7,5},{5,7},{10,8},{8,10},{11,... | collective-permute-start | bytes 1572872 | tf_op jit(solution)/shard_map/ppermute | solution.py:30
  14.8 5.7 %collective-permute-start.4 = (bf16[3,4,4096]{2,1,0:T(4,128)(2,1)S(1)}, bf16[3,4,4096]{2,1,0:T(4,128)(2,1)S(1)}, u32[]{:S(2)}, u32[]{:S(2)}) collective-permute-start(bf16[3,4,4096]{2,1,0:T(4,128)(2,1)S(1)} %get-tuple-element.22.query_ref), channel_id=1, source_target_pairs={{8,0},{12,4},{0,8},{4,12},{9,1},{13,5},{1,9},{5,13},{10,2},{14,6},... | collective-permute-start | bytes 294920 | tf_op jit(solution)/shard_map/ppermute | solution.py:30
  17.5 9.2 %collective-permute-start.8 = (bf16[3,4,4096]{2,1,0:T(4,128)(2,1)S(1)}, bf16[3,4,4096]{2,1,0:T(4,128)(2,1)S(1)}, u32[]{:S(2)}, u32[]{:S(2)}) collective-permute-start(bf16[3,4,4096]{2,1,0:T(4,128)(2,1)S(1)} %get-tuple-element.22.query_ref), channel_id=1, source_target_pairs={{4,0},{0,4},{12,8},{8,12},{5,1},{1,5},{13,9},{9,13},{6,2},{2,6},{1... | collective-permute-start | bytes 294920 | tf_op jit(solution)/shard_map/ppermute | solution.py:30
  20.5 7.2 %collective-permute-start.5 = (bf16[3,4,4096]{2,1,0:T(4,128)(2,1)S(1)}, bf16[3,4,4096]{2,1,0:T(4,128)(2,1)S(1)}, u32[]{:S(2)}, u32[]{:S(2)}) collective-permute-start(bf16[3,4,4096]{2,1,0:T(4,128)(2,1)S(1)} %collective-permute-done.4.query_ref), channel_id=1, source_target_pairs={{4,0},{0,4},{12,8},{8,12},{5,1},{1,5},{13,9},{9,13},{6,2},{2,6},{1... | collective-permute-start | bytes 294920 | tf_op jit(solution)/shard_map/ppermute | solution.py:30
  23.2 8.4 %copy-start.5 = (bf16[2,4,32,512]{3,2,1,0:T(8,128)(2,1)S(1)}, bf16[2,4,32,512]{3,2,1,0:T(8,128)(2,1)}, u32[]{:S(2)}) copy-start(bf16[2,4,32,512]{3,2,1,0:T(8,128)(2,1)} %suffix_ref.1) | copy-start | bytes 786436
  23.2 8.4 %copy-start.7 = (bf16[2,4,3,512]{3,1,2,0:T(4,128)(2,1)S(1)}, bf16[2,4,3,512]{3,1,2,0:T(4,128)(2,1)}, u32[]{:S(2)}) copy-start(bf16[2,4,3,512]{3,1,2,0:T(4,128)(2,1)} %param.13) | copy-start | bytes 73732
  23.2 9.6 %collective-permute-start.7 = (bf16[3,4,4224]{2,1,0:T(4,128)(2,1)S(1)}, bf16[3,4,4224]{2,1,0:T(4,128)(2,1)S(1)}, u32[]{:S(2)}, u32[]{:S(2)}) collective-permute-start(bf16[3,4,4224]{2,1,0:T(4,128)(2,1)S(1)} %shard_map.133), channel_id=1, source_target_pairs={{0,8},{4,12},{8,0},{12,4},{1,9},{5,13},{9,1},{13,5},{2,10},{6,14},... | collective-permute-start | bytes 304136 | tf_op jit(solution)/shard_map/ppermute | solution.py:35
  27.7 5.2 %collective-permute-start.9 = (bf16[3,4,4224]{2,1,0:T(4,128)(2,1)S(1)}, bf16[3,4,4224]{2,1,0:T(4,128)(2,1)S(1)}, u32[]{:S(2)}, u32[]{:S(2)}) collective-permute-start(bf16[3,4,4224]{2,1,0:T(4,128)(2,1)S(1)} %shard_map.134), channel_id=1, source_target_pairs={{0,4},{4,0},{8,12},{12,8},{1,5},{5,1},{9,13},{13,9},{2,6},{6,2},{1... | collective-permute-start | bytes 304136 | tf_op jit(solution)/shard_map/ppermute | solution.py:35
  28.8 6.6 %collective-permute-start.6 = (bf16[3,4,4224]{2,1,0:T(4,128)(2,1)S(1)}, bf16[3,4,4224]{2,1,0:T(4,128)(2,1)S(1)}, u32[]{:S(2)}, u32[]{:S(2)}) collective-permute-start(bf16[3,4,4224]{2,1,0:T(4,128)(2,1)S(1)} %shard_map.132), channel_id=1, source_target_pairs={{0,12},{4,8},{8,4},{12,0},{1,13},{5,9},{9,5},{13,1},{2,14},{6,10},... | collective-permute-start | bytes 304136 | tf_op jit(solution)/shard_map/ppermute | solution.py:35
  36.0 1.2 %collective-permute-start.11 = (f32[16,128]{1,0:T(8,128)S(1)}, f32[16,128]{1,0:T(8,128)S(1)}, u32[]{:S(2)}, u32[]{:S(2)}) collective-permute-start(f32[16,128]{1,0:T(8,128)S(1)} %get-tuple-element.29.refs_0_), channel_id=1, source_target_pairs={{1,0},{0,1},{3,2},{2,3},{5,4},{4,5},{7,6},{6,7},{9,8},{8,9},{11,10... | collective-permute-start | bytes 24584 | tf_op jit(solution)/shard_map/ppermute | solution.py:30

commit v7 on v6

--- a/solution.py
+++ b/solution.py
@@ -183,7 +183,8 @@
     return out
 
 
-def far_kernel(scale, query_ref, kv_ref, out_ref, rows_ref, kept, stats_ref):
+def far_kernel(scale, query_ref, kv_ref, *refs):
+    out_ref, rows_ref, kept, stats_ref = refs[-4:]
     steps, rows, width = query_ref.shape
     heads = width // HEAD_SIZE
     kv_heads = kv_ref.shape[2] // HEAD_SIZE
@@ -468,14 +469,14 @@
     piece_of = {0: queries}
     for k in range(1, seq_count):
         piece_of[k] = fetch(piece_of[k - 1], "seq", 1) if k % 2 else fetch(queries, "seq", k)
-    order = list(range(2, seq_count)) + [1]
+    order = [1] + list(range(2, seq_count))
     messages = []
     for k in order:
         messages.append(
             call(
                 functools.partial(far_kernel, scale),
                 message,
-                (piece_of[k], prompt_key_value),
+                (piece_of[k], prompt_key_value, *messages[: k == 2]),
                 scratch=query_scratch,
             )
         )
@@ -501,10 +502,9 @@
         fetch(output_up_factors, "adapter", j) for j in range(1, adapters)
     ]
     partials = [send(part, "seq", k) for part, k in zip(messages, order)]
-    last = max(seq_count - 3, 0)
-    early, partials = partials[:last] + partials[last + 1 :], partials[last : last + 1]
+    early, partials = partials[:-1], partials[-1:]
     if early:
-        own, level = call(blend_kernel, part_shapes, (*early, own, level))
+        own, level = call(blend_kernel, part_shapes, (*early[::-1], own, level))
     attended, out_rank = call(
         functools.partial(merge_kernel, len(partials), adapters),
         (

time: 38.2 us -> 38.2 us (level)
    ppermute x4, waiting for transfers between devices: 2.79 us -> 1.86 us  [send(): lax.ppermute(value, axis, [(i, peer(i, offset, size)) for i in range(size)])]
    ppermute x9, waiting for transfers between devices: 5.64 us -> 6.56 us  [fetch(): lax.ppermute(value, axis, [(peer(i, offset, size), i) for i in range(size)])]
  transfers between devices with their start and end apart: 13 -> 13, of which waited for: 8 -> 9; matrix products, arithmetic and copies ran while one was open for 3% -> 3% of each run, Pallas kernels for 17% -> 17%
where the time goes in v7:
time: 38.2 us; the launch traced here: 38 us
  starting transfers between devices  19 us (50%)
  waiting for transfers between devices  8.42 us (22%)
  Pallas kernels  7.71 us (20%)
  other arithmetic  1.31 us (3%)
  local copies, waits for them, and re-layouts  0.78 us (2%)
  between operations  0.78 us (2%)
    ppermute x9, starting transfers between devices, fetch(): lax.ppermute(value, axis, [(peer(i, offset, size), i) for i in range(size)])  11.1 us
    ppermute x4, starting transfers between devices, send(): lax.ppermute(value, axis, [(i, peer(i, offset, size)) for i in range(size)])  7.95 us
    pallas_call x14, Pallas kernels, call(): pl.pallas_call(kernel, out_shape=out_shape, in_specs=specs or [VMEM] * le...  7.71 us
    ppermute x9, waiting for transfers between devices, fetch(): lax.ppermute(value, axis, [(peer(i, offset, size), i) for i in range(size)])  6.56 us
    ppermute x4, waiting for transfers between devices, send(): lax.ppermute(value, axis, [(i, peer(i, offset, size)) for i in range(size)])  1.86 us
    select_n x1, other arithmetic, on_device(): base = jnp.where(lane < width, base, facts.astype(BF16))  1.04 us
    unnamed x16, local copies, waits for them, and re-layouts  0.77 us
  transfers between devices with their start and end apart: 13, of which 9 were waited for; matrix products, arithmetic and copies ran while one was open for 3% of the time, Pallas kernels for 17%

profile of v7, /device:TPU:0, one launch (start us, length us, event | category | flops | bytes accessed | tf_op | source)
XLA Modules:
  0.0 38.0 jit_solution(10282179533281855093)
XLA Ops:
  0.6 3.0 %collective-permute-start = (bf16[3,4,4096]{2,1,0:T(4,128)(2,1)}, bf16[3,4,4096]{2,1,0:T(4,128)(2,1)S(1)}, u32[]{:S(2)}, u32[]{:S(2)}) collective-permute-start(bf16[3,4,4096]{2,1,0:T(4,128)(2,1)} %bitcast.8), channel_id=1, source_target_pairs={{2,0},{0,2},{3,1},{1,3},{6,4},{4,6},{7,5},{5,7},{10,8},{8,10},{11,... | collective-permute-start | bytes 294920 | tf_op jit(solution)/shard_map/ppermute | solution.py:30
  3.6 1.0 %fusion.refs_3_.refs_2_ = bf16[3,4,4224]{2,1,0:T(4,128)(2,1)S(1)} fusion(s32[4]{0:T(128)} %bitcast.12, s32[4]{0:T(128)} %param.15, bf16[3,4,4096]{2,1,0:T(4,128)(2,1)} %bitcast.11, pred[4224]{0:T(1024)(128)(4,1)S(1)} %get-tuple-element.37, pred[4224]{0:T(1024)(128)(4,1)S(1)} %get-tuple-element.38), kind=kLoop, calls=%fused_computation.1 | loop fusion | flops 152064 | bytes 208160 | tf_op jit(solution)/shard_map/jit(_where)/select_n | solution.py:402
  4.8 0.2 multiply_cosine_fusion
  5.1 0.7 %copy-done.1 = bf16[1,64,4096]{2,1,0:T(8,128)(2,1)S(1)} copy-done((bf16[1,64,4096]{2,1,0:T(8,128)(2,1)S(1)}, bf16[1,64,4096]{2,1,0:T(8,128)(2,1)}, u32[]{:S(2)}) %copy-start.1) | copy-done | bytes 524312
  5.9 0.3 shard_map.126
  6.1 1.0 %collective-permute-done.refs_0_ = bf16[3,4,4096]{2,1,0:T(4,128)(2,1)S(1)} collective-permute-done((bf16[3,4,4096]{2,1,0:T(4,128)(2,1)}, bf16[3,4,4096]{2,1,0:T(4,128)(2,1)S(1)}, u32[]{:S(2)}, u32[]{:S(2)}) %collective-permute-start) | collective-permute-done | bytes 98336 | tf_op jit(solution)/shard_map/ppermute | solution.py:30
  7.1 0.3 shard_map.127._.refs_0_
  7.4 2.0 %collective-permute-done.2.refs_3_ = bf16[3,4,4224]{2,1,0:T(4,128)(2,1)S(1)} collective-permute-done((bf16[3,4,4224]{2,1,0:T(4,128)(2,1)S(1)}, bf16[3,4,4224]{2,1,0:T(4,128)(2,1)S(1)}, u32[]{:S(2)}, u32[]{:S(2)}) %collective-permute-start.2) | collective-permute-done | bytes 101408 | tf_op jit(solution)/shard_map/ppermute | solution.py:30
  9.4 0.4 shard_map.129.refs_5_
  9.8 1.6 %collective-permute-start.3 = (bf16[3,4,4096]{2,1,0:T(4,128)(2,1)S(1)}, bf16[3,4,4096]{2,1,0:T(4,128)(2,1)S(1)}, u32[]{:S(2)}, u32[]{:S(2)}) collective-permute-start(bf16[3,4,4096]{2,1,0:T(4,128)(2,1)S(1)} %shard_map.129.refs_5_), channel_id=1, source_target_pairs={{0,2},{2,0},{1,3},{3,1},{4,6},{6,4},{5,7},{7,5},{8,10},{10,8},{9,1... | collective-permute-start | bytes 294920 | tf_op jit(solution)/shard_map/ppermute | solution.py:35
  11.4 0.4 shard_map.130.refs_0_
  11.8 0.6 %collective-permute-start.10 = (bf16[1,64,4096]{2,1,0:T(8,128)(2,1)S(1)}, bf16[1,64,4096]{2,1,0:T(8,128)(2,1)S(1)}, u32[]{:S(2)}, u32[]{:S(2)}) collective-permute-start(bf16[1,64,4096]{2,1,0:T(8,128)(2,1)S(1)} %copy-done.3), channel_id=1, source_target_pairs={{2,0},{0,2},{3,1},{1,3},{6,4},{4,6},{7,5},{5,7},{10,8},{8,10},{11,... | collective-permute-start | bytes 1572872 | tf_op jit(solution)/shard_map/ppermute | solution.py:30
  12.4 1.5 %collective-permute-start.12 = (bf16[1,64,4096]{2,1,0:T(8,128)(2,1)S(1)}, bf16[1,64,4096]{2,1,0:T(8,128)(2,1)S(1)}, u32[]{:S(2)}, u32[]{:S(2)}) collective-permute-start(bf16[1,64,4096]{2,1,0:T(8,128)(2,1)S(1)} %copy-done.4), channel_id=1, source_target_pairs={{2,0},{0,2},{3,1},{1,3},{6,4},{4,6},{7,5},{5,7},{10,8},{8,10},{11,... | collective-permute-start | bytes 1572872 | tf_op jit(solution)/shard_map/ppermute | solution.py:30
  13.9 0.8 %collective-permute-done.3.refs_1_ = bf16[3,4,4096]{2,1,0:T(4,128)(2,1)S(1)} collective-permute-done((bf16[3,4,4096]{2,1,0:T(4,128)(2,1)S(1)}, bf16[3,4,4096]{2,1,0:T(4,128)(2,1)S(1)}, u32[]{:S(2)}, u32[]{:S(2)}) %collective-permute-start.3) | collective-permute-done | bytes 98336 | tf_op jit(solution)/shard_map/ppermute | solution.py:35
  14.8 2.7 %collective-permute-start.4 = (bf16[3,4,4096]{2,1,0:T(4,128)(2,1)S(1)}, bf16[3,4,4096]{2,1,0:T(4,128)(2,1)S(1)}, u32[]{:S(2)}, u32[]{:S(2)}) collective-permute-start(bf16[3,4,4096]{2,1,0:T(4,128)(2,1)S(1)} %get-tuple-element.22.query_ref), channel_id=1, source_target_pairs={{8,0},{12,4},{0,8},{4,12},{9,1},{13,5},{1,9},{5,13},{10,2},{14,6},... | collective-permute-start | bytes 294920 | tf_op jit(solution)/shard_map/ppermute | solution.py:30
  17.5 1.6 %collective-permute-start.7 = (bf16[3,4,4096]{2,1,0:T(4,128)(2,1)S(1)}, bf16[3,4,4096]{2,1,0:T(4,128)(2,1)S(1)}, u32[]{:S(2)}, u32[]{:S(2)}) collective-permute-start(bf16[3,4,4096]{2,1,0:T(4,128)(2,1)S(1)} %get-tuple-element.22.query_ref), channel_id=1, source_target_pairs={{4,0},{0,4},{12,8},{8,12},{5,1},{1,5},{13,9},{9,13},{6,2},{2,6},{1... | collective-permute-start | bytes 294920 | tf_op jit(solution)/shard_map/ppermute | solution.py:30
  19.0 1.5 %collective-permute-done.4.query_ref = bf16[3,4,4096]{2,1,0:T(4,128)(2,1)S(1)} collective-permute-done((bf16[3,4,4096]{2,1,0:T(4,128)(2,1)S(1)}, bf16[3,4,4096]{2,1,0:T(4,128)(2,1)S(1)}, u32[]{:S(2)}, u32[]{:S(2)}) %collective-permute-start.4) | collective-permute-done | bytes 98336 | tf_op jit(solution)/shard_map/ppermute | solution.py:30
  20.5 1.7 %collective-permute-start.5 = (bf16[3,4,4096]{2,1,0:T(4,128)(2,1)S(1)}, bf16[3,4,4096]{2,1,0:T(4,128)(2,1)S(1)}, u32[]{:S(2)}, u32[]{:S(2)}) collective-permute-start(bf16[3,4,4096]{2,1,0:T(4,128)(2,1)S(1)} %collective-permute-done.4.query_ref), channel_id=1, source_target_pairs={{4,0},{0,4},{12,8},{8,12},{5,1},{1,5},{13,9},{9,13},{6,2},{2,6},{1... | collective-permute-start | bytes 294920 | tf_op jit(solution)/shard_map/ppermute | solution.py:30
  22.2 0.9 %collective-permute-done.7.query_ref = bf16[3,4,4096]{2,1,0:T(4,128)(2,1)S(1)} collective-permute-done((bf16[3,4,4096]{2,1,0:T(4,128)(2,1)S(1)}, bf16[3,4,4096]{2,1,0:T(4,128)(2,1)S(1)}, u32[]{:S(2)}, u32[]{:S(2)}) %collective-permute-start.7) | collective-permute-done | bytes 98336 | tf_op jit(solution)/shard_map/ppermute | solution.py:30
  23.1 1.0 %shard_map.133.refs_0_ = bf16[3,4,4224]{2,1,0:T(4,128)(2,1)S(1)} custom-call(bf16[3,4,4096]{2,1,0:T(4,128)(2,1)S(1)} %collective-permute-done.7.query_ref, bf16[2,1024,512]{2,1,0:T(8,128)(2,1)S(1)} %copy-done), custom_call_target="tpu_custom_call" | custom-call | flops 1048576 | bytes 1048576 | tf_op jit(solution)/shard_map/pallas_call | solution.py:43
  24.2 1.0 %shard_map.134 = bf16[3,4,4224]{2,1,0:T(4,128)(2,1)S(1)} custom-call(bf16[3,4,4096]{2,1,0:T(4,128)(2,1)S(1)} %collective-permute-done.4.query_ref, bf16[2,1024,512]{2,1,0:T(8,128)(2,1)S(1)} %copy-done, bf16[3,4,4224]{2,1,0:T(4,128)(2,1)S(1)} %shard_map.133.refs_0_), custom_call_target="tpu_custom_call" | custom-call | flops 1048576 | bytes 1048576 | tf_op jit(solution)/shard_map/pallas_call | solution.py:43
  25.2 2.5 %collective-permute-start.8 = (bf16[3,4,4224]{2,1,0:T(4,128)(2,1)S(1)}, bf16[3,4,4224]{2,1,0:T(4,128)(2,1)S(1)}, u32[]{:S(2)}, u32[]{:S(2)}) collective-permute-start(bf16[3,4,4224]{2,1,0:T(4,128)(2,1)S(1)} %shard_map.134), channel_id=1, source_target_pairs={{0,8},{4,12},{8,0},{12,4},{1,9},{5,13},{9,1},{13,5},{2,10},{6,14},... | collective-permute-start | bytes 304136 | tf_op jit(solution)/shard_map/ppermute | solution.py:35
  27.7 1.0 %shard_map.132 = bf16[3,4,4224]{2,1,0:T(4,128)(2,1)S(1)} custom-call(bf16[3,4,4096]{2,1,0:T(4,128)(2,1)S(1)} %collective-permute-done.5.query_ref, bf16[2,1024,512]{2,1,0:T(8,128)(2,1)S(1)} %copy-done), custom_call_target="tpu_custom_call" | custom-call | flops 1048576 | bytes 1048576 | tf_op jit(solution)/shard_map/pallas_call | solution.py:43
  28.7 3.9 %collective-permute-start.6 = (bf16[3,4,4224]{2,1,0:T(4,128)(2,1)S(1)}, bf16[3,4,4224]{2,1,0:T(4,128)(2,1)S(1)}, u32[]{:S(2)}, u32[]{:S(2)}) collective-permute-start(bf16[3,4,4224]{2,1,0:T(4,128)(2,1)S(1)} %shard_map.132), channel_id=1, source_target_pairs={{0,12},{4,8},{8,4},{12,0},{1,13},{5,9},{9,5},{13,1},{2,14},{6,10},... | collective-permute-start | bytes 304136 | tf_op jit(solution)/shard_map/ppermute | solution.py:35
  32.6 1.1 %shard_map.135 = (f32[3,4,4096]{2,1,0:T(4,128)S(1)}, f32[3,4,128]{2,1,0:T(4,128)S(1)}) custom-call(bf16[3,4,4096]{2,1,0:T(4,128)(2,1)S(1)} %get-tuple-element.22.query_ref, bf16[2,1024,512]{2,1,0:T(8,128)(2,1)S(1)} %copy-done, bf16[2,4,32,512]{3,2,1,0:T(8,128)(2,1)S(1)} %copy-done.5, bf16[2,3,4,512]{3,2,1,0:T(4,128)(2,1)S(1)} %bitcast.10, ...), custom_call_target="tpu_custom_call" | custom-call | flops 1048576 | bytes 1048576 | tf_op jit(solution)/shard_map/pallas_call | solution.py:43
  33.7 0.3 collective-permute-done.8.refs_0_
  34.0 0.5 %shard_map.136 = (f32[3,4,4096]{2,1,0:T(4,128)S(1)}, f32[3,4,128]{2,1,0:T(4,128)S(1)}) custom-call(bf16[3,4,4224]{2,1,0:T(4,128)(2,1)S(1)} %collective-permute-done.8.refs_0_, bf16[3,4,4224]{2,1,0:T(4,128)(2,1)S(1)} %collective-permute-done.9.refs_1_, f32[3,4,4096]{2,1,0:T(4,128)S(1)} %get-tuple-element.24.refs_2_, f32[3,4,128]{2,1,0:T(4,128)S(1)} %get-tuple-element.25.refs_3_), custom_call_target="tpu_custom_call" | custom-call | flops 1048576 | bytes 1048576 | tf_op jit(solution)/shard_map/pallas_call | solution.py:43
  34.5 0.8 %collective-permute-done.6.refs_0_ = bf16[3,4,4224]{2,1,0:T(4,128)(2,1)S(1)} collective-permute-done((bf16[3,4,4224]{2,1,0:T(4,128)(2,1)S(1)}, bf16[3,4,4224]{2,1,0:T(4,128)(2,1)S(1)}, u32[]{:S(2)}, u32[]{:S(2)}) %collective-permute-start.6) | collective-permute-done | bytes 101408 | tf_op jit(solution)/shard_map/ppermute | solution.py:35
  35.3 0.6 %shard_map.137 = (bf16[3,4,4096]{2,1,0:T(4,128)(2,1)S(1)}, f32[16,128]{1,0:T(8,128)S(1)}) custom-call(bf16[3,4,4224]{2,1,0:T(4,128)(2,1)S(1)} %collective-permute-done.6.refs_0_, f32[3,4,4096]{2,1,0:T(4,128)S(1)} %get-tuple-element.26.refs_1_, f32[3,4,128]{2,1,0:T(4,128)S(1)} %get-tuple-element.27.refs_2_, bf16[1,64,4096]{2,1,0:T(8,128)(2,1)S(1)} %copy-done.3, ...), custom_call_target="tpu_custom_call" | custom-call | flops 1048576 | bytes 1048576 | tf_op jit(solution)/shard_map/pallas_call | solution.py:43
  36.0 1.0 %collective-permute-done.12.refs_3_ = bf16[1,64,4096]{2,1,0:T(8,128)(2,1)S(1)} collective-permute-done((bf16[1,64,4096]{2,1,0:T(8,128)(2,1)S(1)}, bf16[1,64,4096]{2,1,0:T(8,128)(2,1)S(1)}, u32[]{:S(2)}, u32[]{:S(2)}) %collective-permute-start.12) | collective-permute-done | bytes 524320 | tf_op jit(solution)/shard_map/ppermute | solution.py:30
  37.0 0.2 collective-permute-done.11.refs_1_
  37.1 0.9 %shard_map.138 = (bf16[3,4,4096]{2,1,0:T(4,128)(2,1)}, bf16[3,4,4096]{2,1,0:T(4,128)(2,1)}) custom-call(f32[16,128]{1,0:T(8,128)S(1)} %get-tuple-element.29.refs_0_, f32[16,128]{1,0:T(8,128)S(1)} %collective-permute-done.11.refs_1_, bf16[1,64,4096]{2,1,0:T(8,128)(2,1)S(1)} %copy-done.4, bf16[1,64,4096]{2,1,0:T(8,128)(2,1)S(1)} %collective-permute-done.12.refs_3_, ...), custom_call_target="tpu_custom_call" | custom-call | flops 1048576 | bytes 1048576 | tf_op jit(solution)/shard_map/pallas_call | solution.py:43
  (31 shorter events, 0.4 us)
Async XLA Ops:
  0.6 6.5 %collective-permute-start = (bf16[3,4,4096]{2,1,0:T(4,128)(2,1)}, bf16[3,4,4096]{2,1,0:T(4,128)(2,1)S(1)}, u32[]{:S(2)}, u32[]{:S(2)}) collective-permute-start(bf16[3,4,4096]{2,1,0:T(4,128)(2,1)} %bitcast.8), channel_id=1, source_target_pairs={{2,0},{0,2},{3,1},{1,3},{6,4},{4,6},{7,5},{5,7},{10,8},{8,10},{11,... | collective-permute-start | bytes 294920 | tf_op jit(solution)/shard_map/ppermute | solution.py:30
  4.7 4.7 %collective-permute-start.2 = (bf16[3,4,4224]{2,1,0:T(4,128)(2,1)S(1)}, bf16[3,4,4224]{2,1,0:T(4,128)(2,1)S(1)}, u32[]{:S(2)}, u32[]{:S(2)}) collective-permute-start(bf16[3,4,4224]{2,1,0:T(4,128)(2,1)S(1)} %fusion.refs_3_.refs_2_), channel_id=1, source_target_pairs={{2,0},{0,2},{3,1},{1,3},{6,4},{4,6},{7,5},{5,7},{10,8},{8,10},{11,... | collective-permute-start | bytes 304136 | tf_op jit(solution)/shard_map/ppermute | solution.py:30
  4.8 1.0 %copy-start.1 = (bf16[1,64,4096]{2,1,0:T(8,128)(2,1)S(1)}, bf16[1,64,4096]{2,1,0:T(8,128)(2,1)}, u32[]{:S(2)}) copy-start(bf16[1,64,4096]{2,1,0:T(8,128)(2,1)} %down_ref.1) | copy-start | bytes 1572868
  4.8 1.0 %copy-start.6 = (bf16[4,3,4096]{2,0,1:T(4,128)(2,1)S(1)}, bf16[4,3,4096]{2,0,1:T(4,128)(2,1)}, u32[]{:S(2)}) copy-start(bf16[4,3,4096]{2,0,1:T(4,128)(2,1)} %param.11) | copy-start | bytes 294916
  4.8 2.5 %copy-start.2 = (bf16[1,64,4096]{2,1,0:T(8,128)(2,1)S(1)}, bf16[1,64,4096]{2,1,0:T(8,128)(2,1)}, u32[]{:S(2)}) copy-start(bf16[1,64,4096]{2,1,0:T(8,128)(2,1)} %in_ref.1) | copy-start | bytes 1572868
  5.8 5.9 %copy-start.3 = (bf16[1,64,4096]{2,1,0:T(8,128)(2,1)S(1)}, bf16[1,64,4096]{2,1,0:T(8,128)(2,1)}, u32[]{:S(2)}) copy-start(bf16[1,64,4096]{2,1,0:T(8,128)(2,1)} %refs_3_) | copy-start | bytes 1572868
  5.8 6.5 %copy-start.4 = (bf16[1,64,4096]{2,1,0:T(8,128)(2,1)S(1)}, bf16[1,64,4096]{2,1,0:T(8,128)(2,1)}, u32[]{:S(2)}) copy-start(bf16[1,64,4096]{2,1,0:T(8,128)(2,1)} %refs_2_) | copy-start | bytes 1572868
  7.3 2.1 %collective-permute-start.1 = (f32[32,64]{1,0:T(8,128)S(1)}, f32[32,64]{1,0:T(8,128)S(1)}, u32[]{:S(2)}, u32[]{:S(2)}) collective-permute-start(f32[32,64]{1,0:T(8,128)S(1)} %shard_map.127._.refs_0_), channel_id=1, source_target_pairs={{1,0},{0,1},{3,2},{2,3},{5,4},{4,5},{7,6},{6,7},{9,8},{8,9},{11,10... | collective-permute-start | bytes 24584 | tf_op jit(solution)/shard_map/ppermute | solution.py:30
  9.8 4.9 %collective-permute-start.3 = (bf16[3,4,4096]{2,1,0:T(4,128)(2,1)S(1)}, bf16[3,4,4096]{2,1,0:T(4,128)(2,1)S(1)}, u32[]{:S(2)}, u32[]{:S(2)}) collective-permute-start(bf16[3,4,4096]{2,1,0:T(4,128)(2,1)S(1)} %shard_map.129.refs_5_), channel_id=1, source_target_pairs={{0,2},{2,0},{1,3},{3,1},{4,6},{6,4},{5,7},{7,5},{8,10},{10,8},{9,1... | collective-permute-start | bytes 294920 | tf_op jit(solution)/shard_map/ppermute | solution.py:35
  11.8 11.3 %copy-start = (bf16[2,1024,512]{2,1,0:T(8,128)(2,1)S(1)}, bf16[2,1024,512]{2,1,0:T(8,128)(2,1)}, u32[]{:S(2)}) copy-start(bf16[2,1024,512]{2,1,0:T(8,128)(2,1)} %kv_ref.7) | copy-start | bytes 6291460
  11.8 23.5 %collective-permute-start.10 = (bf16[1,64,4096]{2,1,0:T(8,128)(2,1)S(1)}, bf16[1,64,4096]{2,1,0:T(8,128)(2,1)S(1)}, u32[]{:S(2)}, u32[]{:S(2)}) collective-permute-start(bf16[1,64,4096]{2,1,0:T(8,128)(2,1)S(1)} %copy-done.3), channel_id=1, source_target_pairs={{2,0},{0,2},{3,1},{1,3},{6,4},{4,6},{7,5},{5,7},{10,8},{8,10},{11,... | collective-permute-start | bytes 1572872 | tf_op jit(solution)/shard_map/ppermute | solution.py:30
  12.4 24.6 %collective-permute-start.12 = (bf16[1,64,4096]{2,1,0:T(8,128)(2,1)S(1)}, bf16[1,64,4096]{2,1,0:T(8,128)(2,1)S(1)}, u32[]{:S(2)}, u32[]{:S(2)}) collective-permute-start(bf16[1,64,4096]{2,1,0:T(8,128)(2,1)S(1)} %copy-done.4), channel_id=1, source_target_pairs={{2,0},{0,2},{3,1},{1,3},{6,4},{4,6},{7,5},{5,7},{10,8},{8,10},{11,... | collective-permute-start | bytes 1572872 | tf_op jit(solution)/shard_map/ppermute | solution.py:30
  14.8 5.7 %collective-permute-start.4 = (bf16[3,4,4096]{2,1,0:T(4,128)(2,1)S(1)}, bf16[3,4,4096]{2,1,0:T(4,128)(2,1)S(1)}, u32[]{:S(2)}, u32[]{:S(2)}) collective-permute-start(bf16[3,4,4096]{2,1,0:T(4,128)(2,1)S(1)} %get-tuple-element.22.query_ref), channel_id=1, source_target_pairs={{8,0},{12,4},{0,8},{4,12},{9,1},{13,5},{1,9},{5,13},{10,2},{14,6},... | collective-permute-start | bytes 294920 | tf_op jit(solution)/shard_map/ppermute | solution.py:30
  17.5 5.6 %collective-permute-start.7 = (bf16[3,4,4096]{2,1,0:T(4,128)(2,1)S(1)}, bf16[3,4,4096]{2,1,0:T(4,128)(2,1)S(1)}, u32[]{:S(2)}, u32[]{:S(2)}) collective-permute-start(bf16[3,4,4096]{2,1,0:T(4,128)(2,1)S(1)} %get-tuple-element.22.query_ref), channel_id=1, source_target_pairs={{4,0},{0,4},{12,8},{8,12},{5,1},{1,5},{13,9},{9,13},{6,2},{2,6},{1... | collective-permute-start | bytes 294920 | tf_op jit(solution)/shard_map/ppermute | solution.py:30
  20.5 7.1 %collective-permute-start.5 = (bf16[3,4,4096]{2,1,0:T(4,128)(2,1)S(1)}, bf16[3,4,4096]{2,1,0:T(4,128)(2,1)S(1)}, u32[]{:S(2)}, u32[]{:S(2)}) collective-permute-start(bf16[3,4,4096]{2,1,0:T(4,128)(2,1)S(1)} %collective-permute-done.4.query_ref), channel_id=1, source_target_pairs={{4,0},{0,4},{12,8},{8,12},{5,1},{1,5},{13,9},{9,13},{6,2},{2,6},{1... | collective-permute-start | bytes 294920 | tf_op jit(solution)/shard_map/ppermute | solution.py:30
  24.1 8.4 %copy-start.5 = (bf16[2,4,32,512]{3,2,1,0:T(8,128)(2,1)S(1)}, bf16[2,4,32,512]{3,2,1,0:T(8,128)(2,1)}, u32[]{:S(2)}) copy-start(bf16[2,4,32,512]{3,2,1,0:T(8,128)(2,1)} %suffix_ref.1) | copy-start | bytes 786436
  24.1 8.4 %copy-start.7 = (bf16[2,4,3,512]{3,1,2,0:T(4,128)(2,1)S(1)}, bf16[2,4,3,512]{3,1,2,0:T(4,128)(2,1)}, u32[]{:S(2)}) copy-start(bf16[2,4,3,512]{3,1,2,0:T(4,128)(2,1)} %param.13) | copy-start | bytes 73732
  25.2 8.8 %collective-permute-start.8 = (bf16[3,4,4224]{2,1,0:T(4,128)(2,1)S(1)}, bf16[3,4,4224]{2,1,0:T(4,128)(2,1)S(1)}, u32[]{:S(2)}, u32[]{:S(2)}) collective-permute-start(bf16[3,4,4224]{2,1,0:T(4,128)(2,1)S(1)} %shard_map.134), channel_id=1, source_target_pairs={{0,8},{4,12},{8,0},{12,4},{1,9},{5,13},{9,1},{13,5},{2,10},{6,14},... | collective-permute-start | bytes 304136 | tf_op jit(solution)/shard_map/ppermute | solution.py:35
  27.7 6.3 %collective-permute-start.9 = (bf16[3,4,4224]{2,1,0:T(4,128)(2,1)S(1)}, bf16[3,4,4224]{2,1,0:T(4,128)(2,1)S(1)}, u32[]{:S(2)}, u32[]{:S(2)}) collective-permute-start(bf16[3,4,4224]{2,1,0:T(4,128)(2,1)S(1)} %shard_map.133.refs_0_), channel_id=1, source_target_pairs={{0,4},{4,0},{8,12},{12,8},{1,5},{5,1},{9,13},{13,9},{2,6},{6,2},{1... | collective-permute-start | bytes 304136 | tf_op jit(solution)/shard_map/ppermute | solution.py:35
  28.7 6.6 %collective-permute-start.6 = (bf16[3,4,4224]{2,1,0:T(4,128)(2,1)S(1)}, bf16[3,4,4224]{2,1,0:T(4,128)(2,1)S(1)}, u32[]{:S(2)}, u32[]{:S(2)}) collective-permute-start(bf16[3,4,4224]{2,1,0:T(4,128)(2,1)S(1)} %shard_map.132), channel_id=1, source_target_pairs={{0,12},{4,8},{8,4},{12,0},{1,13},{5,9},{9,5},{13,1},{2,14},{6,10},... | collective-permute-start | bytes 304136 | tf_op jit(solution)/shard_map/ppermute | solution.py:35
  35.9 1.2 %collective-permute-start.11 = (f32[16,128]{1,0:T(8,128)S(1)}, f32[16,128]{1,0:T(8,128)S(1)}, u32[]{:S(2)}, u32[]{:S(2)}) collective-permute-start(f32[16,128]{1,0:T(8,128)S(1)} %get-tuple-element.29.refs_0_), channel_id=1, source_target_pairs={{1,0},{0,1},{3,2},{2,3},{5,4},{4,5},{7,6},{6,7},{9,8},{8,9},{11,10... | collective-permute-start | bytes 24584 | tf_op jit(solution)/shard_map/ppermute | solution.py:30

commit v8 on v6

--- a/solution.py
+++ b/solution.py
@@ -132,10 +132,10 @@
     owner = meta_ref[:, LANES // 2 : LANES // 2 + 1] // resident
     x = lax.axis_index("adapter")
     for t in range(out_ref.shape[0]):
-        picked = queries[0][t].astype(F32)
+        picked = queries[0][t]
         for j in range(1, adapters):
-            picked = jnp.where(owner == peer(x, j, adapters), queries[j][t].astype(F32), picked)
-        out_ref[t] = picked.astype(BF16)
+            picked = jnp.where(owner == peer(x, j, adapters), queries[j][t], picked)
+        out_ref[t] = picked
 
 
 def load_queries(query_ref, rows_ref):

time: 38.2 us -> 38.2 us (level)
  no operation moved by 1% of the time
where the time goes in v8:
time: 38.2 us; the launch traced here: 38 us
  starting transfers between devices  19 us (50%)
  waiting for transfers between devices  8.44 us (22%)
  Pallas kernels  7.68 us (20%)
  other arithmetic  1.31 us (3%)
  between operations  0.8 us (2%)
  local copies, waits for them, and re-layouts  0.78 us (2%)
    ppermute x9, starting transfers between devices, fetch(): lax.ppermute(value, axis, [(peer(i, offset, size), i) for i in range(size)])  11.1 us
    ppermute x4, starting transfers between devices, send(): lax.ppermute(value, axis, [(i, peer(i, offset, size)) for i in range(size)])  7.92 us
    pallas_call x14, Pallas kernels, call(): pl.pallas_call(kernel, out_shape=out_shape, in_specs=specs or [VMEM] * le...  7.68 us
    ppermute x9, waiting for transfers between devices, fetch(): lax.ppermute(value, axis, [(peer(i, offset, size), i) for i in range(size)])  5.64 us
    ppermute x4, waiting for transfers between devices, send(): lax.ppermute(value, axis, [(i, peer(i, offset, size)) for i in range(size)])  2.8 us
    select_n x1, other arithmetic, on_device(): base = jnp.where(lane < width, base, facts.astype(BF16))  1.04 us
    unnamed x16, local copies, waits for them, and re-layouts  0.77 us
  transfers between devices with their start and end apart: 13, of which 8 were waited for; matrix products, arithmetic and copies ran while one was open for 3% of the time, Pallas kernels for 17%

profile of v8, /device:TPU:0, one launch (start us, length us, event | category | flops | bytes accessed | tf_op | source)
XLA Modules:
  0.0 38.0 jit_solution(986968453519166784)
XLA Ops:
  0.6 3.0 %collective-permute-start = (bf16[3,4,4096]{2,1,0:T(4,128)(2,1)}, bf16[3,4,4096]{2,1,0:T(4,128)(2,1)S(1)}, u32[]{:S(2)}, u32[]{:S(2)}) collective-permute-start(bf16[3,4,4096]{2,1,0:T(4,128)(2,1)} %bitcast.8), channel_id=1, source_target_pairs={{2,0},{0,2},{3,1},{1,3},{6,4},{4,6},{7,5},{5,7},{10,8},{8,10},{11,... | collective-permute-start | bytes 294920 | tf_op jit(solution)/shard_map/ppermute | solution.py:30
  3.6 1.0 %fusion.refs_3_.refs_2_ = bf16[3,4,4224]{2,1,0:T(4,128)(2,1)S(1)} fusion(s32[4]{0:T(128)} %bitcast.12, s32[4]{0:T(128)} %param.15, bf16[3,4,4096]{2,1,0:T(4,128)(2,1)} %bitcast.11, pred[4224]{0:T(1024)(128)(4,1)S(1)} %get-tuple-element.37, pred[4224]{0:T(1024)(128)(4,1)S(1)} %get-tuple-element.38), kind=kLoop, calls=%fused_computation.1 | loop fusion | flops 152064 | bytes 208160 | tf_op jit(solution)/shard_map/jit(_where)/select_n | solution.py:401
  4.7 0.1 collective-permute-start.2
  4.8 0.2 multiply_cosine_fusion
  5.1 0.7 %copy-done.1 = bf16[1,64,4096]{2,1,0:T(8,128)(2,1)S(1)} copy-done((bf16[1,64,4096]{2,1,0:T(8,128)(2,1)S(1)}, bf16[1,64,4096]{2,1,0:T(8,128)(2,1)}, u32[]{:S(2)}) %copy-start.1) | copy-done | bytes 524312
  5.9 0.3 shard_map.126
  6.1 1.0 %collective-permute-done.refs_0_ = bf16[3,4,4096]{2,1,0:T(4,128)(2,1)S(1)} collective-permute-done((bf16[3,4,4096]{2,1,0:T(4,128)(2,1)}, bf16[3,4,4096]{2,1,0:T(4,128)(2,1)S(1)}, u32[]{:S(2)}, u32[]{:S(2)}) %collective-permute-start) | collective-permute-done | bytes 98336 | tf_op jit(solution)/shard_map/ppermute | solution.py:30
  7.1 0.3 shard_map.127._.refs_0_
  7.4 2.0 %collective-permute-done.2.refs_3_ = bf16[3,4,4224]{2,1,0:T(4,128)(2,1)S(1)} collective-permute-done((bf16[3,4,4224]{2,1,0:T(4,128)(2,1)S(1)}, bf16[3,4,4224]{2,1,0:T(4,128)(2,1)S(1)}, u32[]{:S(2)}, u32[]{:S(2)}) %collective-permute-start.2) | collective-permute-done | bytes 101408 | tf_op jit(solution)/shard_map/ppermute | solution.py:30
  9.4 0.4 shard_map.129.refs_5_
  9.8 1.6 %collective-permute-start.3 = (bf16[3,4,4096]{2,1,0:T(4,128)(2,1)S(1)}, bf16[3,4,4096]{2,1,0:T(4,128)(2,1)S(1)}, u32[]{:S(2)}, u32[]{:S(2)}) collective-permute-start(bf16[3,4,4096]{2,1,0:T(4,128)(2,1)S(1)} %shard_map.129.refs_5_), channel_id=1, source_target_pairs={{0,2},{2,0},{1,3},{3,1},{4,6},{6,4},{5,7},{7,5},{8,10},{10,8},{9,1... | collective-permute-start | bytes 294920 | tf_op jit(solution)/shard_map/ppermute | solution.py:35
  11.4 0.4 shard_map.130.refs_0_
  11.8 0.6 %collective-permute-start.10 = (bf16[1,64,4096]{2,1,0:T(8,128)(2,1)S(1)}, bf16[1,64,4096]{2,1,0:T(8,128)(2,1)S(1)}, u32[]{:S(2)}, u32[]{:S(2)}) collective-permute-start(bf16[1,64,4096]{2,1,0:T(8,128)(2,1)S(1)} %copy-done.3), channel_id=1, source_target_pairs={{2,0},{0,2},{3,1},{1,3},{6,4},{4,6},{7,5},{5,7},{10,8},{8,10},{11,... | collective-permute-start | bytes 1572872 | tf_op jit(solution)/shard_map/ppermute | solution.py:30
  12.4 1.5 %collective-permute-start.12 = (bf16[1,64,4096]{2,1,0:T(8,128)(2,1)S(1)}, bf16[1,64,4096]{2,1,0:T(8,128)(2,1)S(1)}, u32[]{:S(2)}, u32[]{:S(2)}) collective-permute-start(bf16[1,64,4096]{2,1,0:T(8,128)(2,1)S(1)} %copy-done.4), channel_id=1, source_target_pairs={{2,0},{0,2},{3,1},{1,3},{6,4},{4,6},{7,5},{5,7},{10,8},{8,10},{11,... | collective-permute-start | bytes 1572872 | tf_op jit(solution)/shard_map/ppermute | solution.py:30
  13.9 0.8 %collective-permute-done.3.refs_1_ = bf16[3,4,4096]{2,1,0:T(4,128)(2,1)S(1)} collective-permute-done((bf16[3,4,4096]{2,1,0:T(4,128)(2,1)S(1)}, bf16[3,4,4096]{2,1,0:T(4,128)(2,1)S(1)}, u32[]{:S(2)}, u32[]{:S(2)}) %collective-permute-start.3) | collective-permute-done | bytes 98336 | tf_op jit(solution)/shard_map/ppermute | solution.py:35
  14.7 0.1 shard_map.131
  14.8 2.7 %collective-permute-start.4 = (bf16[3,4,4096]{2,1,0:T(4,128)(2,1)S(1)}, bf16[3,4,4096]{2,1,0:T(4,128)(2,1)S(1)}, u32[]{:S(2)}, u32[]{:S(2)}) collective-permute-start(bf16[3,4,4096]{2,1,0:T(4,128)(2,1)S(1)} %get-tuple-element.22.query_ref), channel_id=1, source_target_pairs={{8,0},{12,4},{0,8},{4,12},{9,1},{13,5},{1,9},{5,13},{10,2},{14,6},... | collective-permute-start | bytes 294920 | tf_op jit(solution)/shard_map/ppermute | solution.py:30
  17.4 1.6 %collective-permute-start.8 = (bf16[3,4,4096]{2,1,0:T(4,128)(2,1)S(1)}, bf16[3,4,4096]{2,1,0:T(4,128)(2,1)S(1)}, u32[]{:S(2)}, u32[]{:S(2)}) collective-permute-start(bf16[3,4,4096]{2,1,0:T(4,128)(2,1)S(1)} %get-tuple-element.22.query_ref), channel_id=1, source_target_pairs={{4,0},{0,4},{12,8},{8,12},{5,1},{1,5},{13,9},{9,13},{6,2},{2,6},{1... | collective-permute-start | bytes 294920 | tf_op jit(solution)/shard_map/ppermute | solution.py:30
  19.0 1.5 %collective-permute-done.4.query_ref = bf16[3,4,4096]{2,1,0:T(4,128)(2,1)S(1)} collective-permute-done((bf16[3,4,4096]{2,1,0:T(4,128)(2,1)S(1)}, bf16[3,4,4096]{2,1,0:T(4,128)(2,1)S(1)}, u32[]{:S(2)}, u32[]{:S(2)}) %collective-permute-start.4) | collective-permute-done | bytes 98336 | tf_op jit(solution)/shard_map/ppermute | solution.py:30
  20.5 1.7 %collective-permute-start.5 = (bf16[3,4,4096]{2,1,0:T(4,128)(2,1)S(1)}, bf16[3,4,4096]{2,1,0:T(4,128)(2,1)S(1)}, u32[]{:S(2)}, u32[]{:S(2)}) collective-permute-start(bf16[3,4,4096]{2,1,0:T(4,128)(2,1)S(1)} %collective-permute-done.4.query_ref), channel_id=1, source_target_pairs={{4,0},{0,4},{12,8},{8,12},{5,1},{1,5},{13,9},{9,13},{6,2},{2,6},{1... | collective-permute-start | bytes 294920 | tf_op jit(solution)/shard_map/ppermute | solution.py:30
  22.2 1.0 %shard_map.133 = bf16[3,4,4224]{2,1,0:T(4,128)(2,1)S(1)} custom-call(bf16[3,4,4096]{2,1,0:T(4,128)(2,1)S(1)} %collective-permute-done.4.query_ref, bf16[2,1024,512]{2,1,0:T(8,128)(2,1)S(1)} %copy-done), custom_call_target="tpu_custom_call" | custom-call | flops 1048576 | bytes 1048576 | tf_op jit(solution)/shard_map/pallas_call | solution.py:43
  23.2 3.4 %collective-permute-start.7 = (bf16[3,4,4224]{2,1,0:T(4,128)(2,1)S(1)}, bf16[3,4,4224]{2,1,0:T(4,128)(2,1)S(1)}, u32[]{:S(2)}, u32[]{:S(2)}) collective-permute-start(bf16[3,4,4224]{2,1,0:T(4,128)(2,1)S(1)} %shard_map.133), channel_id=1, source_target_pairs={{0,8},{4,12},{8,0},{12,4},{1,9},{5,13},{9,1},{13,5},{2,10},{6,14},... | collective-permute-start | bytes 304136 | tf_op jit(solution)/shard_map/ppermute | solution.py:35
  26.6 1.0 %shard_map.134 = bf16[3,4,4224]{2,1,0:T(4,128)(2,1)S(1)} custom-call(bf16[3,4,4096]{2,1,0:T(4,128)(2,1)S(1)} %collective-permute-done.8.query_ref, bf16[2,1024,512]{2,1,0:T(8,128)(2,1)S(1)} %copy-done), custom_call_target="tpu_custom_call" | custom-call | flops 1048576 | bytes 1048576 | tf_op jit(solution)/shard_map/pallas_call | solution.py:43
  27.7 1.0 %shard_map.132 = bf16[3,4,4224]{2,1,0:T(4,128)(2,1)S(1)} custom-call(bf16[3,4,4096]{2,1,0:T(4,128)(2,1)S(1)} %collective-permute-done.5.query_ref, bf16[2,1024,512]{2,1,0:T(8,128)(2,1)S(1)} %copy-done), custom_call_target="tpu_custom_call" | custom-call | flops 1048576 | bytes 1048576 | tf_op jit(solution)/shard_map/pallas_call | solution.py:43
  28.7 2.9 %collective-permute-start.6 = (bf16[3,4,4224]{2,1,0:T(4,128)(2,1)S(1)}, bf16[3,4,4224]{2,1,0:T(4,128)(2,1)S(1)}, u32[]{:S(2)}, u32[]{:S(2)}) collective-permute-start(bf16[3,4,4224]{2,1,0:T(4,128)(2,1)S(1)} %shard_map.132), channel_id=1, source_target_pairs={{0,12},{4,8},{8,4},{12,0},{1,13},{5,9},{9,5},{13,1},{2,14},{6,10},... | collective-permute-start | bytes 304136 | tf_op jit(solution)/shard_map/ppermute | solution.py:35
  31.6 1.1 %shard_map.135 = (f32[3,4,4096]{2,1,0:T(4,128)S(1)}, f32[3,4,128]{2,1,0:T(4,128)S(1)}) custom-call(bf16[3,4,4096]{2,1,0:T(4,128)(2,1)S(1)} %get-tuple-element.22.query_ref, bf16[2,1024,512]{2,1,0:T(8,128)(2,1)S(1)} %copy-done, bf16[2,4,32,512]{3,2,1,0:T(8,128)(2,1)S(1)} %copy-done.5, bf16[2,3,4,512]{3,2,1,0:T(4,128)(2,1)S(1)} %bitcast.10, ...), custom_call_target="tpu_custom_call" | custom-call | flops 1048576 | bytes 1048576 | tf_op jit(solution)/shard_map/pallas_call | solution.py:43
  32.8 0.5 %shard_map.136 = (f32[3,4,4096]{2,1,0:T(4,128)S(1)}, f32[3,4,128]{2,1,0:T(4,128)S(1)}) custom-call(bf16[3,4,4224]{2,1,0:T(4,128)(2,1)S(1)} %collective-permute-done.7.refs_0_, bf16[3,4,4224]{2,1,0:T(4,128)(2,1)S(1)} %collective-permute-done.9.refs_1_, f32[3,4,4096]{2,1,0:T(4,128)S(1)} %get-tuple-element.24.refs_2_, f32[3,4,128]{2,1,0:T(4,128)S(1)} %get-tuple-element.25.refs_3_), custom_call_target="tpu_custom_call" | custom-call | flops 1048576 | bytes 1048576 | tf_op jit(solution)/shard_map/pallas_call | solution.py:43
  33.4 1.9 %collective-permute-done.6.refs_0_ = bf16[3,4,4224]{2,1,0:T(4,128)(2,1)S(1)} collective-permute-done((bf16[3,4,4224]{2,1,0:T(4,128)(2,1)S(1)}, bf16[3,4,4224]{2,1,0:T(4,128)(2,1)S(1)}, u32[]{:S(2)}, u32[]{:S(2)}) %collective-permute-start.6) | collective-permute-done | bytes 101408 | tf_op jit(solution)/shard_map/ppermute | solution.py:35
  35.3 0.6 %shard_map.137 = (bf16[3,4,4096]{2,1,0:T(4,128)(2,1)S(1)}, f32[16,128]{1,0:T(8,128)S(1)}) custom-call(bf16[3,4,4224]{2,1,0:T(4,128)(2,1)S(1)} %collective-permute-done.6.refs_0_, f32[3,4,4096]{2,1,0:T(4,128)S(1)} %get-tuple-element.26.refs_1_, f32[3,4,128]{2,1,0:T(4,128)S(1)} %get-tuple-element.27.refs_2_, bf16[1,64,4096]{2,1,0:T(8,128)(2,1)S(1)} %copy-done.3, ...), custom_call_target="tpu_custom_call" | custom-call | flops 1048576 | bytes 1048576 | tf_op jit(solution)/shard_map/pallas_call | solution.py:43
  35.9 1.0 %collective-permute-done.12.refs_3_ = bf16[1,64,4096]{2,1,0:T(8,128)(2,1)S(1)} collective-permute-done((bf16[1,64,4096]{2,1,0:T(8,128)(2,1)S(1)}, bf16[1,64,4096]{2,1,0:T(8,128)(2,1)S(1)}, u32[]{:S(2)}, u32[]{:S(2)}) %collective-permute-start.12) | collective-permute-done | bytes 524320 | tf_op jit(solution)/shard_map/ppermute | solution.py:30
  37.0 0.1 collective-permute-done.11.refs_1_
  37.1 0.9 %shard_map.138 = (bf16[3,4,4096]{2,1,0:T(4,128)(2,1)}, bf16[3,4,4096]{2,1,0:T(4,128)(2,1)}) custom-call(f32[16,128]{1,0:T(8,128)S(1)} %get-tuple-element.29.refs_0_, f32[16,128]{1,0:T(8,128)S(1)} %collective-permute-done.11.refs_1_, bf16[1,64,4096]{2,1,0:T(8,128)(2,1)S(1)} %copy-done.4, bf16[1,64,4096]{2,1,0:T(8,128)(2,1)S(1)} %collective-permute-done.12.refs_3_, ...), custom_call_target="tpu_custom_call" | custom-call | flops 1048576 | bytes 1048576 | tf_op jit(solution)/shard_map/pallas_call | solution.py:43
  (31 shorter events, 0.3 us)
Async XLA Ops:
  0.6 6.5 %collective-permute-start = (bf16[3,4,4096]{2,1,0:T(4,128)(2,1)}, bf16[3,4,4096]{2,1,0:T(4,128)(2,1)S(1)}, u32[]{:S(2)}, u32[]{:S(2)}) collective-permute-start(bf16[3,4,4096]{2,1,0:T(4,128)(2,1)} %bitcast.8), channel_id=1, source_target_pairs={{2,0},{0,2},{3,1},{1,3},{6,4},{4,6},{7,5},{5,7},{10,8},{8,10},{11,... | collective-permute-start | bytes 294920 | tf_op jit(solution)/shard_map/ppermute | solution.py:30
  4.7 4.7 %collective-permute-start.2 = (bf16[3,4,4224]{2,1,0:T(4,128)(2,1)S(1)}, bf16[3,4,4224]{2,1,0:T(4,128)(2,1)S(1)}, u32[]{:S(2)}, u32[]{:S(2)}) collective-permute-start(bf16[3,4,4224]{2,1,0:T(4,128)(2,1)S(1)} %fusion.refs_3_.refs_2_), channel_id=1, source_target_pairs={{2,0},{0,2},{3,1},{1,3},{6,4},{4,6},{7,5},{5,7},{10,8},{8,10},{11,... | collective-permute-start | bytes 304136 | tf_op jit(solution)/shard_map/ppermute | solution.py:30
  4.8 1.0 %copy-start.1 = (bf16[1,64,4096]{2,1,0:T(8,128)(2,1)S(1)}, bf16[1,64,4096]{2,1,0:T(8,128)(2,1)}, u32[]{:S(2)}) copy-start(bf16[1,64,4096]{2,1,0:T(8,128)(2,1)} %down_ref.1) | copy-start | bytes 1572868
  4.8 1.0 %copy-start.6 = (bf16[4,3,4096]{2,0,1:T(4,128)(2,1)S(1)}, bf16[4,3,4096]{2,0,1:T(4,128)(2,1)}, u32[]{:S(2)}) copy-start(bf16[4,3,4096]{2,0,1:T(4,128)(2,1)} %param.11) | copy-start | bytes 294916
  4.8 2.5 %copy-start.2 = (bf16[1,64,4096]{2,1,0:T(8,128)(2,1)S(1)}, bf16[1,64,4096]{2,1,0:T(8,128)(2,1)}, u32[]{:S(2)}) copy-start(bf16[1,64,4096]{2,1,0:T(8,128)(2,1)} %in_ref.1) | copy-start | bytes 1572868
  5.8 5.9 %copy-start.3 = (bf16[1,64,4096]{2,1,0:T(8,128)(2,1)S(1)}, bf16[1,64,4096]{2,1,0:T(8,128)(2,1)}, u32[]{:S(2)}) copy-start(bf16[1,64,4096]{2,1,0:T(8,128)(2,1)} %refs_3_) | copy-start | bytes 1572868
  5.8 6.5 %copy-start.4 = (bf16[1,64,4096]{2,1,0:T(8,128)(2,1)S(1)}, bf16[1,64,4096]{2,1,0:T(8,128)(2,1)}, u32[]{:S(2)}) copy-start(bf16[1,64,4096]{2,1,0:T(8,128)(2,1)} %refs_2_) | copy-start | bytes 1572868
  7.3 2.1 %collective-permute-start.1 = (f32[32,64]{1,0:T(8,128)S(1)}, f32[32,64]{1,0:T(8,128)S(1)}, u32[]{:S(2)}, u32[]{:S(2)}) collective-permute-start(f32[32,64]{1,0:T(8,128)S(1)} %shard_map.127._.refs_0_), channel_id=1, source_target_pairs={{1,0},{0,1},{3,2},{2,3},{5,4},{4,5},{7,6},{6,7},{9,8},{8,9},{11,10... | collective-permute-start | bytes 24584 | tf_op jit(solution)/shard_map/ppermute | solution.py:30
  9.8 4.9 %collective-permute-start.3 = (bf16[3,4,4096]{2,1,0:T(4,128)(2,1)S(1)}, bf16[3,4,4096]{2,1,0:T(4,128)(2,1)S(1)}, u32[]{:S(2)}, u32[]{:S(2)}) collective-permute-start(bf16[3,4,4096]{2,1,0:T(4,128)(2,1)S(1)} %shard_map.129.refs_5_), channel_id=1, source_target_pairs={{0,2},{2,0},{1,3},{3,1},{4,6},{6,4},{5,7},{7,5},{8,10},{10,8},{9,1... | collective-permute-start | bytes 294920 | tf_op jit(solution)/shard_map/ppermute | solution.py:35
  11.8 10.4 %copy-start = (bf16[2,1024,512]{2,1,0:T(8,128)(2,1)S(1)}, bf16[2,1024,512]{2,1,0:T(8,128)(2,1)}, u32[]{:S(2)}) copy-start(bf16[2,1024,512]{2,1,0:T(8,128)(2,1)} %kv_ref.7) | copy-start | bytes 6291460
  11.8 23.5 %collective-permute-start.10 = (bf16[1,64,4096]{2,1,0:T(8,128)(2,1)S(1)}, bf16[1,64,4096]{2,1,0:T(8,128)(2,1)S(1)}, u32[]{:S(2)}, u32[]{:S(2)}) collective-permute-start(bf16[1,64,4096]{2,1,0:T(8,128)(2,1)S(1)} %copy-done.3), channel_id=1, source_target_pairs={{2,0},{0,2},{3,1},{1,3},{6,4},{4,6},{7,5},{5,7},{10,8},{8,10},{11,... | collective-permute-start | bytes 1572872 | tf_op jit(solution)/shard_map/ppermute | solution.py:30
  12.4 24.6 %collective-permute-start.12 = (bf16[1,64,4096]{2,1,0:T(8,128)(2,1)S(1)}, bf16[1,64,4096]{2,1,0:T(8,128)(2,1)S(1)}, u32[]{:S(2)}, u32[]{:S(2)}) collective-permute-start(bf16[1,64,4096]{2,1,0:T(8,128)(2,1)S(1)} %copy-done.4), channel_id=1, source_target_pairs={{2,0},{0,2},{3,1},{1,3},{6,4},{4,6},{7,5},{5,7},{10,8},{8,10},{11,... | collective-permute-start | bytes 1572872 | tf_op jit(solution)/shard_map/ppermute | solution.py:30
  14.8 5.7 %collective-permute-start.4 = (bf16[3,4,4096]{2,1,0:T(4,128)(2,1)S(1)}, bf16[3,4,4096]{2,1,0:T(4,128)(2,1)S(1)}, u32[]{:S(2)}, u32[]{:S(2)}) collective-permute-start(bf16[3,4,4096]{2,1,0:T(4,128)(2,1)S(1)} %get-tuple-element.22.query_ref), channel_id=1, source_target_pairs={{8,0},{12,4},{0,8},{4,12},{9,1},{13,5},{1,9},{5,13},{10,2},{14,6},... | collective-permute-start | bytes 294920 | tf_op jit(solution)/shard_map/ppermute | solution.py:30
  17.4 9.2 %collective-permute-start.8 = (bf16[3,4,4096]{2,1,0:T(4,128)(2,1)S(1)}, bf16[3,4,4096]{2,1,0:T(4,128)(2,1)S(1)}, u32[]{:S(2)}, u32[]{:S(2)}) collective-permute-start(bf16[3,4,4096]{2,1,0:T(4,128)(2,1)S(1)} %get-tuple-element.22.query_ref), channel_id=1, source_target_pairs={{4,0},{0,4},{12,8},{8,12},{5,1},{1,5},{13,9},{9,13},{6,2},{2,6},{1... | collective-permute-start | bytes 294920 | tf_op jit(solution)/shard_map/ppermute | solution.py:30
  20.5 7.2 %collective-permute-start.5 = (bf16[3,4,4096]{2,1,0:T(4,128)(2,1)S(1)}, bf16[3,4,4096]{2,1,0:T(4,128)(2,1)S(1)}, u32[]{:S(2)}, u32[]{:S(2)}) collective-permute-start(bf16[3,4,4096]{2,1,0:T(4,128)(2,1)S(1)} %collective-permute-done.4.query_ref), channel_id=1, source_target_pairs={{4,0},{0,4},{12,8},{8,12},{5,1},{1,5},{13,9},{9,13},{6,2},{2,6},{1... | collective-permute-start | bytes 294920 | tf_op jit(solution)/shard_map/ppermute | solution.py:30
  23.2 8.4 %copy-start.5 = (bf16[2,4,32,512]{3,2,1,0:T(8,128)(2,1)S(1)}, bf16[2,4,32,512]{3,2,1,0:T(8,128)(2,1)}, u32[]{:S(2)}) copy-start(bf16[2,4,32,512]{3,2,1,0:T(8,128)(2,1)} %suffix_ref.1) | copy-start | bytes 786436
  23.2 8.4 %copy-start.7 = (bf16[2,4,3,512]{3,1,2,0:T(4,128)(2,1)S(1)}, bf16[2,4,3,512]{3,1,2,0:T(4,128)(2,1)}, u32[]{:S(2)}) copy-start(bf16[2,4,3,512]{3,1,2,0:T(4,128)(2,1)} %param.13) | copy-start | bytes 73732
  23.2 9.6 %collective-permute-start.7 = (bf16[3,4,4224]{2,1,0:T(4,128)(2,1)S(1)}, bf16[3,4,4224]{2,1,0:T(4,128)(2,1)S(1)}, u32[]{:S(2)}, u32[]{:S(2)}) collective-permute-start(bf16[3,4,4224]{2,1,0:T(4,128)(2,1)S(1)} %shard_map.133), channel_id=1, source_target_pairs={{0,8},{4,12},{8,0},{12,4},{1,9},{5,13},{9,1},{13,5},{2,10},{6,14},... | collective-permute-start | bytes 304136 | tf_op jit(solution)/shard_map/ppermute | solution.py:35
  27.7 5.2 %collective-permute-start.9 = (bf16[3,4,4224]{2,1,0:T(4,128)(2,1)S(1)}, bf16[3,4,4224]{2,1,0:T(4,128)(2,1)S(1)}, u32[]{:S(2)}, u32[]{:S(2)}) collective-permute-start(bf16[3,4,4224]{2,1,0:T(4,128)(2,1)S(1)} %shard_map.134), channel_id=1, source_target_pairs={{0,4},{4,0},{8,12},{12,8},{1,5},{5,1},{9,13},{13,9},{2,6},{6,2},{1... | collective-permute-start | bytes 304136 | tf_op jit(solution)/shard_map/ppermute | solution.py:35
  28.7 6.6 %collective-permute-start.6 = (bf16[3,4,4224]{2,1,0:T(4,128)(2,1)S(1)}, bf16[3,4,4224]{2,1,0:T(4,128)(2,1)S(1)}, u32[]{:S(2)}, u32[]{:S(2)}) collective-permute-start(bf16[3,4,4224]{2,1,0:T(4,128)(2,1)S(1)} %shard_map.132), channel_id=1, source_target_pairs={{0,12},{4,8},{8,4},{12,0},{1,13},{5,9},{9,5},{13,1},{2,14},{6,10},... | collective-permute-start | bytes 304136 | tf_op jit(solution)/shard_map/ppermute | solution.py:35
  35.9 1.2 %collective-permute-start.11 = (f32[16,128]{1,0:T(8,128)S(1)}, f32[16,128]{1,0:T(8,128)S(1)}, u32[]{:S(2)}, u32[]{:S(2)}) collective-permute-start(f32[16,128]{1,0:T(8,128)S(1)} %get-tuple-element.29.refs_0_), channel_id=1, source_target_pairs={{1,0},{0,1},{3,2},{2,3},{5,4},{4,5},{7,6},{6,7},{9,8},{8,9},{11,10... | collective-permute-start | bytes 24584 | tf_op jit(solution)/shard_map/ppermute | solution.py:30
